TPU v7x, 256 devices: a whole 4x4x8 slice. The times are simulated.
256 devices in a mesh: grp: 16 (over z, y_lo), head: 16 (over x, y_hi, core).
Axes of the slice: x: 4, y: 4 (y_hi: 2, y_lo: 2; y = y_hi * 2 + y_lo), z: 8, core: 2. Of those that a mesh axis runs over, the one named last changes fastest.
Arguments:
- queries: bfloat16 [16, 192, 24576], P('grp', 'head'), may hold values from -8 to 8
- span_latent: bfloat16 [16, 192, 512], P('grp', 'head'), may hold values from -6 to 6
- span_rope: bfloat16 [16, 192, 64], P('grp', 'head'), may hold values from -6 to 6
- pool_latent: bfloat16 [8192, 8, 512], P(('grp', 'head')), may hold values from -6 to 6
- pool_rope: bfloat16 [8192, 512], P(('grp', 'head')), may hold values from -8 to 8
- page_table: int32 [16, 256], replicated, may hold values from 0 to 8191, as said below
- cache_len: int32 [16], replicated, may hold values from 512 to 2048, as said below
- span_len: int32 [16], replicated, may hold values from 48 to 192, as said below
- kv_up: bfloat16 [512, 32768], P(None, 'head'), may hold values from -0.375 to 0.375
- out_weight: bfloat16 [16384, 7168], P('head', 'grp'), may hold values from -0.046875 to 0.046875
Outputs:
- layer_out: bfloat16 [16, 192, 7168], P('grp', 'head')
Inputs may be any that keep to these rules, and one draw needn't show every extreme that they name: `page_table`: entries are distinct pool slots; slot t lies on pool device t // 32, devices numbered along grp then head. No request has more than 2 pages on one pool device, and every request has exactly 2 on some device. `cache_len`: some request has exactly 2048. `span_len`: some request has exactly 192.
All inputs are finite; a program needn't handle non-finite values.
Results may differ from a plain program's by a relative error of at most 0.02.
Values may be sent and summed in bfloat16 or wider, within the bound.
No kernel may reach another device: no remote copies, remote signals or barrier semaphores. Data moves between devices by JAX's collectives and lax.ppermute only.
A program may use at most 128 MiB of HBM per device.

v0:
```python
import jax
import jax.numpy as jnp
from jax import lax
from jax.sharding import PartitionSpec as P

LATENT = 512
ROPE = 64
NOPE = 128
VDIM = 128
PAGE = 8
CAP = 2


def shards(
    queries,
    span_latent,
    span_rope,
    pool_latent,
    pool_rope,
    page_table,
    cache_len,
    span_len,
    kv_up,
    out_weight,
):
    groups = lax.axis_size("grp")
    head_count = lax.axis_size("head")
    group = lax.axis_index("grp")
    member = lax.axis_index("head")
    device = group * head_count + member
    slots = pool_latent.shape[0]
    pages = page_table.shape[1]
    score_scale = (NOPE + ROPE) ** (-0.5)
    exchanged = lax.all_to_all(queries, "head", split_axis=2, concat_axis=1, tiled=True)
    span_rows = exchanged.shape[1]
    local_heads = kv_up.shape[1] // (NOPE + VDIM)
    heads_view = exchanged[0].reshape(span_rows, local_heads, NOPE + ROPE)
    query_plain = heads_view[..., :NOPE]
    query_rope = heads_view[..., NOPE:]
    up_view = kv_up.reshape(LATENT, local_heads, NOPE + VDIM)
    key_up = up_view[..., :NOPE]
    value_up = up_view[..., NOPE:]
    absorbed = jnp.einsum(
        "rhn,chn->rhc", query_plain, key_up, preferred_element_type=jnp.float32
    ).astype(jnp.bfloat16)
    new_latent, new_rope = (
        lax.all_gather(span_latent, "head", axis=1, tiled=True),
        lax.all_gather(span_rope, "head", axis=1, tiled=True),
    )
    owners = page_table // slots
    slot_of = page_table % slots
    owned = (owners == device).astype(jnp.int32)
    ranking = jnp.cumsum(owned, axis=1) - 1
    chosen = (owned[:, None, :] == 1) & (
        ranking[:, None, :] == jnp.arange(CAP, dtype=jnp.int32)[None, :, None]
    )
    send_slot = jnp.sum(jnp.where(chosen, slot_of[:, None, :], 0), axis=2)
    filled = jnp.any(chosen, axis=2)
    send_latent = jnp.where(
        filled[:, :, None, None], pool_latent[send_slot], jnp.zeros((), jnp.bfloat16)
    )
    send_rope = jnp.where(filled[:, :, None], pool_rope[send_slot], jnp.zeros((), jnp.bfloat16))
    back_latent, back_rope = (
        lax.all_to_all(send_latent, "grp", split_axis=0, concat_axis=0, tiled=True),
        lax.all_to_all(send_rope, "grp", split_axis=0, concat_axis=0, tiled=True),
    )
    every_latent, every_rope = (
        lax.all_gather(back_latent[None], "head", axis=0, tiled=True),
        lax.all_gather(back_rope[None], "head", axis=0, tiled=True),
    )
    my_table = lax.dynamic_index_in_dim(page_table, group, 0, keepdims=False)
    source = my_table // slots
    order = jnp.arange(pages, dtype=jnp.int32)
    before = (source[None, :] == source[:, None]) & (order[None, :] < order[:, None])
    place = jnp.sum(before.astype(jnp.int32), axis=1)
    flat = (source % head_count * groups + source // head_count) * CAP + place
    cache_latent = every_latent.reshape(-1, PAGE, LATENT)[flat].reshape(pages * PAGE, LATENT)
    cache_rope = every_rope.reshape(-1, PAGE * ROPE)[flat].reshape(pages * PAGE, ROPE)
    key_latent = jnp.concatenate([cache_latent, new_latent[0]], 0)
    key_rope = jnp.concatenate([cache_rope, new_rope[0]], 0)
    cached = lax.dynamic_index_in_dim(cache_len, group, 0, keepdims=False)
    appended = lax.dynamic_index_in_dim(span_len, group, 0, keepdims=False)
    context = pages * PAGE
    rows = jnp.arange(span_rows, dtype=jnp.int32)
    places = jnp.arange(context + span_rows, dtype=jnp.int32)
    visible = jnp.where(
        places[None, :] < context,
        places[None, :] < cached,
        places[None, :] - context <= rows[:, None],
    )
    scores = jnp.einsum("rhc,kc->rhk", absorbed, key_latent, preferred_element_type=jnp.float32)
    scores = scores + jnp.einsum(
        "rhe,ke->rhk", query_rope, key_rope, preferred_element_type=jnp.float32
    )
    scores = jnp.where(visible[:, None, :], scores * score_scale, -jnp.inf)
    highest = jnp.max(scores, axis=-1, keepdims=True)
    expo = jnp.exp(scores - highest)
    weights = (expo / jnp.sum(expo, axis=-1, keepdims=True)).astype(jnp.bfloat16)
    mixed_latent = jnp.einsum(
        "rhk,kc->rhc", weights, key_latent, preferred_element_type=jnp.float32
    ).astype(jnp.bfloat16)
    head_out = jnp.einsum(
        "rhc,chv->rhv", mixed_latent, value_up, preferred_element_type=jnp.float32
    )
    head_out = jnp.where(rows[:, None, None] < appended, head_out, 0.0)
    attended = head_out.reshape(span_rows, local_heads * VDIM).astype(jnp.bfloat16)
    full_weight = lax.all_gather(out_weight, "grp", axis=1, tiled=True)
    summed = lax.psum_scatter(
        jnp.dot(attended, full_weight, preferred_element_type=jnp.float32).astype(jnp.bfloat16),
        "head",
        scatter_dimension=0,
        tiled=True,
    )
    return summed[None]


def solution(mesh):
    return jax.shard_map(
        shards,
        mesh=mesh,
        in_specs=(
            P("grp", "head", None),
            P("grp", "head", None),
            P("grp", "head", None),
            P(("grp", "head"), None, None),
            P(("grp", "head"), None),
            P(),
            P(),
            P(),
            P(None, "head"),
            P("head", "grp"),
        ),
        out_specs=P("grp", "head", None),
        check_vma=False,
    )
```

profile of v0, /device:TPU:29, one launch (start us, length us, event | category | flops | bytes accessed | tf_op | source)
XLA Modules:
  0.0 517.9 jit_solution(12358640922037591544)
XLA Ops:
  6.6 0.8 add_select_fusion
  7.4 0.7 convert_compare_fusion
  8.1 0.6 reduce-window.6
  8.7 0.2 slice_reduce_fusion
  8.9 0.1 copy_bitcast_fusion.1
  9.0 0.1 fusion.31
  9.2 0.1 select_reduce_fusion
  9.3 0.1 copy.73
  9.4 0.1 reshape.297
  9.5 0.1 copy.72
  9.6 0.6 gather_fusion
  10.2 0.1 broadcast_select_fusion
  10.3 18.6 %all_to_all.25 = bf16[16,2,8,512]{3,2,1,0:T(8,128)(2,1)} all-to-all(bf16[16,2,8,512]{3,2,1,0:T(8,128)(2,1)S(1)} %broadcast_select_fusion), channel_id=1, replica_groups=mesh['grp'=16,'head'=16] {'grp'}, dimensions={0} | all-to-all | bytes 524288 | tf_op jit(solution)/shard_map/all_to_all | solution.py:64
  28.9 0.0 all-gather.5.cloned.1.call-start
  28.9 0.7 all-gather.5.cloned.1.call-update
  29.6 0.6 gather_fusion.2
  30.3 0.7 broadcast_select_fusion.1
  31.0 4.5 all-to-all-start.2
  35.6 19.3 %copy.66 = bf16[1,12,24576]{1,0,2:T(2,128)(2,1)} copy(bf16[1,12,24576]{2,1,0:T(8,128)(2,1)S(1)} %copy-done.3) | data formatting | bytes 1179648 | tf_op args[0]
  54.8 0.5 broadcast.348
  55.4 134.9 %reduce.2 = bf16[24576,12]{1,0:T(8,128)(2,1)} reduce(bf16[24576,1,12]{2,1,0:T(2,128)(2,1)} %bitcast.80, bf16[]{:T(256)} %broadcast.348), dimensions={1}, to_apply=%bitcast.69.reduce_sub_computation | reduce | bytes 1179650
  190.3 14.3 %reshape.337 = bf16[16,2,9216]{2,1,0:T(2,128)(2,1)} reshape(bf16[24576,12]{1,0:T(8,128)(2,1)} %reduce.2) | data formatting | bytes 1179648
  204.6 23.5 %all_gather.18 = bf16[1,192,64]{2,0,1:T(2,128)(2,1)S(1)} all-gather(bf16[1,12,64]{2,0,1:T(2,128)(2,1)S(1)} %copy.77), channel_id=1, replica_groups=mesh['grp'=16,'head'=16] {'head'}, dimensions={1}, use_global_device_ids=true | all-gather | bytes 26112 | tf_op jit(solution)/shard_map/all_gather | solution.py:48
  228.1 0.1 copy.78
  228.2 2.9 copy.64
  231.1 34.2 %all_gather.16 = bf16[1,192,512]{2,0,1:T(2,128)(2,1)S(1)} all-gather(bf16[1,12,512]{2,0,1:T(2,128)(2,1)S(1)} %copy.74), channel_id=1, replica_groups=mesh['grp'=16,'head'=16] {'head'}, dimensions={1}, use_global_device_ids=true | all-gather | bytes 208896 | tf_op jit(solution)/shard_map/all_gather | solution.py:47
  265.3 0.7 copy.120
  266.0 0.6 dynamic_slice.12
  266.7 0.6 dynamic_slice.11
  267.3 0.7 and_select_fusion
  268.0 0.7 iota_compare_fusion.3
  268.7 0.2 convert_reduce_fusion
  268.9 1.1 fusion.5
  270.0 0.6 iota_compare_fusion.5
  270.7 12.2 %all-to-all-start = ((bf16[16,2,9216]{2,1,0:T(2,128)(2,1)}), bf16[16,2,9216]{2,1,0:T(2,128)(2,1)S(1)}, u32[]{:S(2)}, u32[]{:S(2)}) async-start(bf16[16,2,9216]{2,1,0:T(2,128)(2,1)} %reshape.337), calls=%async_computation | async-start | bytes 1179648 | tf_op jit(solution)/shard_map/all_to_all | solution.py:34
  282.9 42.2 %all-gather.1 = bf16[256,2,512]{2,1,0:T(2,128)(2,1)} all-gather(bf16[16,2,512]{2,1,0:T(2,128)(2,1)S(1)} %all-to-all-done.2), channel_id=3, replica_groups=mesh['grp'=16,'head'=16] {'head'}, dimensions={0}, use_global_device_ids=true | all-gather | bytes 557056 | tf_op jit(solution)/shard_map/all_gather | solution.py:69
  325.1 1.2 reshape.293
  326.4 1.2 gather_fusion.3
  327.5 0.3 reshape.294
  327.8 0.2 copy.79
  328.0 16.6 %reshape.338 = bf16[24576,1,12]{2,1,0:T(2,128)(2,1)} reshape(bf16[16,2,9216]{2,1,0:T(2,128)(2,1)S(1)} %all-to-all-done) | data formatting | bytes 1179648
  344.7 24.3 %copy.67 = bf16[1,12,24576]{2,1,0:T(8,128)(2,1)} copy(bf16[1,12,24576]{1,0,2:T(2,128)(2,1)} %bitcast.79) | data formatting | bytes 1179648 | tf_op jit(solution)/shard_map/all_to_all | solution.py:34
  368.9 1.4 copy.93
  370.3 1.2 copy.68
  371.6 2.5 reshape_squeeze.3
  374.0 1.1 slice.32
  375.1 1.7 fusion.10
  376.8 7.1 %fusion.24 = f32[2240,192,8]{0,1,2:T(8,128)} fusion(bf16[192,8,64]{2,1,0:T(8,128)(2,1)S(1)} %slice-done, bf16[192,64]{0,1:T(8,128)(2,1)S(1)} %bitcast.91, bf16[2048,64]{0,1:T(8,128)(2,1)S(1)} %copy.79), kind=kOutput, calls=%fused_computation.29 | convolution fusion | flops 440975360 | bytes 14245888 | tf_op jit(solution)/shard_map/rhe,ke->rhk/dot_general | solution.py:92
  383.9 4.3 gather_fusion.1
  388.2 26.3 %fusion.41 = (f32[192,8]{1,0:T(8,128)S(1)}, f32[192,8,2240]{2,1,0:T(8,128)}) fusion(f32[2240,192,8]{0,1,2:T(8,128)} %fusion.24, pred[192,2240]{1,0:T(8,128)(4,1)S(1)} %copy-done.4, bf16[192,8,512]{2,0,1:T(8,128)(2,1)} %fusion.10, bf16[192,512]{1,0:T(8,128)(2,1)S(1)} %bitcast.89, bf16[2048,512]{1,0:T(8,128)(2,1)} %bitcast.85), kind=kOutput, calls=%fused_computation.93 | convolution fusion | flops 3545008384 | bytes 31827968 | tf_op jit(solution)/shard_map/sub | solution.py:97
  414.5 9.6 %fusion.6 = bf16[192,8,512]{2,1,0:T(8,128)(2,1)S(1)} fusion(f32[192,8,2240]{2,1,0:T(8,128)} %get-tuple-element.10, f32[192,8]{1,0:T(8,128)S(1)} %get-tuple-element.9, bf16[192,512]{1,0:T(8,128)(2,1)S(1)} %bitcast.90, bf16[2048,512]{1,0:T(8,128)(2,1)} %bitcast.86), kind=kOutput, calls=%fused_computation.16 | convolution fusion | flops 3535470592 | bytes 17635328 | tf_op jit(solution)/shard_map/rhk,kc->rhc/dot_general | solution.py:99
  424.2 0.7 fusion.17
  424.9 0.0 all-gather.5.cloned.1.call-done
  424.9 10.1 %convolution_convert_fusion = bf16[192,7168]{1,0:T(8,128)(2,1)S(1)} fusion(bf16[1024,7168]{0,1:T(8,128)(2,1)} %all-gather.5.cloned.1.call-done, bf16[8,24,8,128]{3,2,1,0:T(8,128)(2,1)S(1)} %fusion.17), kind=kOutput, calls=%fused_computation.10 | convolution fusion | flops 2819948544 | bytes 17825792 | tf_op jit(solution)/shard_map/dot_general | solution.py:109
  435.1 48.1 %fusion = bf16[16,7168]{1,0:T(8,128)(2,1)S(1)} fusion(bf16[192,7168]{1,0:T(8,128)(2,1)S(1)} %convolution_convert_fusion), kind=kCustom, calls=%all-reduce-scatter | all-reduce-scatter fusion | flops 1835009 | bytes 2982912
  483.2 3.7 collective-permute-start
  486.9 7.2 %collective-permute-start.1 = (bf16[16,7168]{1,0:T(8,128)(2,1)S(1)}, bf16[16,7168]{1,0:T(8,128)(2,1)S(1)}, u32[]{:S(2)}, u32[]{:S(2)}) collective-permute-start(bf16[16,7168]{1,0:T(8,128)(2,1)S(1)} %fusion), channel_id=1, source_target_pairs={{0,2},{1,3},{2,4},{3,5},{4,6},{5,7},{6,8},{7,9},{8,10},{9,11},{10,... | collective-permute-start | bytes 688136
  494.1 1.9 collective-permute-start.2
  496.0 0.1 slice.37
  496.1 1.9 collective-permute-start.3
  498.1 0.6 dynamic-slice.4
  499.3 8.3 %collective-permute-done.3 = bf16[12,7168]{1,0:T(8,128)(2,1)S(1)} collective-permute-done((bf16[12,7168]{1,0:T(8,128)(2,1)S(1)}, bf16[12,7168]{1,0:T(8,128)(2,1)S(1)}, u32[]{:S(2)}, u32[]{:S(2)}) %collective-permute-start.3) | collective-permute-done | bytes 172064
  507.6 2.3 concatenate.8
  509.9 0.8 dynamic-slice_bitcast_fusion
  (45 shorter events, 0.3 us)
Async XLA Ops:
  6.5 3.0 copy-start
  6.5 23.1 %copy-start.2 = (bf16[32,512]{1,0:T(8,128)(2,1)S(1)}, bf16[32,512]{1,0:T(8,128)(2,1)}, u32[]{:S(2)}) copy-start(bf16[32,512]{1,0:T(8,128)(2,1)} %param.14) | copy-start | bytes 98308
  6.5 29.0 %copy-start.3 = (bf16[1,12,24576]{2,1,0:T(8,128)(2,1)S(1)}, bf16[1,12,24576]{2,1,0:T(8,128)(2,1)}, u32[]{:S(2)}) copy-start(bf16[1,12,24576]{2,1,0:T(8,128)(2,1)} %param.10) | copy-start | bytes 1769476
  6.5 377.3 %all-gather.7.cloned.1.call-start = ((), (), s32[]{:S(2)}) async-start(), calls=%async_computation.4 | async-start | bytes 4456448 | tf_op jit(solution)/shard_map/all_gather | solution.py:68
  28.9 396.0 %all-gather.5.cloned.1.call-start = ((), (), s32[]{:S(2)}) async-start(), calls=%async_computation.3 | async-start | bytes 15597568 | tf_op jit(solution)/shard_map/all_gather | solution.py:107
  31.0 239.6 %all-to-all-start.2 = ((bf16[16,2,512]{2,1,0:T(2,128)(2,1)}), bf16[16,2,512]{2,1,0:T(2,128)(2,1)S(1)}, u32[]{:S(2)}, u32[]{:S(2)}) async-start(bf16[16,2,512]{2,1,0:T(2,128)(2,1)} %broadcast_select_fusion.1), calls=%async_computation.2 | async-start | bytes 65536 | tf_op jit(solution)/shard_map/all_to_all | solution.py:65
  190.3 14.3 %copy-start.7 = (bf16[1,12,64]{2,1,0:T(8,128)(2,1)S(1)}, bf16[1,12,64]{2,1,0:T(8,128)(2,1)}, u32[]{:S(2)}) copy-start(bf16[1,12,64]{2,1,0:T(8,128)(2,1)} %param.12) | copy-start | bytes 4612
  204.6 26.5 %copy-start.6 = (bf16[1,12,512]{2,1,0:T(8,128)(2,1)S(1)}, bf16[1,12,512]{2,1,0:T(8,128)(2,1)}, u32[]{:S(2)}) copy-start(bf16[1,12,512]{2,1,0:T(8,128)(2,1)} %param.11) | copy-start | bytes 36868
  204.6 61.5 %copy-start.9 = (s32[16]{0:T(128)S(1)}, s32[16]{0:T(128)}, u32[]{:S(2)}) copy-start(s32[16]{0:T(128)} %param.16) | copy-start | bytes 196
  204.6 62.1 %copy-start.10 = (s32[16]{0:T(128)S(1)}, s32[16]{0:T(128)}, u32[]{:S(2)}) copy-start(s32[16]{0:T(128)} %param.17) | copy-start | bytes 196
  270.7 57.4 %all-to-all-start = ((bf16[16,2,9216]{2,1,0:T(2,128)(2,1)}), bf16[16,2,9216]{2,1,0:T(2,128)(2,1)S(1)}, u32[]{:S(2)}, u32[]{:S(2)}) async-start(bf16[16,2,9216]{2,1,0:T(2,128)(2,1)} %reshape.337), calls=%async_computation | async-start | bytes 1179648 | tf_op jit(solution)/shard_map/all_to_all | solution.py:34
  374.0 2.8 slice-start
  383.9 4.3 copy-start.4
  383.9 4.3 copy-start.5
  424.9 85.8 %copy-start.1 = (bf16[32,8,512]{2,1,0:T(8,128)(2,1)S(1)}, bf16[32,8,512]{2,1,0:T(8,128)(2,1)}, u32[]{:S(2)}) copy-start(bf16[32,8,512]{2,1,0:T(8,128)(2,1)} %param.13) | copy-start | bytes 786436
  435.1 63.0 %copy-start.8 = (u32[256]{0:T(256)S(1)}, u32[256]{0:T(256)}, u32[]{:S(2)}) copy-start(u32[256]{0:T(256)} %constant.113) | copy-start | bytes 3076
  483.2 24.4 %collective-permute-start = (bf16[16,7168]{1,0:T(8,128)(2,1)S(1)}, bf16[16,7168]{1,0:T(8,128)(2,1)S(1)}, u32[]{:S(2)}, u32[]{:S(2)}) collective-permute-start(bf16[16,7168]{1,0:T(8,128)(2,1)S(1)} %fusion), channel_id=1, source_target_pairs={{0,1},{1,2},{2,3},{3,4},{4,5},{5,6},{6,7},{7,8},{8,9},{9,10},{10,1... | collective-permute-start | bytes 688136
  486.9 20.7 %collective-permute-start.1 = (bf16[16,7168]{1,0:T(8,128)(2,1)S(1)}, bf16[16,7168]{1,0:T(8,128)(2,1)S(1)}, u32[]{:S(2)}, u32[]{:S(2)}) collective-permute-start(bf16[16,7168]{1,0:T(8,128)(2,1)S(1)} %fusion), channel_id=1, source_target_pairs={{0,2},{1,3},{2,4},{3,5},{4,6},{5,7},{6,8},{7,9},{8,10},{9,11},{10,... | collective-permute-start | bytes 688136
  494.1 13.5 %collective-permute-start.2 = (bf16[16,7168]{1,0:T(8,128)(2,1)S(1)}, bf16[16,7168]{1,0:T(8,128)(2,1)S(1)}, u32[]{:S(2)}, u32[]{:S(2)}) collective-permute-start(bf16[16,7168]{1,0:T(8,128)(2,1)S(1)} %fusion), channel_id=1, source_target_pairs={{0,3},{1,4},{2,5},{3,6},{4,7},{5,8},{6,9},{7,10},{8,11},{9,12},{10... | collective-permute-start | bytes 688136
  496.1 11.5 %collective-permute-start.3 = (bf16[12,7168]{1,0:T(8,128)(2,1)S(1)}, bf16[12,7168]{1,0:T(8,128)(2,1)S(1)}, u32[]{:S(2)}, u32[]{:S(2)}) collective-permute-start(bf16[12,7168]{1,0:T(8,128)(2,1)S(1)} %slice.37), channel_id=1, source_target_pairs={{0,4},{1,5},{2,6},{3,7},{4,8},{5,9},{6,10},{7,11},{8,12},{9,13},{1... | collective-permute-start | bytes 516104
Sparse Core Ops, SparseCore 0:
  29.0 57.7 all-gather.6
  88.6 325.6 all-gather.4
where the time goes:
time: 528 us; the launch traced here: 518 us
  blocking collectives  167 us (32%)
  other arithmetic  142 us (27%)
  local copies, waits for them, and re-layouts  98.7 us (19%)
  matrix products  55.5 us (11%)
  starting transfers between devices  31.6 us (6%)
  between operations  14.8 us (3%)
  waiting for transfers between devices  9.04 us (2%)
    unnamed x1, other arithmetic  135 us
    unnamed x34, local copies, waits for them, and re-layouts  58.6 us
    unnamed x1, blocking collectives  48.1 us
    all_gather x1, blocking collectives, shards(): lax.all_gather(back_rope[None], 'head', axis=0, tiled=True)  42.2 us
    all_gather x1, blocking collectives, shards(): lax.all_gather(span_latent, 'head', axis=1, tiled=True)  34.2 us
    sub x1, matrix products, shards(): expo = jnp.exp(scores - highest)  26.3 us
    all_to_all x3, local copies, waits for them, and re-layouts, shards(): lax.all_to_all(queries, 'head', split_axis=2, concat_axis=1, tiled=True)  25.5 us
    all_gather x1, blocking collectives, shards(): lax.all_gather(span_rope, 'head', axis=1, tiled=True)  23.5 us
  transfers between devices with their start and end apart: 8, of which 1 were waited for; matrix products, arithmetic and copies ran while one was open for 54% of the time, Pallas kernels for 0%

commit v1 on v0

v1 whole, which is shorter than its diff:
```python
import functools

import jax
import jax.numpy as jnp
import numpy as np
from jax import lax
from jax.experimental import pallas as pl
from jax.experimental.pallas import tpu as pltpu
from jax.sharding import Mesh
from jax.sharding import PartitionSpec as P

LATENT = 512
ROPE = 64
NOPE = 128
VDIM = 128
PAGE = 8
CAP = 2
WIDTH = LATENT + ROPE
QHEAD = NOPE + ROPE
HEADS_HERE = 8
SPAN = 192
OWN = 12
CTX = 2048
KEYS = CTX + SPAN
BF = jnp.bfloat16
F32 = jnp.float32
NEG = -1e30
LOG2E = 1.4426950408889634


def step(axis, count, by):
    def send(value):
        return lax.ppermute(value, axis, [(i, (i + by) % count) for i in range(count)])

    return send


def split_body(q_ref, o_ref):
    for part in range(4):
        o_ref[part] = q_ref[:, part * 1536 : (part + 1) * 1536]


def split_queries(q):
    return pl.pallas_call(
        split_body,
        grid=(4,),
        in_specs=[pl.BlockSpec((OWN, 4 * 1536), lambda i: (0, i))],
        out_specs=pl.BlockSpec((4, OWN, 1536), lambda i: (i, 0, 0)),
        out_shape=jax.ShapeDtypeStruct((16, OWN, 1536), BF),
        name="split_queries",
    )(q)


CHUNKS = [(0, 512), (512, 512), (1024, 512), (1536, 512), (2048, 192)]


def attend_body(lens_ref, q_ref, up_ref, key_ref, o_ref, qcat, scores):
    cached = lens_ref[0]
    appended = lens_ref[1]
    scale = LOG2E * (QHEAD**-0.5)
    for h in range(2):
        rows = slice(h * SPAN, (h + 1) * SPAN)
        plain = q_ref[:, h * QHEAD : h * QHEAD + NOPE]
        key_up = up_ref[:, h * 256 : h * 256 + NOPE]
        qcat[rows, :LATENT] = lax.dot_general(
            plain, key_up, (((1,), (1,)), ((), ())), preferred_element_type=F32
        ).astype(BF)
        qcat[rows, LATENT:] = q_ref[:, h * QHEAD + NOPE : (h + 1) * QHEAD]
    query = qcat[...]
    highest = jnp.full((2 * SPAN, 1), NEG, F32)
    for start, size in CHUNKS:
        s = lax.dot_general(
            query, key_ref[start : start + size, :], (((1,), (1,)), ((), ())), preferred_element_type=F32
        )
        if start < CTX:
            at = start + lax.broadcasted_iota(jnp.int32, (1, size), 1)
            s = jnp.where(at < cached, s, NEG)
        else:
            row = lax.broadcasted_iota(jnp.int32, (SPAN, SPAN), 0)
            col = lax.broadcasted_iota(jnp.int32, (SPAN, SPAN), 1)
            bias = jnp.where(col <= row, 0.0, NEG).astype(F32)
            s = s + jnp.concatenate([bias, bias], 0)
        scores[:, start : start + size] = s
        highest = jnp.maximum(highest, jnp.max(s, axis=1, keepdims=True))
    total = jnp.zeros((2 * SPAN, 1), F32)
    mixed = jnp.zeros((2 * SPAN, LATENT), F32)
    shift = highest * scale
    for start, size in CHUNKS:
        p = jnp.exp2(scores[:, start : start + size] * scale - shift)
        total = total + jnp.sum(p, axis=1, keepdims=True)
        mixed = mixed + jnp.dot(
            p.astype(BF), key_ref[start : start + size, :LATENT], preferred_element_type=F32
        )
    mixed = (mixed / total).astype(BF)
    live = lax.broadcasted_iota(jnp.int32, (SPAN, 1), 0) < appended
    for h in range(2):
        value_up = up_ref[:, h * 256 + NOPE : (h + 1) * 256]
        out = jnp.dot(mixed[h * SPAN : (h + 1) * SPAN], value_up, preferred_element_type=F32)
        o_ref[:, h * VDIM : (h + 1) * VDIM] = jnp.where(live, out, 0.0).astype(BF)


def attend(lens, q, up, keys):
    return pl.pallas_call(
        attend_body,
        grid_spec=pltpu.PrefetchScalarGridSpec(
            num_scalar_prefetch=1,
            grid=(4,),
            in_specs=[
                pl.BlockSpec((SPAN, 2 * QHEAD), lambda i, s: (0, i)),
                pl.BlockSpec((LATENT, 512), lambda i, s: (0, i)),
                pl.BlockSpec((KEYS, WIDTH), lambda i, s: (0, 0)),
            ],
            out_specs=pl.BlockSpec((SPAN, 256), lambda i, s: (0, i)),
            scratch_shapes=[
                pltpu.VMEM((2 * SPAN, WIDTH), BF),
                pltpu.VMEM((2 * SPAN, KEYS), F32),
            ],
        ),
        out_shape=jax.ShapeDtypeStruct((SPAN, HEADS_HERE * VDIM), BF),
        compiler_params=pltpu.CompilerParams(vmem_limit_bytes=40 * 1024 * 1024),
        cost_estimate=pl.CostEstimate(
            flops=8_000_000_000, bytes_accessed=6_000_000, transcendentals=3_500_000
        ),
        name="attend",
    )(lens, q, up, keys)


def project_body(own_ref, mate_ref, w_ref, o_ref):
    nt = (((1,), (1,)), ((), ()))
    for half in range(2):
        w_own = w_ref[:, :224, half * 512 : (half + 1) * 512].reshape(896, 512)
        w_mate = w_ref[:, 224:, half * 512 : (half + 1) * 512].reshape(896, 512)
        part = lax.dot_general(
            own_ref[:, half * 512 : (half + 1) * 512], w_own, nt, preferred_element_type=F32
        ) + lax.dot_general(
            mate_ref[:, half * 512 : (half + 1) * 512], w_mate, nt, preferred_element_type=F32
        )
        total = part if half == 0 else total + part
    for request in range(2):
        for place in range(8):
            at = request * SPAN + place * 24
            o_ref[place, request] = total[at : at + 24].astype(BF)


def project(own, mate, weight):
    return pl.pallas_call(
        project_body,
        grid=(2,),
        in_specs=[
            pl.BlockSpec((2 * SPAN, 1024), lambda i: (0, 0)),
            pl.BlockSpec((2 * SPAN, 1024), lambda i: (0, 0)),
            pl.BlockSpec((4, 448, 1024), lambda i: (i, 0, 0)),
        ],
        out_specs=pl.BlockSpec((8, 2, 24, 896), lambda i: (0, 0, 0, i)),
        out_shape=jax.ShapeDtypeStruct((8, 2, 24, 1792), BF),
        compiler_params=pltpu.CompilerParams(vmem_limit_bytes=40 * 1024 * 1024),
        name="project",
    )(own, mate, weight)


def shards(
    queries,
    span_latent,
    span_rope,
    pool_latent,
    pool_rope,
    page_table,
    cache_len,
    span_len,
    kv_up,
    out_weight,
):
    zi, yl, xi, yh, ci = (lax.axis_index(a) for a in ("z", "yl", "x", "yh", "c"))
    group = zi * 2 + yl
    member = (xi * 2 + yh) * 2 + ci
    device = group * 16 + member
    slots = pool_latent.shape[0]
    pages = page_table.shape[1]
    swap_c = step("c", 2, 1)
    swap_yl = step("yl", 2, 1)
    swap_yh = step("yh", 2, 1)

    turned = out_weight.T
    kept = lax.dynamic_slice_in_dim(turned, ci * 224, 224, 0)
    given = lax.dynamic_slice_in_dim(turned, (1 - ci) * 224, 224, 0)
    columns = jnp.concatenate([kept, swap_c(given)], 0)
    weight = lax.all_gather(columns, "z", axis=0, tiled=False)

    owners = page_table // slots
    slot_of = page_table % slots
    owned = (owners == device).astype(jnp.int32)
    ranking = jnp.cumsum(owned, axis=1) - 1
    chosen = (owned[:, None, :] == 1) & (
        ranking[:, None, :] == jnp.arange(CAP, dtype=jnp.int32)[None, :, None]
    )
    send_slot = jnp.sum(jnp.where(chosen, slot_of[:, None, :], 0), axis=2)
    filled = jnp.any(chosen, axis=2)
    pool = jnp.concatenate([pool_latent, pool_rope.reshape(slots, PAGE, ROPE)], 2)
    send = jnp.where(filled[:, :, None, None], pool[send_slot], jnp.zeros((), BF))
    send = send.reshape(16, 1, CAP * PAGE, WIDTH)
    send = jnp.broadcast_to(send, (16, 2, CAP * PAGE, WIDTH)).reshape(32, CAP * PAGE, WIDTH)
    back = lax.all_to_all(send, ("z", "yl", "yh"), split_axis=0, concat_axis=0, tiled=True)

    fresh = jnp.concatenate([span_latent[0], span_rope[0]], 1)
    fresh = jnp.pad(fresh, ((0, 4), (0, 0)))
    mine = jnp.concatenate([back.reshape(512, WIDTH), fresh, swap_yh(fresh)], 0)
    half = mine.shape[0] // 2
    left = step("x", 4, 1)(mine)
    right = step("x", 4, -1)(mine)
    far_a = step("x", 4, 1)(left[:half])
    far_b = step("x", 4, -1)(right[half:])

    sent = split_queries(queries[0])
    exchanged = lax.all_to_all(sent, ("x", "yh", "c"), split_axis=0, concat_axis=0, tiled=True)
    q = exchanged.reshape(SPAN, HEADS_HERE * QHEAD)

    column = jnp.concatenate([mine, left, right, far_a, far_b], 0)
    both = jnp.concatenate([column, swap_c(column)], 0).reshape(8, 68, PAGE, WIDTH)
    piece_of = jnp.array([0, 2, 3, 1], jnp.int32)
    my_table = lax.dynamic_index_in_dim(page_table, group, 0, keepdims=False)
    source = my_table // slots
    order = jnp.arange(pages, dtype=jnp.int32)
    before = (source[None, :] == source[:, None]) & (order[None, :] < order[:, None])
    place = jnp.sum(before.astype(jnp.int32), axis=1)
    from_group = source // 16
    from_member = source % 16
    from_x = from_member // 4
    from_yh = (from_member // 2) % 2
    from_c = from_member % 2
    block = jnp.where(from_c == ci, 0, 4) + piece_of[(from_x - xi) % 4]
    flat = block * 68 + (from_group * 2 + from_yh) * CAP + place
    cache = both.reshape(8 * 68, PAGE, WIDTH)[flat].reshape(CTX, WIDTH)
    heads16 = jnp.arange(16, dtype=jnp.int32)
    block16 = jnp.where(heads16 % 2 == ci, 0, 4) + piece_of[(heads16 // 4 - xi) % 4]
    which = jnp.where((heads16 // 2) % 2 == yh, 0, 1)
    news = both[:, 64:].reshape(16, 16, WIDTH)[block16 * 2 + which][:, :OWN].reshape(SPAN, WIDTH)
    keys = jnp.concatenate([cache, news], 0)

    lens = jnp.stack(
        [
            lax.dynamic_index_in_dim(cache_len, group, 0, keepdims=False),
            lax.dynamic_index_in_dim(span_len, group, 0, keepdims=False),
        ]
    )
    attended = attend(lens, q, kv_up, keys)
    own = jnp.concatenate([attended, swap_yl(attended)], 0)
    mate = swap_c(own)
    partial = project(own, mate, weight)
    shared = lax.all_to_all(partial, ("x", "yh"), split_axis=0, concat_axis=0, tiled=True)
    summed = jnp.sum(shared.astype(F32), axis=0).astype(BF)
    summed = summed.reshape(2, 2, OWN, 1792)
    own_rows = lax.dynamic_index_in_dim(summed, ci, 1, keepdims=False)
    mate_rows = lax.dynamic_index_in_dim(summed, 1 - ci, 1, keepdims=False)
    here = own_rows[0]
    from_c = swap_c(mate_rows[0])
    from_yl = swap_yl(own_rows[1])
    from_both = lax.ppermute(mate_rows[1], ("yl", "c"), [(i, 3 - i) for i in range(4)])
    same = jnp.stack([here, from_c])
    other = jnp.stack([from_yl, from_both])
    first = jnp.where(yl == 0, same, other)
    second = jnp.where(yl == 0, other, same)
    grid = jnp.stack([first, second])
    grid = jnp.where(ci == 0, grid, grid[:, ::-1])
    grid = grid.reshape(2, 2, OWN, 8, 224)
    out = jnp.transpose(grid, (2, 3, 0, 1, 4)).reshape(OWN, 7168)
    return out[None]


def solution(mesh):
    fine = Mesh(mesh.devices.reshape(8, 2, 4, 2, 2), ("z", "yl", "x", "yh", "c"))
    grp, head = ("z", "yl"), ("x", "yh", "c")
    return jax.shard_map(
        shards,
        mesh=fine,
        in_specs=(
            P(grp, head, None),
            P(grp, head, None),
            P(grp, head, None),
            P(grp + head, None, None),
            P(grp + head, None),
            P(),
            P(),
            P(),
            P(None, head),
            P(head, grp),
        ),
        out_specs=P(grp, head, None),
        check_vma=False,
    )
```

time: 528 us -> 211 us (0.40)
  the two profiles are of different devices: /device:TPU:29 before, /device:TPU:1 now
where the time goes in v1:
time: 211 us; the launch traced here: 210 us
  waiting for transfers between devices  63.6 us (30%)
  blocking collectives  35.8 us (17%)
  starting transfers between devices  32.6 us (15%)
  local copies, waits for them, and re-layouts  30.8 us (15%)
  Pallas kernels  27.5 us (13%)
  between operations  13.8 us (7%)
  other arithmetic  6.05 us (3%)
    all_to_all x1, blocking collectives, shards(): lax.all_to_all(send, ('z', 'yl', 'yh'), split_axis=0, concat_axis=0, tile...  35.8 us
    ppermute x11, waiting for transfers between devices, send(): lax.ppermute(value, axis, [(i, (i + by) % count) for i in range(count)])  30.8 us
    all_to_all x1, waiting for transfers between devices, shards(): lax.all_to_all(partial, ('x', 'yh'), split_axis=0, concat_axis=0, tiled=T...  20.8 us
    pallas_call x1, Pallas kernels, attend(): pl.pallas_call(attend_body, grid_spec=pltpu.PrefetchScalarGridSpec(num_sc...  19.7 us
    ppermute x11, starting transfers between devices, send(): lax.ppermute(value, axis, [(i, (i + by) % count) for i in range(count)])  18.5 us
    all_to_all x1, waiting for transfers between devices, shards(): lax.all_to_all(sent, ('x', 'yh', 'c'), split_axis=0, concat_axis=0, tiled...  10.5 us
    unnamed x29, local copies, waits for them, and re-layouts  8.96 us
    all_to_all x1, starting transfers between devices, shards(): lax.all_to_all(sent, ('x', 'yh', 'c'), split_axis=0, concat_axis=0, tiled...  7.71 us
  transfers between devices with their start and end apart: 15, of which 10 were waited for; matrix products, arithmetic and copies ran while one was open for 13% of the time, Pallas kernels for 11%

profile of v1, /device:TPU:1, one launch (start us, length us, event | category | flops | bytes accessed | tf_op | source)
XLA Modules:
  0.0 210.2 jit_solution(6242547727158780610)
XLA Ops:
  6.5 1.3 dynamic-slice_bitcast_fusion.1
  7.8 3.3 %collective-permute-start.8 = (bf16[224,1024]{1,0:T(8,128)(2,1)S(1)}, bf16[224,1024]{1,0:T(8,128)(2,1)S(1)}, u32[]{:S(2)}, u32[]{:S(2)}) collective-permute-start(bf16[224,1024]{1,0:T(8,128)(2,1)S(1)} %get-tuple-element.10), channel_id=1, source_target_pairs={{0,1},{1,0},{2,3},{3,2},{4,5},{5,4},{6,7},{7,6},{8,9},{9,8},{10,11... | collective-permute-start | bytes 1376264 | tf_op jit(solution)/shard_map/ppermute | solution.py:33
  11.1 1.4 collective-permute-done.8
  12.6 1.0 pad_maximum_fusion.1
  13.7 0.6 reduce-window.6
  14.3 0.2 slice_reduce_fusion
  14.6 0.1 select_reduce_fusion
  15.0 0.1 fusion.4
  15.3 0.6 gather_fusion
  15.9 0.1 bitcast_select_fusion
  16.1 35.8 %all_to_all.15 = bf16[32,16,576]{2,1,0:T(8,128)(2,1)S(1)} all-to-all(bf16[32,16,576]{2,1,0:T(8,128)(2,1)S(1)} %bitcast.77), channel_id=1, replica_groups=mesh['z'=8,'yl'=2,'x'=4,'yh'=2,'c'=2] {'z','yl','yh'}, dimensions={0} | all-to-all | bytes 1179648 | tf_op jit(solution)/shard_map/all_to_all | solution.py:202
  51.9 1.0 constant_dynamic-update-slice_fusion.6
  52.9 0.6 constant_dynamic-update-slice_fusion.5
  53.5 2.9 %collective-permute-start = (bf16[16,576]{1,0:T(8,128)(2,1)S(1)}, bf16[16,576]{1,0:T(8,128)(2,1)S(1)}, u32[]{:S(2)}, u32[]{:S(2)}) collective-permute-start(bf16[16,576]{1,0:T(8,128)(2,1)S(1)} %get-tuple-element.31), channel_id=1, source_target_pairs={{0,2},{2,0},{1,3},{3,1},{4,6},{6,4},{5,7},{7,5},{8,10},{10,8},{9,1... | collective-permute-start | bytes 55304 | tf_op jit(solution)/shard_map/ppermute | solution.py:33
  56.3 1.3 collective-permute-done
  57.7 1.3 collective-permute-start.1
  59.0 1.4 collective-permute-start.2
  60.4 13.2 %collective-permute-done.1 = bf16[544,576]{1,0:T(8,128)(2,1)S(1)} collective-permute-done((bf16[544,576]{1,0:T(8,128)(2,1)S(1)}, bf16[544,576]{1,0:T(8,128)(2,1)S(1)}, u32[]{:S(2)}, u32[]{:S(2)}) %collective-permute-start.1) | collective-permute-done | bytes 626720 | tf_op jit(solution)/shard_map/ppermute | solution.py:33
  73.8 0.6 constant_dynamic-update-slice_fusion.4
  74.4 2.7 %collective-permute-start.4 = (bf16[272,576]{1,0:T(8,128)(2,1)S(1)}, bf16[272,576]{1,0:T(8,128)(2,1)S(1)}, u32[]{:S(2)}, u32[]{:S(2)}) collective-permute-start(bf16[272,576]{1,0:T(8,128)(2,1)S(1)} %slice.59), channel_id=1, source_target_pairs={{0,12},{4,0},{8,4},{12,8},{1,13},{5,1},{9,5},{13,9},{2,14},{6,2},{... | collective-permute-start | bytes 940040 | tf_op jit(solution)/shard_map/ppermute | solution.py:33
  77.1 1.0 constant_dynamic-update-slice_fusion.3
  78.2 1.0 constant_dynamic-update-slice_fusion.2
  79.2 2.3 %collective-permute-done.3 = bf16[272,576]{1,0:T(8,128)(2,1)S(1)} collective-permute-done((bf16[272,576]{1,0:T(8,128)(2,1)S(1)}, bf16[272,576]{1,0:T(8,128)(2,1)S(1)}, u32[]{:S(2)}, u32[]{:S(2)}) %collective-permute-start.3) | collective-permute-done | bytes 313376 | tf_op jit(solution)/shard_map/ppermute | solution.py:33
  81.5 0.8 constant_dynamic-update-slice_fusion.1
  82.3 0.8 constant_dynamic-update-slice_fusion
  83.1 3.4 %copy.79 = bf16[2176,576]{0,1:T(8,128)(2,1)} copy(bf16[2176,576]{1,0:T(8,128)(2,1)S(1)} %get-tuple-element.17) | data formatting | bytes 5013504 | tf_op jit(solution)/shard_map/concatenate | solution.py:217
  86.5 4.1 %collective-permute-start.5 = (bf16[2176,576]{0,1:T(8,128)(2,1)}, bf16[2176,576]{0,1:T(8,128)(2,1)}, u32[]{:S(2)}, u32[]{:S(2)}) collective-permute-start(bf16[2176,576]{0,1:T(8,128)(2,1)} %copy.79), channel_id=1, source_target_pairs={{0,1},{1,0},{2,3},{3,2},{4,5},{5,4},{6,7},{7,6},{8,9},{9,8},{10,11... | collective-permute-start | bytes 7520264 | tf_op jit(solution)/shard_map/ppermute | solution.py:33
  90.6 3.3 %split_queries.1 = bf16[16,12,1536]{2,1,0:T(8,128)(2,1)} custom-call(bf16[12,24576]{1,0:T(8,128)(2,1)} %bitcast.82), custom_call_target="tpu_custom_call" | custom-call | tf_op jit(solution)/shard_map/split_queries/pallas_call | solution.py:44
  93.9 7.7 %all-to-all-start = ((bf16[16,12,1536]{2,1,0:T(8,128)(2,1)}), bf16[16,12,1536]{2,1,0:T(8,128)(2,1)S(1)}, u32[]{:S(2)}, u32[]{:S(2)}) async-start(bf16[16,12,1536]{2,1,0:T(8,128)(2,1)} %split_queries.1), calls=%async_computation | async-start | bytes 1572864 | tf_op jit(solution)/shard_map/all_to_all | solution.py:214
  101.6 0.7 dynamic_slice.24
  102.3 0.6 dynamic_slice.25
  102.9 0.7 gather_fusion.2
  103.6 1.4 pad_add_fusion.lens_ref
  105.0 0.2 convert_reduce_fusion
  105.3 10.5 %all-to-all-done = bf16[16,12,1536]{2,1,0:T(8,128)(2,1)S(1)} async-done(((bf16[16,12,1536]{2,1,0:T(8,128)(2,1)}), bf16[16,12,1536]{2,1,0:T(8,128)(2,1)S(1)}, u32[]{:S(2)}, u32[]{:S(2)}) %all-to-all-start) | async-done | bytes 589856 | tf_op jit(solution)/shard_map/all_to_all | solution.py:214
  115.8 0.1 reshape.753.q_ref
  115.9 3.9 %copy.80 = bf16[2176,576]{1,0:T(8,128)(2,1)S(1)} copy(bf16[2176,576]{0,1:T(8,128)(2,1)} %collective-permute-done.5) | data formatting | bytes 5013504 | tf_op jit(solution)/shard_map/ppermute | solution.py:33
  119.8 1.8 constant_dynamic-update-slice_fusion.7
  121.6 1.0 slice.60
  122.6 0.6 gather_fusion.3
  123.4 3.7 %gather_fusion.1 = bf16[256,8,576]{2,1,0:T(8,128)(2,1)S(1)} fusion(bf16[544,8,576]{2,1,0:T(8,128)(2,1)} %bitcast.8, s32[1024]{0:T(1024)S(1)} %get-tuple-element.33), kind=kCustom, calls=%fused_computation.1 | custom fusion | bytes 4719616 | tf_op jit(solution)/shard_map/gather | solution.py:232
  127.1 0.3 pad_maximum_fusion.key_ref
  127.3 1.3 copy-done.1
  128.6 19.7 %attend.1 = bf16[192,1024]{1,0:T(8,128)(2,1)S(1)} custom-call(s32[2]{0:T(128)S(1)} %pad_add_fusion.lens_ref, bf16[192,1536]{1,0:T(8,128)(2,1)S(1)} %reshape.753.q_ref, bf16[512,2048]{1,0:T(8,128)(2,1)S(1)} %copy-done.1, bf16[2240,576]{1,0:T(8,128)(2,1)S(1)} %pad_maximum_fusion.key_ref), custom_call_target="tpu_custom_call" | custom-call | flops 8000000000 | bytes 6000000 | tf_op jit(solution)/shard_map/attend/pallas_call | solution.py:103
  148.4 9.5 %collective-permute-done.6 = bf16[192,1024]{1,0:T(8,128)(2,1)S(1)} collective-permute-done((bf16[192,1024]{1,0:T(8,128)(2,1)S(1)}, bf16[192,1024]{1,0:T(8,128)(2,1)S(1)}, u32[]{:S(2)}, u32[]{:S(2)}) %collective-permute-start.6) | collective-permute-done | bytes 393248 | tf_op jit(solution)/shard_map/ppermute | solution.py:33
  158.0 2.1 %collective-permute-start.7 = (bf16[384,1024]{1,0:T(8,128)(2,1)S(1)}, bf16[384,1024]{1,0:T(8,128)(2,1)S(1)}, u32[]{:S(2)}, u32[]{:S(2)}) collective-permute-start(bf16[384,1024]{1,0:T(8,128)(2,1)S(1)} %pad_maximum_fusion.2.own_ref), channel_id=1, source_target_pairs={{0,1},{1,0},{2,3},{3,2},{4,5},{5,4},{6,7},{7,6},{8,9},{9,8},{10,11... | collective-permute-start | bytes 2359304 | tf_op jit(solution)/shard_map/ppermute | solution.py:33
  160.1 1.9 collective-permute-done.7.mate_ref
  162.0 3.1 %copy-done = bf16[3584,1024]{1,0:T(8,128)(2,1)S(1)} copy-done((bf16[3584,1024]{1,0:T(8,128)(2,1)S(1)}, bf16[3584,1024]{1,0:T(8,128)(2,1)}, u32[]{:S(2)}) %copy-start) | copy-done | bytes 7340056
  165.1 4.5 %project.1 = bf16[8,2,24,1792]{3,2,1,0:T(8,128)(2,1)} custom-call(bf16[384,1024]{1,0:T(8,128)(2,1)S(1)} %pad_maximum_fusion.2.own_ref, bf16[384,1024]{1,0:T(8,128)(2,1)S(1)} %collective-permute-done.7.mate_ref, bf16[8,448,1024]{2,1,0:T(8,128)(2,1)S(1)} %bitcast.73), custom_call_target="tpu_custom_call" | custom-call | tf_op jit(solution)/shard_map/project/pallas_call | solution.py:146
  169.6 3.6 %all-to-all-start.2 = ((bf16[8,2,24,1792]{3,2,1,0:T(8,128)(2,1)}), bf16[8,2,24,1792]{3,2,1,0:T(8,128)(2,1)S(1)}, u32[]{:S(2)}, u32[]{:S(2)}) async-start(bf16[8,2,24,1792]{3,2,1,0:T(8,128)(2,1)} %project.1), calls=%async_computation.2 | async-start | bytes 2752512 | tf_op jit(solution)/shard_map/all_to_all | solution.py:249
  173.2 20.8 %all-to-all-done.2 = bf16[8,2,24,1792]{3,2,1,0:T(8,128)(2,1)S(1)} async-done(((bf16[8,2,24,1792]{3,2,1,0:T(8,128)(2,1)}), bf16[8,2,24,1792]{3,2,1,0:T(8,128)(2,1)S(1)}, u32[]{:S(2)}, u32[]{:S(2)}) %all-to-all-start.2) | async-done | bytes 1376288 | tf_op jit(solution)/shard_map/all_to_all | solution.py:249
  194.0 0.2 reduce_sum.38
  194.2 0.1 copy.81
  194.4 0.3 constant_dynamic-slice_fusion.1
  194.7 0.3 collective-permute-start.10
  195.0 2.8 %collective-permute-start.11 = (bf16[12,1792]{1,0:T(8,128)(2,1)S(1)}, bf16[12,1792]{1,0:T(8,128)(2,1)S(1)}, u32[]{:S(2)}, u32[]{:S(2)}) collective-permute-start(bf16[12,1792]{1,0:T(8,128)(2,1)S(1)} %bitcast.84), channel_id=1, source_target_pairs={{0,17},{1,16},{16,1},{17,0},{2,19},{3,18},{18,3},{19,2},{4,21},{5,... | collective-permute-start | bytes 129032 | tf_op jit(solution)/shard_map/ppermute | solution.py:257
  198.0 1.1 collective-permute-done.9
  199.3 1.5 collective-permute-done.11
  200.8 0.5 broadcast_select_fusion.1
  201.3 0.4 pad_maximum_fusion.6
  201.7 0.1 broadcast_select_fusion.2
  201.9 0.3 reshape.827
  202.1 0.2 copy.86
  202.3 1.0 broadcast_in_dim_reshape.3
  (61 shorter events, 1.6 us)
Async XLA Ops:
  6.5 7.1 %copy-start.4 = (s32[16,256]{1,0:T(8,128)S(1)}, s32[16,256]{1,0:T(8,128)}, u32[]{:S(2)}) copy-start(s32[16,256]{1,0:T(8,128)} %param.16) | copy-start | bytes 49156
  6.5 8.3 %copy-start.5 = (bf16[32,512]{1,0:T(8,128)(2,1)S(1)}, bf16[32,512]{1,0:T(8,128)(2,1)}, u32[]{:S(2)}) copy-start(bf16[32,512]{1,0:T(8,128)(2,1)} %param.15) | copy-start | bytes 98308
  6.5 8.7 %copy-start.3 = (bf16[32,8,512]{2,1,0:T(8,128)(2,1)S(1)}, bf16[32,8,512]{2,1,0:T(8,128)(2,1)}, u32[]{:S(2)}) copy-start(bf16[32,8,512]{2,1,0:T(8,128)(2,1)} %param.14) | copy-start | bytes 786436
  6.5 155.5 %all-gather.3.cloned.1.call-start = ((), (), s32[]{:S(2)}) async-start(), calls=%async_computation.3 | async-start | bytes 8257536 | tf_op jit(solution)/shard_map/all_gather | solution.py:187
  7.8 4.8 %collective-permute-start.8 = (bf16[224,1024]{1,0:T(8,128)(2,1)S(1)}, bf16[224,1024]{1,0:T(8,128)(2,1)S(1)}, u32[]{:S(2)}, u32[]{:S(2)}) collective-permute-start(bf16[224,1024]{1,0:T(8,128)(2,1)S(1)} %get-tuple-element.10), channel_id=1, source_target_pairs={{0,1},{1,0},{2,3},{3,2},{4,5},{5,4},{6,7},{7,6},{8,9},{9,8},{10,11... | collective-permute-start | bytes 1376264 | tf_op jit(solution)/shard_map/ppermute | solution.py:33
  15.3 37.6 %copy-start.6 = (bf16[1,12,512]{2,1,0:T(8,128)(2,1)S(1)}, bf16[1,12,512]{2,1,0:T(8,128)(2,1)}, u32[]{:S(2)}) copy-start(bf16[1,12,512]{2,1,0:T(8,128)(2,1)} %param.12) | copy-start | bytes 36868
  15.3 37.6 %copy-start.7 = (bf16[1,12,64]{2,1,0:T(8,128)(2,1)S(1)}, bf16[1,12,64]{2,1,0:T(8,128)(2,1)}, u32[]{:S(2)}) copy-start(bf16[1,12,64]{2,1,0:T(8,128)(2,1)} %param.13) | copy-start | bytes 4612
  53.5 4.1 %collective-permute-start = (bf16[16,576]{1,0:T(8,128)(2,1)S(1)}, bf16[16,576]{1,0:T(8,128)(2,1)S(1)}, u32[]{:S(2)}, u32[]{:S(2)}) collective-permute-start(bf16[16,576]{1,0:T(8,128)(2,1)S(1)} %get-tuple-element.31), channel_id=1, source_target_pairs={{0,2},{2,0},{1,3},{3,1},{4,6},{6,4},{5,7},{7,5},{8,10},{10,8},{9,1... | collective-permute-start | bytes 55304 | tf_op jit(solution)/shard_map/ppermute | solution.py:33
  57.7 15.9 %collective-permute-start.1 = (bf16[544,576]{1,0:T(8,128)(2,1)S(1)}, bf16[544,576]{1,0:T(8,128)(2,1)S(1)}, u32[]{:S(2)}, u32[]{:S(2)}) collective-permute-start(bf16[544,576]{1,0:T(8,128)(2,1)S(1)} %pad_maximum_fusion.3), channel_id=1, source_target_pairs={{0,4},{4,8},{8,12},{12,0},{1,5},{5,9},{9,13},{13,1},{2,6},{6,10},{... | collective-permute-start | bytes 1880072 | tf_op jit(solution)/shard_map/ppermute | solution.py:33
  59.0 15.4 %collective-permute-start.2 = (bf16[544,576]{1,0:T(8,128)(2,1)S(1)}, bf16[544,576]{1,0:T(8,128)(2,1)S(1)}, u32[]{:S(2)}, u32[]{:S(2)}) collective-permute-start(bf16[544,576]{1,0:T(8,128)(2,1)S(1)} %pad_maximum_fusion.3), channel_id=1, source_target_pairs={{0,12},{4,0},{8,4},{12,8},{1,13},{5,1},{9,5},{13,9},{2,14},{6,2},{... | collective-permute-start | bytes 1880072 | tf_op jit(solution)/shard_map/ppermute | solution.py:33
  73.6 7.8 %collective-permute-start.3 = (bf16[272,576]{1,0:T(8,128)(2,1)S(1)}, bf16[272,576]{1,0:T(8,128)(2,1)S(1)}, u32[]{:S(2)}, u32[]{:S(2)}) collective-permute-start(bf16[272,576]{1,0:T(8,128)(2,1)S(1)} %slice.58), channel_id=1, source_target_pairs={{0,4},{4,8},{8,12},{12,0},{1,5},{5,9},{9,13},{13,1},{2,6},{6,10},{... | collective-permute-start | bytes 940040 | tf_op jit(solution)/shard_map/ppermute | solution.py:33
  74.4 7.9 %collective-permute-start.4 = (bf16[272,576]{1,0:T(8,128)(2,1)S(1)}, bf16[272,576]{1,0:T(8,128)(2,1)S(1)}, u32[]{:S(2)}, u32[]{:S(2)}) collective-permute-start(bf16[272,576]{1,0:T(8,128)(2,1)S(1)} %slice.59), channel_id=1, source_target_pairs={{0,12},{4,0},{8,4},{12,8},{1,13},{5,1},{9,5},{13,9},{2,14},{6,2},{... | collective-permute-start | bytes 940040 | tf_op jit(solution)/shard_map/ppermute | solution.py:33
  86.5 15.1 %copy-start.8 = (s32[16]{0:T(128)S(1)}, s32[16]{0:T(128)}, u32[]{:S(2)}) copy-start(s32[16]{0:T(128)} %param.17) | copy-start | bytes 196
  86.5 15.8 %copy-start.9 = (s32[16]{0:T(128)S(1)}, s32[16]{0:T(128)}, u32[]{:S(2)}) copy-start(s32[16]{0:T(128)} %param.18) | copy-start | bytes 196
  86.5 16.4 %copy-start.2 = (s32[4]{0:T(128)S(1)}, s32[4]{0:T(128)}, u32[]{:S(2)}) copy-start(s32[4]{0:T(128)} %constant.212.clone) | copy-start | bytes 52
  86.5 29.4 %collective-permute-start.5 = (bf16[2176,576]{0,1:T(8,128)(2,1)}, bf16[2176,576]{0,1:T(8,128)(2,1)}, u32[]{:S(2)}, u32[]{:S(2)}) collective-permute-start(bf16[2176,576]{0,1:T(8,128)(2,1)} %copy.79), channel_id=1, source_target_pairs={{0,1},{1,0},{2,3},{3,2},{4,5},{5,4},{6,7},{7,6},{8,9},{9,8},{10,11... | collective-permute-start | bytes 7520264 | tf_op jit(solution)/shard_map/ppermute | solution.py:33
  93.9 21.9 %all-to-all-start = ((bf16[16,12,1536]{2,1,0:T(8,128)(2,1)}), bf16[16,12,1536]{2,1,0:T(8,128)(2,1)S(1)}, u32[]{:S(2)}, u32[]{:S(2)}) async-start(bf16[16,12,1536]{2,1,0:T(8,128)(2,1)} %split_queries.1), calls=%async_computation | async-start | bytes 1572864 | tf_op jit(solution)/shard_map/all_to_all | solution.py:214
  127.1 1.6 copy-start.1
  148.3 9.6 %collective-permute-start.6 = (bf16[192,1024]{1,0:T(8,128)(2,1)S(1)}, bf16[192,1024]{1,0:T(8,128)(2,1)S(1)}, u32[]{:S(2)}, u32[]{:S(2)}) collective-permute-start(bf16[192,1024]{1,0:T(8,128)(2,1)S(1)} %attend.1), channel_id=1, source_target_pairs={{0,16},{16,0},{1,17},{17,1},{2,18},{18,2},{3,19},{19,3},{4,20},{20... | collective-permute-start | bytes 1179656 | tf_op jit(solution)/shard_map/ppermute | solution.py:33
  158.0 4.0 %collective-permute-start.7 = (bf16[384,1024]{1,0:T(8,128)(2,1)S(1)}, bf16[384,1024]{1,0:T(8,128)(2,1)S(1)}, u32[]{:S(2)}, u32[]{:S(2)}) collective-permute-start(bf16[384,1024]{1,0:T(8,128)(2,1)S(1)} %pad_maximum_fusion.2.own_ref), channel_id=1, source_target_pairs={{0,1},{1,0},{2,3},{3,2},{4,5},{5,4},{6,7},{7,6},{8,9},{9,8},{10,11... | collective-permute-start | bytes 2359304 | tf_op jit(solution)/shard_map/ppermute | solution.py:33
  162.0 3.1 %copy-start = (bf16[3584,1024]{1,0:T(8,128)(2,1)S(1)}, bf16[3584,1024]{1,0:T(8,128)(2,1)}, u32[]{:S(2)}) copy-start(bf16[3584,1024]{1,0:T(8,128)(2,1)} %all-gather.3.cloned.1.call-done) | copy-start | bytes 22020100
  169.6 24.4 %all-to-all-start.2 = ((bf16[8,2,24,1792]{3,2,1,0:T(8,128)(2,1)}), bf16[8,2,24,1792]{3,2,1,0:T(8,128)(2,1)S(1)}, u32[]{:S(2)}, u32[]{:S(2)}) async-start(bf16[8,2,24,1792]{3,2,1,0:T(8,128)(2,1)} %project.1), calls=%async_computation.2 | async-start | bytes 2752512 | tf_op jit(solution)/shard_map/all_to_all | solution.py:249
  194.7 3.3 %collective-permute-start.10 = (bf16[12,1792]{1,0:T(8,128)(2,1)S(1)}, bf16[12,1792]{1,0:T(8,128)(2,1)S(1)}, u32[]{:S(2)}, u32[]{:S(2)}) collective-permute-start(bf16[12,1792]{1,0:T(8,128)(2,1)S(1)} %bitcast.86), channel_id=1, source_target_pairs={{0,16},{16,0},{1,17},{17,1},{2,18},{18,2},{3,19},{19,3},{4,20},{20... | collective-permute-start | bytes 129032 | tf_op jit(solution)/shard_map/ppermute | solution.py:33
  195.0 5.7 %collective-permute-start.11 = (bf16[12,1792]{1,0:T(8,128)(2,1)S(1)}, bf16[12,1792]{1,0:T(8,128)(2,1)S(1)}, u32[]{:S(2)}, u32[]{:S(2)}) collective-permute-start(bf16[12,1792]{1,0:T(8,128)(2,1)S(1)} %bitcast.84), channel_id=1, source_target_pairs={{0,17},{1,16},{16,1},{17,0},{2,19},{3,18},{18,3},{19,2},{4,21},{5,... | collective-permute-start | bytes 129032 | tf_op jit(solution)/shard_map/ppermute | solution.py:257
  197.9 1.3 collective-permute-start.9
Sparse Core Ops, SparseCore 0:
  13.7 98.8 all-gather.2

commit v2 on v1

v2 whole, which is shorter than its diff:
```python
import jax
import jax.numpy as jnp
from jax import lax
from jax.experimental import pallas as pl
from jax.experimental.pallas import tpu as pltpu
from jax.sharding import Mesh
from jax.sharding import PartitionSpec as P

LATENT = 512
ROPE = 64
NOPE = 128
VDIM = 128
PAGE = 8
QHEAD = NOPE + ROPE
HEADS_HERE = 8
SPAN = 192
OWN = 12
CTX = 2048
BF = jnp.bfloat16
F32 = jnp.float32
NEG = -1e30
LOG2E = 1.4426950408889634


def step(axis, count, by):
    def send(value):
        return lax.ppermute(value, axis, [(i, (i + by) % count) for i in range(count)])

    return send


def split_body(q_ref, o_ref):
    for part in range(4):
        o_ref[part] = q_ref[:, part * 1536 : (part + 1) * 1536]


def split_queries(q):
    return pl.pallas_call(
        split_body,
        grid=(4,),
        in_specs=[pl.BlockSpec((OWN, 4 * 1536), lambda i: (0, i))],
        out_specs=pl.BlockSpec((4, OWN, 1536), lambda i: (i, 0, 0)),
        out_shape=jax.ShapeDtypeStruct((16, OWN, 1536), BF),
        name="split_queries",
    )(q)


PIECE = 34
CHUNKS = [(0, 512), (512, 512), (1024, 512), (1536, 512), (2048, 256)]
ALLKEYS = CTX + 256
KWIDTH = LATENT + 2 * ROPE


def tiles_of(page):
    return jnp.concatenate([page[:, j * 128 : (j + 1) * 128] for j in range(4)], 0)


def pack_body(slot_ref, pool_ref, rope_ref, span_ref, span_rope_ref, o_ref, f_ref):
    def one(dest, carry):
        first = slot_ref[2 * dest]
        second = slot_ref[2 * dest + 1]
        tiles = jnp.concatenate([tiles_of(pool_ref[first]), tiles_of(pool_ref[second])], 0)
        rope = jnp.concatenate([rope_ref[first], rope_ref[second]], 1)
        for copy in range(2):
            o_ref[2 * dest + copy, :64] = tiles
            o_ref[2 * dest + copy, 64:] = rope
        return carry

    lax.fori_loop(0, 16, one, 0)
    for k in range(2):
        f_ref[k, :64] = jnp.concatenate([tiles_of(span_ref[k, :8]), tiles_of(span_ref[k, 8:])], 0)
        f_ref[k, 64:] = jnp.concatenate([span_rope_ref[k, :8], span_rope_ref[k, 8:]], 1)


def pack(slots, pool, rope, span, span_rope):
    vmem = pl.BlockSpec(memory_space=pltpu.VMEM)
    return pl.pallas_call(
        pack_body,
        in_specs=[pl.BlockSpec(memory_space=pltpu.SMEM), vmem, vmem, vmem, vmem],
        out_specs=[vmem, vmem],
        out_shape=[
            jax.ShapeDtypeStruct((32, 72, 128), BF),
            jax.ShapeDtypeStruct((2, 72, 128), BF),
        ],
        name="pack",
    )(slots, pool, rope, span, span_rope)


PLACES = ((0, 34), (34, 34), (68, 34), (102, 17), (119, 17))


def attend_body(lens_ref, index_ref, q_ref, up_ref, *rest):
    pieces = rest[:10]
    o_ref, held, keys, qcat, scores, sems = rest[10:]
    cached = lens_ref[0]
    appended = lens_ref[1]
    scale = LOG2E * (QHEAD**-0.5)

    @pl.when(pl.program_id(0) == 0)
    def assemble():
        copies = []
        for n, piece in enumerate(pieces):
            start, size = PLACES[n % 5]
            start += 136 * (n // 5)
            copies.append(pltpu.make_async_copy(piece, held.at[start : start + size], sems.at[n]))
        for copy in copies:
            copy.start()
        for copy in copies:
            copy.wait()
        lane_half = lax.broadcasted_iota(jnp.int32, (8, 128), 1) // 64

        def pair(i, carry):
            lat, rope = [], []
            for k in range(2):
                at = index_ref[2 * i + k]
                block = at // 2
                place = at % 2
                lat.append(held[block, pl.ds(pl.multiple_of(place * 32, 32), 32), :])
                rope.append(jnp.where(lane_half == place, held[block, 64:72, :], jnp.zeros((), BF)))
            rows = pl.ds(pl.multiple_of(i * 16, 16), 16)
            for j in range(4):
                keys[rows, j * 128 : (j + 1) * 128] = jnp.concatenate(
                    [lat[0][8 * j : 8 * j + 8], lat[1][8 * j : 8 * j + 8]], 0
                )
            keys[rows, LATENT:] = jnp.concatenate(rope, 0)
            return carry

        lax.fori_loop(0, ALLKEYS // 16, pair, 0, unroll=2)

    for h in range(2):
        rows = slice(h * SPAN, (h + 1) * SPAN)
        plain = q_ref[:, h * QHEAD : h * QHEAD + NOPE]
        key_up = up_ref[:, h * 256 : h * 256 + NOPE]
        qcat[rows, :LATENT] = lax.dot_general(
            plain, key_up, (((1,), (1,)), ((), ())), preferred_element_type=F32
        ).astype(BF)
        rope = q_ref[:, h * QHEAD + NOPE : (h + 1) * QHEAD]
        qcat[rows, LATENT:] = jnp.concatenate([rope, rope], 1)
    query = qcat[...]
    highest = jnp.full((2 * SPAN, 1), NEG, F32)
    for start, size in CHUNKS:
        s = lax.dot_general(
            query, keys[start : start + size, :], (((1,), (1,)), ((), ())), preferred_element_type=F32
        )
        if start < CTX:
            at = start + lax.broadcasted_iota(jnp.int32, (1, size), 1)
            s = jnp.where(at < cached, s, NEG)
        else:
            row = lax.broadcasted_iota(jnp.int32, (SPAN, 256), 0)
            col = lax.broadcasted_iota(jnp.int32, (SPAN, 256), 1)
            token = col % 16
            seen = (token < OWN) & (col // 16 * OWN + token <= row)
            bias = jnp.where(seen, 0.0, NEG).astype(F32)
            s = s + jnp.concatenate([bias, bias], 0)
        scores[:, start : start + size] = s
        highest = jnp.maximum(highest, jnp.max(s, axis=1, keepdims=True))
    total = jnp.zeros((2 * SPAN, 1), F32)
    mixed = jnp.zeros((2 * SPAN, LATENT), F32)
    shift = highest * scale
    for start, size in CHUNKS:
        p = jnp.exp2(scores[:, start : start + size] * scale - shift)
        total = total + jnp.sum(p, axis=1, keepdims=True)
        mixed = mixed + jnp.dot(
            p.astype(BF), keys[start : start + size, :LATENT], preferred_element_type=F32
        )
    mixed = (mixed / total).astype(BF)
    live = lax.broadcasted_iota(jnp.int32, (SPAN, 1), 0) < appended
    for h in range(2):
        value_up = up_ref[:, h * 256 + NOPE : (h + 1) * 256]
        out = jnp.dot(mixed[h * SPAN : (h + 1) * SPAN], value_up, preferred_element_type=F32)
        o_ref[:, h * VDIM : (h + 1) * VDIM] = jnp.where(live, out, 0.0).astype(BF)


def attend(lens, index, q, up, pieces):
    return pl.pallas_call(
        attend_body,
        grid_spec=pltpu.PrefetchScalarGridSpec(
            num_scalar_prefetch=2,
            grid=(4,),
            in_specs=[
                pl.BlockSpec((SPAN, 2 * QHEAD), lambda i, *s: (0, i)),
                pl.BlockSpec((LATENT, 512), lambda i, *s: (0, i)),
            ]
            + [pl.BlockSpec(memory_space=pl.ANY)] * 10,
            out_specs=pl.BlockSpec((SPAN, 256), lambda i, *s: (0, i)),
            scratch_shapes=[
                pltpu.VMEM((8 * PIECE, 72, 128), BF),
                pltpu.VMEM((ALLKEYS, KWIDTH), BF),
                pltpu.VMEM((2 * SPAN, KWIDTH), BF),
                pltpu.VMEM((2 * SPAN, ALLKEYS), F32),
                pltpu.SemaphoreType.DMA((10,)),
            ],
        ),
        out_shape=jax.ShapeDtypeStruct((SPAN, HEADS_HERE * VDIM), BF),
        compiler_params=pltpu.CompilerParams(vmem_limit_bytes=40 * 1024 * 1024),
        cost_estimate=pl.CostEstimate(
            flops=8_000_000_000, bytes_accessed=6_000_000, transcendentals=3_500_000
        ),
        name="attend",
    )(lens, index, q, up, *pieces)


def project_body(own_ref, own_y_ref, mate_ref, mate_y_ref, w_ref, o_ref):
    nt = (((1,), (1,)), ((), ()))
    for request, (own, mate) in enumerate(((own_ref, mate_ref), (own_y_ref, mate_y_ref))):
        total = lax.dot_general(
            own[...], w_ref[:, :224].reshape(896, 1024), nt, preferred_element_type=F32
        ) + lax.dot_general(
            mate[...], w_ref[:, 224:].reshape(896, 1024), nt, preferred_element_type=F32
        )
        for place in range(8):
            o_ref[place, request] = total[place * 24 : (place + 1) * 24].astype(BF)


def project(own, own_y, mate, mate_y, weight):
    return pl.pallas_call(
        project_body,
        grid=(2,),
        in_specs=[pl.BlockSpec((SPAN, 1024), lambda i: (0, 0))] * 4
        + [pl.BlockSpec((4, 448, 1024), lambda i: (i, 0, 0))],
        out_specs=pl.BlockSpec((8, 2, 24, 896), lambda i: (0, 0, 0, i)),
        out_shape=jax.ShapeDtypeStruct((8, 2, 24, 1792), BF),
        compiler_params=pltpu.CompilerParams(vmem_limit_bytes=40 * 1024 * 1024),
        name="project",
    )(own, own_y, mate, mate_y, weight)


def total_body(where_ref, x_ref, *outs):
    core = where_ref[1]
    for request in range(2):
        value = jnp.sum(x_ref[:, request].astype(F32), axis=0)
        low, high = value[:OWN], value[OWN:]
        outs[2 * request][...] = jnp.where(core == 0, low, high).astype(BF)
        outs[2 * request + 1][...] = jnp.where(core == 0, high, low).astype(BF)


def total_parts(where, shared):
    vmem = pl.BlockSpec(memory_space=pltpu.VMEM)
    return pl.pallas_call(
        total_body,
        in_specs=[pl.BlockSpec(memory_space=pltpu.SMEM), vmem],
        out_specs=[vmem] * 4,
        out_shape=[jax.ShapeDtypeStruct((OWN, 1792), BF)] * 4,
        name="total_parts",
    )(where, shared)


def arrange_body(where_ref, here_ref, c_ref, y_ref, both_ref, o_ref):
    yl, core = where_ref[0], where_ref[1]
    here, mate, near, far = (r[...].astype(F32) for r in (here_ref, c_ref, y_ref, both_ref))
    same = (jnp.where(core == 0, here, mate), jnp.where(core == 0, mate, here))
    other = (jnp.where(core == 0, near, far), jnp.where(core == 0, far, near))
    parts = [jnp.where(yl == 0, same[k], other[k]) for k in range(2)]
    parts += [jnp.where(yl == 0, other[k], same[k]) for k in range(2)]
    for z in range(8):
        o_ref[:, z * 896 : (z + 1) * 896] = jnp.concatenate(
            [p[:, z * 224 : (z + 1) * 224] for p in parts], 1
        ).astype(BF)


def arrange(where, here, mate, near, far):
    vmem = pl.BlockSpec(memory_space=pltpu.VMEM)
    return pl.pallas_call(
        arrange_body,
        in_specs=[pl.BlockSpec(memory_space=pltpu.SMEM)] + [vmem] * 4,
        out_specs=vmem,
        out_shape=jax.ShapeDtypeStruct((OWN, 7168), BF),
        name="arrange",
    )(where, here, mate, near, far)


def shards(
    queries,
    span_latent,
    span_rope,
    pool_latent,
    pool_rope,
    page_table,
    cache_len,
    span_len,
    kv_up,
    out_weight,
):
    zi, yl, xi, yh, ci = (lax.axis_index(a) for a in ("z", "yl", "x", "yh", "c"))
    group = zi * 2 + yl
    member = (xi * 2 + yh) * 2 + ci
    device = group * 16 + member
    slots = pool_latent.shape[0]
    pages = page_table.shape[1]
    swap_c = step("c", 2, 1)
    swap_yl = step("yl", 2, 1)
    swap_yh = step("yh", 2, 1)

    owners = page_table // slots
    slot_of = page_table % slots
    order = jnp.arange(pages, dtype=jnp.int32)
    marked = order[None, :] * slots + slot_of
    owned = owners == device
    first = jnp.min(jnp.where(owned, marked, pages * slots), axis=1)
    last = jnp.max(jnp.where(owned, marked, 0), axis=1)
    picked = jnp.stack([first % slots, last % slots], 1).reshape(32)
    sent_pages, fresh = pack(
        picked,
        pool_latent,
        pool_rope.reshape(slots, PAGE, ROPE),
        jnp.pad(jnp.concatenate([span_latent, swap_yh(span_latent)], 0), ((0, 0), (0, 4), (0, 0))),
        jnp.pad(jnp.concatenate([span_rope, swap_yh(span_rope)], 0), ((0, 0), (0, 4), (0, 0))),
    )
    back = lax.all_to_all(sent_pages, ("z", "yl", "yh"), split_axis=0, concat_axis=0, tiled=True)

    turned = out_weight.T
    kept = lax.dynamic_slice_in_dim(turned, ci * 224, 224, 0)
    given = lax.dynamic_slice_in_dim(turned, (1 - ci) * 224, 224, 0)
    columns = jnp.concatenate([kept, swap_c(given)], 0)
    columns, back = lax.optimization_barrier((columns, back))
    weight = lax.all_gather(columns, "z", axis=0, tiled=False)

    mine = jnp.concatenate([back, fresh], 0)
    half = PIECE // 2
    left = step("x", 4, 1)(mine)
    right = step("x", 4, -1)(mine)

    sent = split_queries(queries[0])
    sent, back = lax.optimization_barrier((sent, back))
    exchanged = lax.all_to_all(sent, ("x", "yh", "c"), split_axis=0, concat_axis=0, tiled=True)
    q = exchanged.reshape(SPAN, HEADS_HERE * QHEAD)
    mine_c = swap_c(mine)
    left, right, q = lax.optimization_barrier((left, right, q))
    far_a = step("x", 4, 1)(left[:half])
    far_b = step("x", 4, -1)(right[half:])
    left_c, right_c = swap_c(left), swap_c(right)
    pieces = [mine, left, right, far_a, far_b, mine_c, left_c, right_c, swap_c(far_a), swap_c(far_b)]

    my_table = lax.dynamic_index_in_dim(page_table, group, 0, keepdims=False)
    source = my_table // slots
    before = (source[None, :] == source[:, None]) & (order[None, :] < order[:, None])
    place = jnp.minimum(jnp.sum(before.astype(jnp.int32), axis=1), 1)
    from_group = source // 16
    from_member = source % 16

    def piece_index(of_member):
        apart = (of_member // 4 - xi) % 4
        number = jnp.where(apart == 0, 0, jnp.where(apart == 3, 1, jnp.where(apart == 1, 2, 3)))
        return (jnp.where(of_member % 2 == ci, 0, 4) + number) * PIECE

    block = piece_index(from_member) + from_group * 2 + (from_member // 2) % 2
    members = jnp.arange(32, dtype=jnp.int32) // 2
    block_new = piece_index(members) + 32 + jnp.where((members // 2) % 2 == yh, 0, 1)
    index = jnp.concatenate([block * 2 + place, block_new * 2 + jnp.arange(32, dtype=jnp.int32) % 2])

    lens = jnp.stack(
        [
            lax.dynamic_index_in_dim(cache_len, group, 0, keepdims=False),
            lax.dynamic_index_in_dim(span_len, group, 0, keepdims=False),
        ]
    )
    attended = attend(lens, index, q, kv_up, pieces)
    near = swap_yl(attended)
    partial = project(attended, near, swap_c(attended), swap_c(near), weight)
    shared = lax.all_to_all(partial, ("x", "yh"), split_axis=0, concat_axis=0, tiled=True)
    where = jnp.stack([yl, ci]).astype(jnp.int32)
    here, to_c, to_yl, to_both = total_parts(where, shared)
    from_both = lax.ppermute(to_both, ("yl", "c"), [(i, 3 - i) for i in range(4)])
    out = arrange(where, here, swap_c(to_c), swap_yl(to_yl), from_both)
    return out[None]


def solution(mesh):
    fine = Mesh(mesh.devices.reshape(8, 2, 4, 2, 2), ("z", "yl", "x", "yh", "c"))
    grp, head = ("z", "yl"), ("x", "yh", "c")
    return jax.shard_map(
        shards,
        mesh=fine,
        in_specs=(
            P(grp, head, None),
            P(grp, head, None),
            P(grp, head, None),
            P(grp + head, None, None),
            P(grp + head, None),
            P(),
            P(),
            P(),
            P(None, head),
            P(head, grp),
        ),
        out_specs=P(grp, head, None),
        check_vma=False,
    )
```

time: 211 us -> 186 us (0.88)
  blocking collectives: 35.8 us -> 0 us
  local copies, waits for them, and re-layouts: 30.8 us -> 11.3 us
  Pallas kernels: 27.5 us -> 40.5 us
  starting transfers between devices: 32.6 us -> 44.1 us
  waiting for transfers between devices: 63.6 us -> 68.2 us
    all_to_all x1 -> x0, blocking collectives: 35.8 us -> none  [shards(): lax.all_to_all(send, ('z', 'yl', 'yh'), split_axis=0, concat_axis=0, tile...]
    all_to_all x0 -> x1, waiting for transfers between devices: none -> 12.1 us  [shards(): lax.all_to_all(sent_pages, ('z', 'yl', 'yh'), split_axis=0, concat_axis=0...]
    all_to_all x0 -> x1, starting transfers between devices: none -> 9.91 us  [shards(): lax.all_to_all(sent_pages, ('z', 'yl', 'yh'), split_axis=0, concat_axis=0...]
    pallas_call x1 -> x4, Pallas kernels: 4.54 us -> 12.9 us  [the longest x1 5.98 us: project(): pl.pallas_call(project_body, grid=(2,), in_specs=[pl.BlockSpec((SPAN, 102...]
    ppermute x11 -> x17, waiting for transfers between devices: 30.8 us -> 24.3 us  [send(): lax.ppermute(value, axis, [(i, (i + by) % count) for i in range(count)])]
    concatenate x3 -> x1, local copies, waits for them, and re-layouts: 6 us -> 0.01 us  [shards(): mine = jnp.concatenate([back, fresh], 0)]
    gather x4 -> x0, local copies, waits for them, and re-layouts: 5.56 us -> none  [the longest x1 3.69 us: shards(): cache = both.reshape(8 * 68, PAGE, WIDTH)[flat].reshape(CTX, WIDTH)]
    pallas_call x1, Pallas kernels: 19.7 us -> 24.3 us  [attend(): pl.pallas_call(attend_body, grid_spec=pltpu.PrefetchScalarGridSpec(num_sc...]
  transfers between devices with their start and end apart: 15 -> 22, of which waited for: 10 -> 12; matrix products, arithmetic and copies ran while one was open for 13% -> 6% of each run, Pallas kernels for 11% -> 15%
where the time goes in v2:
time: 186 us; the launch traced here: 185 us
  waiting for transfers between devices  68.2 us (37%)
  starting transfers between devices  44.1 us (24%)
  Pallas kernels  40.5 us (22%)
  between operations  13.6 us (7%)
  local copies, waits for them, and re-layouts  11.3 us (6%)
  other arithmetic  7.47 us (4%)
    pallas_call x1, Pallas kernels, attend(): pl.pallas_call(attend_body, grid_spec=pltpu.PrefetchScalarGridSpec(num_sc...  24.3 us
    ppermute x17, waiting for transfers between devices, send(): lax.ppermute(value, axis, [(i, (i + by) % count) for i in range(count)])  24.3 us
    all_to_all x1, waiting for transfers between devices, shards(): lax.all_to_all(partial, ('x', 'yh'), split_axis=0, concat_axis=0, tiled=T...  19.7 us
    ppermute x17, starting transfers between devices, send(): lax.ppermute(value, axis, [(i, (i + by) % count) for i in range(count)])  17.6 us
    all_to_all x1, waiting for transfers between devices, shards(): lax.all_to_all(sent_pages, ('z', 'yl', 'yh'), split_axis=0, concat_axis=0...  12.1 us
    all_to_all x1, waiting for transfers between devices, shards(): lax.all_to_all(sent, ('x', 'yh', 'c'), split_axis=0, concat_axis=0, tiled...  10.8 us
    all_to_all x1, starting transfers between devices, shards(): lax.all_to_all(sent_pages, ('z', 'yl', 'yh'), split_axis=0, concat_axis=0...  9.91 us
    all_to_all x1, starting transfers between devices, shards(): lax.all_to_all(sent, ('x', 'yh', 'c'), split_axis=0, concat_axis=0, tiled...  9.17 us
  transfers between devices with their start and end apart: 22, of which 12 were waited for; matrix products, arithmetic and copies ran while one was open for 6% of the time, Pallas kernels for 15%

profile of v2, /device:TPU:1, one launch (start us, length us, event | category | flops | bytes accessed | tf_op | source)
XLA Modules:
  0.0 185.2 jit_solution(9074112483261030172)
XLA Ops:
  6.5 3.7 %collective-permute-start.1 = (bf16[1,12,512]{2,1,0:T(8,128)(2,1)}, bf16[1,12,512]{2,1,0:T(8,128)(2,1)S(1)}, u32[]{:S(2)}, u32[]{:S(2)}) collective-permute-start(bf16[1,12,512]{2,1,0:T(8,128)(2,1)} %param.11), channel_id=1, source_target_pairs={{0,2},{2,0},{1,3},{3,1},{4,6},{6,4},{5,7},{7,5},{8,10},{10,8},{9,1... | collective-permute-start | bytes 36872 | tf_op jit(solution)/shard_map/ppermute | solution.py:27
  10.3 0.0 collective-permute-start.2
  10.3 0.8 select_reduce_fusion.1
  11.2 0.1 copy.13
  11.3 0.7 reshape.116.slot_ref
  12.0 1.5 reshape.117.rope_ref
  13.5 1.3 collective-permute-done.2
  14.8 1.3 fusion.10.span_rope_ref
  16.1 1.3 fusion.3.span_ref
  17.4 3.0 %pack.1 = (bf16[32,72,128]{2,1,0:T(8,128)(2,1)}, bf16[2,72,128]{2,1,0:T(8,128)(2,1)}) custom-call(s32[32]{0:T(128)} %reshape.116.slot_ref, bf16[32,8,512]{2,1,0:T(8,128)(2,1)} %pool_ref.1, bf16[32,8,64]{2,1,0:T(8,128)(2,1)} %reshape.117.rope_ref, bf16[2,16,512]{2,1,0:T(8,128)(2,1)} %fusion.3.span_ref, bf16[2,16,64]{2,1,0:T(8,128)(2,1)} %fusion.10.span_rope_ref), custom_call_target="tpu_custom_call" | custom-call | tf_op jit(solution)/shard_map/pack/pallas_call | solution.py:77
  20.4 9.9 %all-to-all-start = ((bf16[32,72,128]{2,1,0:T(8,128)(2,1)}), bf16[32,72,128]{2,1,0:T(8,128)(2,1)S(1)}, u32[]{:S(2)}, u32[]{:S(2)}) async-start(bf16[32,72,128]{2,1,0:T(8,128)(2,1)} %get-tuple-element.17), calls=%async_computation | async-start | bytes 1179648 | tf_op jit(solution)/shard_map/all_to_all | solution.py:309
  30.3 0.0 all-gather.3.cloned.1.call-start
  30.4 0.1 dynamic-slice_bitcast_fusion.1
  30.4 1.6 collective-permute-start
  32.0 1.4 collective-permute-done
  33.5 1.1 pad_maximum_fusion
  34.6 12.1 %all-to-all-done = bf16[32,72,128]{2,1,0:T(8,128)(2,1)S(1)} async-done(((bf16[32,72,128]{2,1,0:T(8,128)(2,1)}), bf16[32,72,128]{2,1,0:T(8,128)(2,1)S(1)}, u32[]{:S(2)}, u32[]{:S(2)}) %all-to-all-start) | async-done | bytes 589856 | tf_op jit(solution)/shard_map/all_to_all | solution.py:309
  46.7 0.0 all-gather.3.cloned.1.call-update
  46.8 0.0 copy-start.8
  46.8 0.0 copy-start.9
  46.8 1.3 collective-permute-start.3
  48.1 1.5 collective-permute-start.4
  49.6 3.3 %split_queries.1 = bf16[16,12,1536]{2,1,0:T(8,128)(2,1)} custom-call(bf16[12,24576]{1,0:T(8,128)(2,1)} %bitcast.16), custom_call_target="tpu_custom_call" | custom-call | tf_op jit(solution)/shard_map/split_queries/pallas_call | solution.py:38
  52.9 9.2 %all-to-all-start.1 = ((bf16[16,12,1536]{2,1,0:T(8,128)(2,1)}), bf16[16,12,1536]{2,1,0:T(8,128)(2,1)}, u32[]{:S(2)}, u32[]{:S(2)}) async-start(bf16[16,12,1536]{2,1,0:T(8,128)(2,1)} %split_queries.1), calls=%async_computation.1 | async-start | bytes 1572864 | tf_op jit(solution)/shard_map/all_to_all | solution.py:325
  62.0 0.6 dynamic_slice.18
  62.6 0.6 dynamic_slice.17
  63.2 1.3 pad_add_fusion.3.lens_ref
  64.6 0.7 and_select_fusion
  65.3 0.2 collective-permute-start.7
  65.5 10.8 %all-to-all-done.1 = bf16[16,12,1536]{2,1,0:T(8,128)(2,1)} async-done(((bf16[16,12,1536]{2,1,0:T(8,128)(2,1)}), bf16[16,12,1536]{2,1,0:T(8,128)(2,1)}, u32[]{:S(2)}, u32[]{:S(2)}) %all-to-all-start.1) | async-done | bytes 589856 | tf_op jit(solution)/shard_map/all_to_all | solution.py:325
  76.3 1.3 reshape.118.q_ref
  77.6 0.0 collective-permute-done.3.rest_1_
  77.6 1.2 collective-permute-start.8
  78.9 0.1 collective-permute-start.9
  79.0 0.1 collective-permute-start.5
  79.1 2.7 %collective-permute-start.6 = (bf16[17,72,128]{2,1,0:T(8,128)(2,1)S(1)}, bf16[17,72,128]{2,1,0:T(8,128)(2,1)S(1)}, u32[]{:S(2)}, u32[]{:S(2)}) collective-permute-start(bf16[17,72,128]{2,1,0:T(8,128)(2,1)S(1)} %slice.7), channel_id=1, source_target_pairs={{0,12},{4,0},{8,4},{12,8},{1,13},{5,1},{9,5},{13,9},{2,14},{6,2},{... | collective-permute-start | bytes 940040 | tf_op jit(solution)/shard_map/ppermute | solution.py:27
  81.7 0.2 convert_reduce_fusion
  81.9 7.0 %collective-permute-done.5.rest_3_ = bf16[17,72,128]{2,1,0:T(8,128)(2,1)S(1)} collective-permute-done((bf16[17,72,128]{2,1,0:T(8,128)(2,1)S(1)}, bf16[17,72,128]{2,1,0:T(8,128)(2,1)S(1)}, u32[]{:S(2)}, u32[]{:S(2)}) %collective-permute-start.5) | collective-permute-done | bytes 313376 | tf_op jit(solution)/shard_map/ppermute | solution.py:27
  88.9 1.2 collective-permute-start.10
  90.1 0.0 collective-permute-done.6.rest_4_
  90.1 0.0 collective-permute-start.11
  90.2 1.1 collective-permute-done.10.rest_8_
  91.3 0.4 collective-permute-done.11.rest_9_
  91.8 1.6 copy-done.1
  93.4 24.3 %attend.1.own_ref = bf16[192,1024]{1,0:T(8,128)(2,1)S(1)} custom-call(s32[2]{0:T(128)S(1)} %pad_add_fusion.3.lens_ref, s32[288]{0:T(512)S(1)} %pad_add_fusion.index_ref, bf16[192,1536]{1,0:T(8,128)(2,1)S(1)} %reshape.118.q_ref, bf16[512,2048]{1,0:T(8,128)(2,1)S(1)} %copy-done.1, bf16[34,72,128]{2,1,0:T(8,128)(2,1)S(1)} %constant_dynamic-update-slice_fusion.rest_0_, ...), custom_call_target="tpu_custom_call" | custom-call | flops 8000000000 | bytes 6000000 | tf_op jit(solution)/shard_map/attend/pallas_call | solution.py:175
  117.7 0.4 collective-permute-start.12
  118.1 0.6 collective-permute-start.13
  118.7 9.5 %collective-permute-done.12.own_y_ref = bf16[192,1024]{1,0:T(8,128)(2,1)S(1)} collective-permute-done((bf16[192,1024]{1,0:T(8,128)(2,1)S(1)}, bf16[192,1024]{1,0:T(8,128)(2,1)S(1)}, u32[]{:S(2)}, u32[]{:S(2)}) %collective-permute-start.12) | collective-permute-done | bytes 393248 | tf_op jit(solution)/shard_map/ppermute | solution.py:27
  128.2 1.1 collective-permute-start.14
  129.3 1.3 collective-permute-done.14.mate_y_ref
  130.7 3.1 %copy-done = bf16[3584,1024]{1,0:T(8,128)(2,1)S(1)} copy-done((bf16[3584,1024]{1,0:T(8,128)(2,1)S(1)}, bf16[3584,1024]{1,0:T(8,128)(2,1)}, u32[]{:S(2)}) %copy-start) | copy-done | bytes 7340056
  133.8 6.0 %project.1 = bf16[8,2,24,1792]{3,2,1,0:T(8,128)(2,1)} custom-call(bf16[192,1024]{1,0:T(8,128)(2,1)S(1)} %attend.1.own_ref, bf16[192,1024]{1,0:T(8,128)(2,1)S(1)} %collective-permute-done.12.own_y_ref, bf16[192,1024]{1,0:T(8,128)(2,1)S(1)} %collective-permute-done.13.mate_ref, bf16[192,1024]{1,0:T(8,128)(2,1)S(1)} %collective-permute-done.14.mate_y_ref, ...), custom_call_target="tpu_custom_call" | custom-call | tf_op jit(solution)/shard_map/project/pallas_call | solution.py:216
  139.7 6.0 %all-to-all-start.2 = ((bf16[8,2,24,1792]{3,2,1,0:T(8,128)(2,1)}), bf16[8,2,24,1792]{3,2,1,0:T(8,128)(2,1)S(1)}, u32[]{:S(2)}, u32[]{:S(2)}) async-start(bf16[8,2,24,1792]{3,2,1,0:T(8,128)(2,1)} %project.1), calls=%async_computation.2 | async-start | bytes 2752512 | tf_op jit(solution)/shard_map/all_to_all | solution.py:360
  145.7 0.6 pad_add_fusion.2.where_ref
  146.3 19.7 %all-to-all-done.2.x_ref = bf16[8,2,24,1792]{3,2,1,0:T(8,128)(2,1)S(1)} async-done(((bf16[8,2,24,1792]{3,2,1,0:T(8,128)(2,1)}), bf16[8,2,24,1792]{3,2,1,0:T(8,128)(2,1)S(1)}, u32[]{:S(2)}, u32[]{:S(2)}) %all-to-all-start.2) | async-done | bytes 1376288 | tf_op jit(solution)/shard_map/all_to_all | solution.py:360
  166.0 1.1 copy-done.2
  167.0 2.2 %total_parts.1 = (bf16[12,1792]{1,0:T(8,128)(2,1)}, bf16[12,1792]{1,0:T(8,128)(2,1)}, bf16[12,1792]{1,0:T(8,128)(2,1)}, bf16[12,1792]{1,0:T(8,128)(2,1)}) custom-call(s32[2]{0:T(128)} %pad_add_fusion.2.where_ref, bf16[8,2,24,1792]{3,2,1,0:T(8,128)(2,1)} %copy-done.2), custom_call_target="tpu_custom_call" | custom-call | tf_op jit(solution)/shard_map/total_parts/pallas_call | solution.py:239
  169.3 1.6 collective-permute-start.15
  170.9 0.3 collective-permute-start.16
  171.2 1.3 collective-permute-start.17
  172.5 2.1 %collective-permute-done.16.y_ref = bf16[12,1792]{1,0:T(8,128)(2,1)S(1)} collective-permute-done((bf16[12,1792]{1,0:T(8,128)(2,1)}, bf16[12,1792]{1,0:T(8,128)(2,1)S(1)}, u32[]{:S(2)}, u32[]{:S(2)}) %collective-permute-start.16) | collective-permute-done | bytes 43040 | tf_op jit(solution)/shard_map/ppermute | solution.py:27
  174.7 1.3 collective-permute-done.17.both_ref
  176.0 0.6 copy-done.6
  176.6 1.7 arrange.1
  (33 shorter events, 0.3 us)
Async XLA Ops:
  6.5 23.8 %copy-start.3 = (bf16[1024,448]{0,1:T(8,128)(2,1)S(1)}, bf16[1024,448]{0,1:T(8,128)(2,1)}, u32[]{:S(2)}) copy-start(bf16[1024,448]{0,1:T(8,128)(2,1)} %param.19) | copy-start | bytes 2752516
  6.5 9.5 %collective-permute-start.1 = (bf16[1,12,512]{2,1,0:T(8,128)(2,1)}, bf16[1,12,512]{2,1,0:T(8,128)(2,1)S(1)}, u32[]{:S(2)}, u32[]{:S(2)}) collective-permute-start(bf16[1,12,512]{2,1,0:T(8,128)(2,1)} %param.11), channel_id=1, source_target_pairs={{0,2},{2,0},{1,3},{3,1},{4,6},{6,4},{5,7},{7,5},{8,10},{10,8},{9,1... | collective-permute-start | bytes 36872 | tf_op jit(solution)/shard_map/ppermute | solution.py:27
  10.3 4.5 %collective-permute-start.2 = (bf16[1,12,64]{2,1,0:T(8,128)(2,1)}, bf16[1,12,64]{2,1,0:T(8,128)(2,1)S(1)}, u32[]{:S(2)}, u32[]{:S(2)}) collective-permute-start(bf16[1,12,64]{2,1,0:T(8,128)(2,1)} %param.12), channel_id=1, source_target_pairs={{0,2},{2,0},{1,3},{3,1},{4,6},{6,4},{5,7},{7,5},{8,10},{10,8},{9,1... | collective-permute-start | bytes 4616 | tf_op jit(solution)/shard_map/ppermute | solution.py:27
  20.4 26.3 %all-to-all-start = ((bf16[32,72,128]{2,1,0:T(8,128)(2,1)}), bf16[32,72,128]{2,1,0:T(8,128)(2,1)S(1)}, u32[]{:S(2)}, u32[]{:S(2)}) async-start(bf16[32,72,128]{2,1,0:T(8,128)(2,1)} %get-tuple-element.17), calls=%async_computation | async-start | bytes 1179648 | tf_op jit(solution)/shard_map/all_to_all | solution.py:309
  30.3 100.4 %all-gather.3.cloned.1.call-start = ((), (), s32[]{:S(2)}) async-start(), calls=%async_computation.3 | async-start | bytes 8257536 | tf_op jit(solution)/shard_map/all_gather | solution.py:316
  30.4 3.0 %collective-permute-start = (bf16[224,1024]{1,0:T(8,128)(2,1)S(1)}, bf16[224,1024]{1,0:T(8,128)(2,1)S(1)}, u32[]{:S(2)}, u32[]{:S(2)}) collective-permute-start(bf16[224,1024]{1,0:T(8,128)(2,1)S(1)} %get-tuple-element.34), channel_id=1, source_target_pairs={{0,1},{1,0},{2,3},{3,2},{4,5},{5,4},{6,7},{7,6},{8,9},{9,8},{10,11... | collective-permute-start | bytes 1376264 | tf_op jit(solution)/shard_map/ppermute | solution.py:27
  33.5 13.3 %copy-start.7 = (bf16[2,72,128]{2,1,0:T(8,128)(2,1)S(1)}, bf16[2,72,128]{2,1,0:T(8,128)(2,1)}, u32[]{:S(2)}) copy-start(bf16[2,72,128]{2,1,0:T(8,128)(2,1)} %get-tuple-element.19) | copy-start | bytes 110596
  46.8 15.2 %copy-start.8 = (s32[16]{0:T(128)S(1)}, s32[16]{0:T(128)}, u32[]{:S(2)}) copy-start(s32[16]{0:T(128)} %param.17) | copy-start | bytes 196
  46.8 15.8 %copy-start.9 = (s32[16]{0:T(128)S(1)}, s32[16]{0:T(128)}, u32[]{:S(2)}) copy-start(s32[16]{0:T(128)} %param.16) | copy-start | bytes 196
  46.8 30.7 %collective-permute-start.3 = (bf16[34,72,128]{2,1,0:T(8,128)(2,1)S(1)}, bf16[34,72,128]{2,1,0:T(8,128)(2,1)S(1)}, u32[]{:S(2)}, u32[]{:S(2)}) collective-permute-start(bf16[34,72,128]{2,1,0:T(8,128)(2,1)S(1)} %constant_dynamic-update-slice_fusion.rest_0_), channel_id=1, source_target_pairs={{0,4},{4,8},{8,12},{12,0},{1,5},{5,9},{9,13},{13,1},{2,6},{6,10},{... | collective-permute-start | bytes 1880072 | tf_op jit(solution)/shard_map/ppermute | solution.py:27
  48.1 29.5 %collective-permute-start.4 = (bf16[34,72,128]{2,1,0:T(8,128)(2,1)S(1)}, bf16[34,72,128]{2,1,0:T(8,128)(2,1)S(1)}, u32[]{:S(2)}, u32[]{:S(2)}) collective-permute-start(bf16[34,72,128]{2,1,0:T(8,128)(2,1)S(1)} %constant_dynamic-update-slice_fusion.rest_0_), channel_id=1, source_target_pairs={{0,12},{4,0},{8,4},{12,8},{1,13},{5,1},{9,5},{13,9},{2,14},{6,2},{... | collective-permute-start | bytes 1880072 | tf_op jit(solution)/shard_map/ppermute | solution.py:27
  52.9 23.4 %all-to-all-start.1 = ((bf16[16,12,1536]{2,1,0:T(8,128)(2,1)}), bf16[16,12,1536]{2,1,0:T(8,128)(2,1)}, u32[]{:S(2)}, u32[]{:S(2)}) async-start(bf16[16,12,1536]{2,1,0:T(8,128)(2,1)} %split_queries.1), calls=%async_computation.1 | async-start | bytes 1572864 | tf_op jit(solution)/shard_map/all_to_all | solution.py:325
  65.3 24.9 %collective-permute-start.7 = (bf16[34,72,128]{2,1,0:T(8,128)(2,1)S(1)}, bf16[34,72,128]{2,1,0:T(8,128)(2,1)S(1)}, u32[]{:S(2)}, u32[]{:S(2)}) collective-permute-start(bf16[34,72,128]{2,1,0:T(8,128)(2,1)S(1)} %constant_dynamic-update-slice_fusion.rest_0_), channel_id=1, source_target_pairs={{0,1},{1,0},{2,3},{3,2},{4,5},{5,4},{6,7},{7,6},{8,9},{9,8},{10,11... | collective-permute-start | bytes 1880072 | tf_op jit(solution)/shard_map/ppermute | solution.py:27
  77.6 12.5 %collective-permute-start.8 = (bf16[34,72,128]{2,1,0:T(8,128)(2,1)S(1)}, bf16[34,72,128]{2,1,0:T(8,128)(2,1)S(1)}, u32[]{:S(2)}, u32[]{:S(2)}) collective-permute-start(bf16[34,72,128]{2,1,0:T(8,128)(2,1)S(1)} %collective-permute-done.3.rest_1_), channel_id=1, source_target_pairs={{0,1},{1,0},{2,3},{3,2},{4,5},{5,4},{6,7},{7,6},{8,9},{9,8},{10,11... | collective-permute-start | bytes 1880072 | tf_op jit(solution)/shard_map/ppermute | solution.py:27
  78.9 11.3 %collective-permute-start.9 = (bf16[34,72,128]{2,1,0:T(8,128)(2,1)S(1)}, bf16[34,72,128]{2,1,0:T(8,128)(2,1)S(1)}, u32[]{:S(2)}, u32[]{:S(2)}) collective-permute-start(bf16[34,72,128]{2,1,0:T(8,128)(2,1)S(1)} %collective-permute-done.4.rest_2_), channel_id=1, source_target_pairs={{0,1},{1,0},{2,3},{3,2},{4,5},{5,4},{6,7},{7,6},{8,9},{9,8},{10,11... | collective-permute-start | bytes 1880072 | tf_op jit(solution)/shard_map/ppermute | solution.py:27
  79.0 9.9 %collective-permute-start.5 = (bf16[17,72,128]{2,1,0:T(8,128)(2,1)S(1)}, bf16[17,72,128]{2,1,0:T(8,128)(2,1)S(1)}, u32[]{:S(2)}, u32[]{:S(2)}) collective-permute-start(bf16[17,72,128]{2,1,0:T(8,128)(2,1)S(1)} %slice.6), channel_id=1, source_target_pairs={{0,4},{4,8},{8,12},{12,0},{1,5},{5,9},{9,13},{13,1},{2,6},{6,10},{... | collective-permute-start | bytes 940040 | tf_op jit(solution)/shard_map/ppermute | solution.py:27
  79.1 11.0 %collective-permute-start.6 = (bf16[17,72,128]{2,1,0:T(8,128)(2,1)S(1)}, bf16[17,72,128]{2,1,0:T(8,128)(2,1)S(1)}, u32[]{:S(2)}, u32[]{:S(2)}) collective-permute-start(bf16[17,72,128]{2,1,0:T(8,128)(2,1)S(1)} %slice.7), channel_id=1, source_target_pairs={{0,12},{4,0},{8,4},{12,8},{1,13},{5,1},{9,5},{13,9},{2,14},{6,2},{... | collective-permute-start | bytes 940040 | tf_op jit(solution)/shard_map/ppermute | solution.py:27
  88.9 2.4 %collective-permute-start.10 = (bf16[17,72,128]{2,1,0:T(8,128)(2,1)S(1)}, bf16[17,72,128]{2,1,0:T(8,128)(2,1)S(1)}, u32[]{:S(2)}, u32[]{:S(2)}) collective-permute-start(bf16[17,72,128]{2,1,0:T(8,128)(2,1)S(1)} %collective-permute-done.5.rest_3_), channel_id=1, source_target_pairs={{0,1},{1,0},{2,3},{3,2},{4,5},{5,4},{6,7},{7,6},{8,9},{9,8},{10,11... | collective-permute-start | bytes 940040 | tf_op jit(solution)/shard_map/ppermute | solution.py:27
  90.1 1.7 collective-permute-start.11
  91.8 1.6 copy-start.1
  117.7 10.5 %collective-permute-start.12 = (bf16[192,1024]{1,0:T(8,128)(2,1)S(1)}, bf16[192,1024]{1,0:T(8,128)(2,1)S(1)}, u32[]{:S(2)}, u32[]{:S(2)}) collective-permute-start(bf16[192,1024]{1,0:T(8,128)(2,1)S(1)} %attend.1.own_ref), channel_id=1, source_target_pairs={{0,16},{16,0},{1,17},{17,1},{2,18},{18,2},{3,19},{19,3},{4,20},{20... | collective-permute-start | bytes 1179656 | tf_op jit(solution)/shard_map/ppermute | solution.py:27
  118.1 11.2 %collective-permute-start.13 = (bf16[192,1024]{1,0:T(8,128)(2,1)S(1)}, bf16[192,1024]{1,0:T(8,128)(2,1)S(1)}, u32[]{:S(2)}, u32[]{:S(2)}) collective-permute-start(bf16[192,1024]{1,0:T(8,128)(2,1)S(1)} %attend.1.own_ref), channel_id=1, source_target_pairs={{0,1},{1,0},{2,3},{3,2},{4,5},{5,4},{6,7},{7,6},{8,9},{9,8},{10,11... | collective-permute-start | bytes 1179656 | tf_op jit(solution)/shard_map/ppermute | solution.py:27
  128.2 2.5 %collective-permute-start.14 = (bf16[192,1024]{1,0:T(8,128)(2,1)S(1)}, bf16[192,1024]{1,0:T(8,128)(2,1)S(1)}, u32[]{:S(2)}, u32[]{:S(2)}) collective-permute-start(bf16[192,1024]{1,0:T(8,128)(2,1)S(1)} %collective-permute-done.12.own_y_ref), channel_id=1, source_target_pairs={{0,1},{1,0},{2,3},{3,2},{4,5},{5,4},{6,7},{7,6},{8,9},{9,8},{10,11... | collective-permute-start | bytes 1179656 | tf_op jit(solution)/shard_map/ppermute | solution.py:27
  130.7 3.1 %copy-start = (bf16[3584,1024]{1,0:T(8,128)(2,1)S(1)}, bf16[3584,1024]{1,0:T(8,128)(2,1)}, u32[]{:S(2)}) copy-start(bf16[3584,1024]{1,0:T(8,128)(2,1)} %all-gather.3.cloned.1.call-done) | copy-start | bytes 22020100
  139.7 26.2 %all-to-all-start.2 = ((bf16[8,2,24,1792]{3,2,1,0:T(8,128)(2,1)}), bf16[8,2,24,1792]{3,2,1,0:T(8,128)(2,1)S(1)}, u32[]{:S(2)}, u32[]{:S(2)}) async-start(bf16[8,2,24,1792]{3,2,1,0:T(8,128)(2,1)} %project.1), calls=%async_computation.2 | async-start | bytes 2752512 | tf_op jit(solution)/shard_map/all_to_all | solution.py:360
  166.0 1.1 copy-start.2
  169.3 3.3 %collective-permute-start.15 = (bf16[12,1792]{1,0:T(8,128)(2,1)}, bf16[12,1792]{1,0:T(8,128)(2,1)S(1)}, u32[]{:S(2)}, u32[]{:S(2)}) collective-permute-start(bf16[12,1792]{1,0:T(8,128)(2,1)} %get-tuple-element.26), channel_id=1, source_target_pairs={{0,1},{1,0},{2,3},{3,2},{4,5},{5,4},{6,7},{7,6},{8,9},{9,8},{10,11... | collective-permute-start | bytes 129032 | tf_op jit(solution)/shard_map/ppermute | solution.py:27
  170.9 3.8 %collective-permute-start.16 = (bf16[12,1792]{1,0:T(8,128)(2,1)}, bf16[12,1792]{1,0:T(8,128)(2,1)S(1)}, u32[]{:S(2)}, u32[]{:S(2)}) collective-permute-start(bf16[12,1792]{1,0:T(8,128)(2,1)} %get-tuple-element.27), channel_id=1, source_target_pairs={{0,16},{16,0},{1,17},{17,1},{2,18},{18,2},{3,19},{19,3},{4,20},{20... | collective-permute-start | bytes 129032 | tf_op jit(solution)/shard_map/ppermute | solution.py:27
  171.2 4.8 %collective-permute-start.17 = (bf16[12,1792]{1,0:T(8,128)(2,1)}, bf16[12,1792]{1,0:T(8,128)(2,1)S(1)}, u32[]{:S(2)}, u32[]{:S(2)}) collective-permute-start(bf16[12,1792]{1,0:T(8,128)(2,1)} %get-tuple-element.28), channel_id=1, source_target_pairs={{0,17},{1,16},{16,1},{17,0},{2,19},{3,18},{18,3},{19,2},{4,21},{5,... | collective-permute-start | bytes 129032 | tf_op jit(solution)/shard_map/ppermute | solution.py:363
  172.5 3.4 %copy-start.4 = (bf16[12,1792]{1,0:T(8,128)(2,1)}, bf16[12,1792]{1,0:T(8,128)(2,1)S(1)}, u32[]{:S(2)}) copy-start(bf16[12,1792]{1,0:T(8,128)(2,1)S(1)} %collective-permute-done.15.c_ref) | copy-start | bytes 129028
  174.6 1.3 copy-start.5
  176.0 0.6 copy-start.6
Sparse Core Ops, SparseCore 0:
  46.9 83.3 all-gather.2

commit v3 on v2

v3 whole, which is shorter than its diff:
```python
import jax
import jax.numpy as jnp
from jax import lax
from jax.experimental import pallas as pl
from jax.experimental.pallas import tpu as pltpu
from jax.sharding import Mesh
from jax.sharding import PartitionSpec as P

LATENT = 512
ROPE = 64
NOPE = 128
VDIM = 128
PAGE = 8
QHEAD = NOPE + ROPE
HEADS_HERE = 8
SPAN = 192
OWN = 12
CTX = 2048
BF = jnp.bfloat16
F32 = jnp.float32
NEG = -1e30
LOG2E = 1.4426950408889634


def step(axis, count, by):
    def send(value):
        return lax.ppermute(value, axis, [(i, (i + by) % count) for i in range(count)])

    return send


def split_body(q_ref, o_ref):
    for part in range(16):
        o_ref[part] = q_ref[:, part * 1536 : (part + 1) * 1536]


def split_queries(q):
    vmem = pl.BlockSpec(memory_space=pltpu.VMEM)
    return pl.pallas_call(
        split_body,
        in_specs=[vmem],
        out_specs=vmem,
        out_shape=jax.ShapeDtypeStruct((16, OWN, 1536), BF),
        name="split_queries",
    )(q)


PIECE = 34
NT = (((1,), (1,)), ((), ()))
VMEM_BYTES = 56 * 1024 * 1024
ALLKEYS = CTX + 256
KWIDTH = LATENT + 2 * ROPE


def tiles_of(page):
    return jnp.concatenate([page[:, j * 128 : (j + 1) * 128] for j in range(4)], 0)


def pack_body(slot_ref, pool_ref, rope_ref, o_ref):
    def one(dest, carry):
        first = slot_ref[2 * dest]
        second = slot_ref[2 * dest + 1]
        tiles = jnp.concatenate([tiles_of(pool_ref[first]), tiles_of(pool_ref[second])], 0)
        rope = jnp.concatenate([rope_ref[first], rope_ref[second]], 1)
        for copy in range(2):
            o_ref[2 * dest + copy, :64] = tiles
            o_ref[2 * dest + copy, 64:] = rope
        return carry

    lax.fori_loop(0, 16, one, 0, unroll=2)


def pack(slots, pool, rope):
    vmem = pl.BlockSpec(memory_space=pltpu.VMEM)
    return pl.pallas_call(
        pack_body,
        in_specs=[pl.BlockSpec(memory_space=pltpu.SMEM), vmem, vmem],
        out_specs=vmem,
        out_shape=jax.ShapeDtypeStruct((32, 72, 128), BF),
        name="pack",
    )(slots, pool, rope)


def fresh_body(span_ref, span_rope_ref, pair_ref, pair_rope_ref, f_ref):
    gap = jnp.zeros((4, LATENT), F32)
    gap_rope = jnp.zeros((4, ROPE), F32)
    for k, (lat, rope) in enumerate(((span_ref, span_rope_ref), (pair_ref, pair_rope_ref))):
        x = jnp.concatenate([lat[0].astype(F32), gap], 0)
        y = jnp.concatenate([rope[0].astype(F32), gap_rope], 0)
        f_ref[k, :64] = jnp.concatenate([tiles_of(x[:8]), tiles_of(x[8:])], 0).astype(BF)
        f_ref[k, 64:] = jnp.concatenate([y[:8], y[8:]], 1).astype(BF)


def pack_fresh(*spans):
    vmem = pl.BlockSpec(memory_space=pltpu.VMEM)
    return pl.pallas_call(
        fresh_body,
        in_specs=[vmem] * 4,
        out_specs=vmem,
        out_shape=jax.ShapeDtypeStruct((2, 72, 128), BF),
        name="pack_fresh",
    )(*spans)


PLACES = ((0, 34), (34, 34), (68, 34), (102, 17), (119, 17))


def assemble_body(index_ref, *rest):
    pieces, keys, held, sems = rest[:10], rest[10], rest[11], rest[12]
    copies = []
    for n, piece in enumerate(pieces):
        start, size = PLACES[n % 5]
        start += 136 * (n // 5)
        copies.append(pltpu.make_async_copy(piece, held.at[start : start + size], sems.at[n]))
    for copy in copies:
        copy.start()
    for copy in copies:
        copy.wait()
    lane_half = lax.broadcasted_iota(jnp.int32, (8, 128), 1) // 64

    def pair(i, carry):
        lat, rope = [], []
        for k in range(2):
            at = index_ref[2 * i + k]
            block = at // 2
            place = at % 2
            lat.append(held[block, pl.ds(pl.multiple_of(place * 32, 32), 32), :])
            rope.append(jnp.where(lane_half == place, held[block, 64:72, :], jnp.zeros((), BF)))
        rows = pl.ds(pl.multiple_of(i * 16, 16), 16)
        for j in range(4):
            keys[rows, j * 128 : (j + 1) * 128] = jnp.concatenate(
                [lat[0][8 * j : 8 * j + 8], lat[1][8 * j : 8 * j + 8]], 0
            )
        keys[rows, LATENT:] = jnp.concatenate(rope, 0)
        return carry

    lax.fori_loop(0, ALLKEYS // 16, pair, 0, unroll=4)


def assemble(index, pieces):
    return pl.pallas_call(
        assemble_body,
        in_specs=[pl.BlockSpec(memory_space=pltpu.SMEM)] + [pl.BlockSpec(memory_space=pl.ANY)] * 10,
        out_specs=pl.BlockSpec(memory_space=pltpu.VMEM),
        out_shape=jax.ShapeDtypeStruct((ALLKEYS, KWIDTH), BF),
        scratch_shapes=[
            pltpu.VMEM((8 * PIECE, 72, 128), BF),
            pltpu.SemaphoreType.DMA((10,)),
        ],
        compiler_params=pltpu.CompilerParams(vmem_limit_bytes=24 * 1024 * 1024),
        cost_estimate=pl.CostEstimate(flops=0, bytes_accessed=16_000_000, transcendentals=0),
        name="assemble",
    )(index, *pieces)


def attend_body(lens_ref, q_ref, up_ref, keys, o_ref, qcat, causal):
    cached = lens_ref[0]
    appended = lens_ref[1]
    scale = LOG2E * (QHEAD**-0.5)

    @pl.when(pl.program_id(0) == 0)
    def prepare():
        row = lax.broadcasted_iota(jnp.int32, (SPAN, 256), 0)
        col = lax.broadcasted_iota(jnp.int32, (SPAN, 256), 1)
        token = col % 16
        seen = (token < OWN) & (col // 16 * OWN + token <= row)
        causal[...] = jnp.where(seen, 0.0, NEG).astype(F32)

    for h in range(2):
        rows = slice(h * SPAN, (h + 1) * SPAN)
        plain = q_ref[:, h * QHEAD : h * QHEAD + NOPE]
        key_up = up_ref[:, h * 256 : h * 256 + NOPE]
        qcat[rows, :LATENT] = lax.dot_general(plain, key_up, NT, preferred_element_type=F32).astype(BF)
        rope = q_ref[:, h * QHEAD + NOPE : (h + 1) * QHEAD]
        qcat[rows, LATENT:] = jnp.concatenate([rope, rope], 1)
    s = lax.dot_general(qcat[...], keys[...], NT, preferred_element_type=F32)
    at = lax.broadcasted_iota(jnp.int32, (1, CTX), 1)
    s = jnp.concatenate(
        [
            s[:, :CTX] + jnp.where(at < cached, 0.0, NEG),
            s[:, CTX:] + jnp.concatenate([causal[...], causal[...]], 0),
        ],
        1,
    )
    highest = jnp.max(s, axis=1, keepdims=True)
    p = jnp.exp2((s - highest) * scale)
    total = jnp.sum(p, axis=1, keepdims=True)
    mixed = jnp.dot(p.astype(BF), keys[:, :LATENT], preferred_element_type=F32)
    mixed = (mixed / total).astype(BF)
    live = lax.broadcasted_iota(jnp.int32, (SPAN, 1), 0) < appended
    for h in range(2):
        value_up = up_ref[:, h * 256 + NOPE : (h + 1) * 256]
        out = jnp.dot(mixed[h * SPAN : (h + 1) * SPAN], value_up, preferred_element_type=F32)
        o_ref[:, h * VDIM : (h + 1) * VDIM] = jnp.where(live, out, 0.0).astype(BF)


def attend(half, lens, q, up, keys):
    return pl.pallas_call(
        attend_body,
        grid_spec=pltpu.PrefetchScalarGridSpec(
            num_scalar_prefetch=1,
            grid=(2,),
            in_specs=[
                pl.BlockSpec((SPAN, 2 * QHEAD), lambda i, s: (0, 2 * half + i)),
                pl.BlockSpec((LATENT, 512), lambda i, s: (0, 2 * half + i)),
                pl.BlockSpec((ALLKEYS, KWIDTH), lambda i, s: (0, 0)),
            ],
            out_specs=pl.BlockSpec((SPAN, 256), lambda i, s: (0, i)),
            scratch_shapes=[
                pltpu.VMEM((2 * SPAN, KWIDTH), BF),
                pltpu.VMEM((SPAN, 256), F32),
            ],
        ),
        out_shape=jax.ShapeDtypeStruct((SPAN, 512), BF),
        compiler_params=pltpu.CompilerParams(vmem_limit_bytes=40 * 1024 * 1024),
        cost_estimate=pl.CostEstimate(
            flops=5_000_000_000, bytes_accessed=4_000_000, transcendentals=1_800_000
        ),
        name="attend",
    )(lens, q, up, keys)


def project_body(*refs):
    parts, w_ref, o_ref = refs[:8], refs[8], refs[9]
    own, near, mate, mate_near = (
        jnp.concatenate([parts[2 * k][...], parts[2 * k + 1][...]], 1) for k in range(4)
    )
    total = lax.dot_general(
        jnp.concatenate([own, near], 0),
        w_ref[:, :224].reshape(896, 1024),
        NT,
        preferred_element_type=F32,
    ) + lax.dot_general(
        jnp.concatenate([mate, mate_near], 0),
        w_ref[:, 224:].reshape(896, 1024),
        NT,
        preferred_element_type=F32,
    )
    for request in range(2):
        for place in range(8):
            at = request * SPAN + place * 24
            o_ref[place, request] = total[at : at + 24].astype(BF)


def project(parts, weight):
    return pl.pallas_call(
        project_body,
        grid=(2,),
        in_specs=[pl.BlockSpec((SPAN, 512), lambda i: (0, 0))] * 8
        + [pl.BlockSpec((4, 448, 1024), lambda i: (i, 0, 0))],
        out_specs=pl.BlockSpec((8, 2, 24, 896), lambda i: (0, 0, 0, i)),
        out_shape=jax.ShapeDtypeStruct((8, 2, 24, 1792), BF),
        compiler_params=pltpu.CompilerParams(vmem_limit_bytes=VMEM_BYTES),
        name="project",
    )(*parts, weight)


def total_body(where_ref, x_ref, *outs):
    core = where_ref[1]
    for request in range(2):
        value = jnp.sum(x_ref[:, request].astype(F32), axis=0)
        low, high = value[:OWN], value[OWN:]
        outs[2 * request][...] = jnp.where(core == 0, low, high).astype(BF)
        outs[2 * request + 1][...] = jnp.where(core == 0, high, low).astype(BF)


def total_parts(where, shared):
    vmem = pl.BlockSpec(memory_space=pltpu.VMEM)
    return pl.pallas_call(
        total_body,
        in_specs=[pl.BlockSpec(memory_space=pltpu.SMEM), vmem],
        out_specs=[vmem] * 4,
        out_shape=[jax.ShapeDtypeStruct((OWN, 1792), BF)] * 4,
        name="total_parts",
    )(where, shared)


def arrange_body(where_ref, here_ref, c_ref, y_ref, both_ref, o_ref):
    yl, core = where_ref[0], where_ref[1]
    here, mate, near, far = (r[...].astype(F32) for r in (here_ref, c_ref, y_ref, both_ref))
    same = (jnp.where(core == 0, here, mate), jnp.where(core == 0, mate, here))
    other = (jnp.where(core == 0, near, far), jnp.where(core == 0, far, near))
    parts = [jnp.where(yl == 0, same[k], other[k]) for k in range(2)]
    parts += [jnp.where(yl == 0, other[k], same[k]) for k in range(2)]
    for z in range(8):
        o_ref[:, z * 896 : (z + 1) * 896] = jnp.concatenate(
            [p[:, z * 224 : (z + 1) * 224] for p in parts], 1
        ).astype(BF)


def arrange(where, here, mate, near, far):
    vmem = pl.BlockSpec(memory_space=pltpu.VMEM)
    return pl.pallas_call(
        arrange_body,
        in_specs=[pl.BlockSpec(memory_space=pltpu.SMEM)] + [vmem] * 4,
        out_specs=vmem,
        out_shape=jax.ShapeDtypeStruct((OWN, 7168), BF),
        name="arrange",
    )(where, here, mate, near, far)


def shards(
    queries,
    span_latent,
    span_rope,
    pool_latent,
    pool_rope,
    page_table,
    cache_len,
    span_len,
    kv_up,
    out_weight,
):
    zi, yl, xi, yh, ci = (lax.axis_index(a) for a in ("z", "yl", "x", "yh", "c"))
    group = zi * 2 + yl
    member = (xi * 2 + yh) * 2 + ci
    device = group * 16 + member
    slots = pool_latent.shape[0]
    pages = page_table.shape[1]
    swap_c = step("c", 2, 1)
    swap_yl = step("yl", 2, 1)
    swap_yh = step("yh", 2, 1)

    pair_latent, pair_rope = swap_yh(span_latent), swap_yh(span_rope)
    owners = page_table // slots
    slot_of = page_table % slots
    order = jnp.arange(pages, dtype=jnp.int32)
    marked = order[None, :] * slots + slot_of
    owned = owners == device
    low = jnp.min(jnp.where(owned, marked, pages * slots), axis=1)
    high = jnp.max(jnp.where(owned, marked, 0), axis=1)
    picked = jnp.stack([low % slots, high % slots], 1).reshape(32)
    sent_pages = pack(picked, pool_latent, pool_rope.reshape(slots, PAGE, ROPE))
    back = lax.all_to_all(sent_pages, ("z", "yl", "yh"), split_axis=0, concat_axis=0, tiled=True)
    fresh = pack_fresh(span_latent, span_rope, pair_latent, pair_rope)
    sent = split_queries(queries[0])
    turned = out_weight.T
    kept = lax.dynamic_slice_in_dim(turned, ci * 224, 224, 0)
    given = lax.dynamic_slice_in_dim(turned, (1 - ci) * 224, 224, 0)
    columns = jnp.concatenate([kept, swap_c(given)], 0)
    back, fresh, sent, columns = lax.optimization_barrier((back, fresh, sent, columns))
    weight = lax.all_gather(columns, "z", axis=0, tiled=False)
    mine = jnp.concatenate([back, fresh], 0)
    half = PIECE // 2
    left = step("x", 4, 1)(mine)
    right = step("x", 4, -1)(mine)
    exchanged = lax.all_to_all(sent, ("x", "yh", "c"), split_axis=0, concat_axis=0, tiled=True)
    q = exchanged.reshape(SPAN, HEADS_HERE * QHEAD)
    mine_c = swap_c(mine)
    far_a = step("x", 4, 1)(left[:half])
    far_b = step("x", 4, -1)(right[half:])
    left_c, right_c = swap_c(left), swap_c(right)
    pieces = [mine, left, right, far_a, far_b, mine_c, left_c, right_c, swap_c(far_a), swap_c(far_b)]

    my_table = lax.dynamic_index_in_dim(page_table, group, 0, keepdims=False)
    source = my_table // slots
    before = (source[None, :] == source[:, None]) & (order[None, :] < order[:, None])
    place = jnp.minimum(jnp.sum(before.astype(jnp.int32), axis=1), 1)
    from_group = source // 16
    from_member = source % 16

    def piece_index(of_member):
        apart = (of_member // 4 - xi) % 4
        number = jnp.where(apart == 0, 0, jnp.where(apart == 3, 1, jnp.where(apart == 1, 2, 3)))
        return (jnp.where(of_member % 2 == ci, 0, 4) + number) * PIECE

    block = piece_index(from_member) + from_group * 2 + (from_member // 2) % 2
    members = jnp.arange(32, dtype=jnp.int32) // 2
    block_new = piece_index(members) + 32 + jnp.where((members // 2) % 2 == yh, 0, 1)
    index = jnp.concatenate([block * 2 + place, block_new * 2 + jnp.arange(32, dtype=jnp.int32) % 2])

    lens = jnp.stack(
        [
            lax.dynamic_index_in_dim(cache_len, group, 0, keepdims=False),
            lax.dynamic_index_in_dim(span_len, group, 0, keepdims=False),
        ]
    )
    keys = assemble(index, pieces)
    own = [attend(half, lens, q, kv_up, keys) for half in range(2)]
    near = [swap_yl(x) for x in own]
    partial = project([*own, *near, *[swap_c(x) for x in own], *[swap_c(x) for x in near]], weight)
    shared = lax.all_to_all(partial, ("x", "yh"), split_axis=0, concat_axis=0, tiled=True)
    where = jnp.stack([yl, ci]).astype(jnp.int32)
    here, to_c, to_yl, to_both = total_parts(where, shared)
    from_both = lax.ppermute(to_both, ("yl", "c"), [(i, 3 - i) for i in range(4)])
    out = arrange(where, here, swap_c(to_c), swap_yl(to_yl), from_both)
    return out[None]


def solution(mesh):
    fine = Mesh(mesh.devices.reshape(8, 2, 4, 2, 2), ("z", "yl", "x", "yh", "c"))
    grp, head = ("z", "yl"), ("x", "yh", "c")
    return jax.shard_map(
        shards,
        mesh=fine,
        in_specs=(
            P(grp, head, None),
            P(grp, head, None),
            P(grp, head, None),
            P(grp + head, None, None),
            P(grp + head, None),
            P(),
            P(),
            P(),
            P(None, head),
            P(head, grp),
        ),
        out_specs=P(grp, head, None),
        check_vma=False,
    )
```

time: 186 us -> 178 us (0.957)
  waiting for transfers between devices: 68.2 us -> 60.7 us
  starting transfers between devices: 44.1 us -> 49.5 us
  other arithmetic: 7.47 us -> 4.87 us
  Pallas kernels: 40.5 us -> 38.2 us
    ppermute x17 -> x20, waiting for transfers between devices: 24.3 us -> 14.6 us  [send(): lax.ppermute(value, axis, [(i, (i + by) % count) for i in range(count)])]
    pallas_call x1 -> x2, Pallas kernels: 24.3 us -> 15.6 us  [attend(): pl.pallas_call(attend_body, grid_spec=pltpu.PrefetchScalarGridSpec(num_sc...]
    all_gather x1, waiting for transfers between devices: 0.01 us -> 7.87 us  [shards(): weight = lax.all_gather(columns, 'z', axis=0, tiled=False)]
    ppermute x17 -> x20, starting transfers between devices: 17.6 us -> 25.1 us  [send(): lax.ppermute(value, axis, [(i, (i + by) % count) for i in range(count)])]
    pallas_call x2 -> x4, Pallas kernels: 9.24 us -> 16.3 us  [the longest x1 7.07 us: project(): pl.pallas_call(project_body, grid=(2,), in_specs=[pl.BlockSpec((SPAN, 512...]
    all_to_all x1, waiting for transfers between devices: 12.1 us -> 5.13 us  [shards(): lax.all_to_all(sent_pages, ('z', 'yl', 'yh'), split_axis=0, concat_axis=0...]
    all_to_all x1, starting transfers between devices: 9.17 us -> 4.54 us  [shards(): lax.all_to_all(sent, ('x', 'yh', 'c'), split_axis=0, concat_axis=0, tiled...]
    unnamed x21 -> x45, local copies, waits for them, and re-layouts: 6.47 us -> 3.04 us
  transfers between devices with their start and end apart: 22 -> 25, of which waited for: 12 -> 10; matrix products, arithmetic and copies ran while one was open for 6% -> 5% of each run, Pallas kernels for 15% -> 14%
where the time goes in v3:
time: 178 us; the launch traced here: 177 us
  waiting for transfers between devices  60.7 us (34%)
  starting transfers between devices  49.5 us (28%)
  Pallas kernels  38.2 us (21%)
  between operations  13.7 us (8%)
  local copies, waits for them, and re-layouts  10.1 us (6%)
  other arithmetic  4.87 us (3%)
    ppermute x20, starting transfers between devices, send(): lax.ppermute(value, axis, [(i, (i + by) % count) for i in range(count)])  25.1 us
    all_to_all x1, waiting for transfers between devices, shards(): lax.all_to_all(partial, ('x', 'yh'), split_axis=0, concat_axis=0, tiled=T...  19.6 us
    pallas_call x2, Pallas kernels, attend(): pl.pallas_call(attend_body, grid_spec=pltpu.PrefetchScalarGridSpec(num_sc...  15.6 us
    ppermute x20, waiting for transfers between devices, send(): lax.ppermute(value, axis, [(i, (i + by) % count) for i in range(count)])  14.6 us
    all_to_all x1, waiting for transfers between devices, shards(): lax.all_to_all(sent, ('x', 'yh', 'c'), split_axis=0, concat_axis=0, tiled...  12.2 us
    all_to_all x1, starting transfers between devices, shards(): lax.all_to_all(sent_pages, ('z', 'yl', 'yh'), split_axis=0, concat_axis=0...  12 us
    all_gather x1, waiting for transfers between devices, shards(): weight = lax.all_gather(columns, 'z', axis=0, tiled=False)  7.87 us
    pallas_call x1, Pallas kernels, project(): pl.pallas_call(project_body, grid=(2,), in_specs=[pl.BlockSpec((SPAN, 512...  7.07 us
  transfers between devices with their start and end apart: 25, of which 10 were waited for; matrix products, arithmetic and copies ran while one was open for 5% of the time, Pallas kernels for 14%

profile of v3, /device:TPU:1, one launch (start us, length us, event | category | flops | bytes accessed | tf_op | source)
XLA Modules:
  0.0 177.1 jit_solution(17352275100755528979)
XLA Ops:
  6.5 0.9 select_reduce_fusion.1
  7.5 0.1 copy.13
  7.6 0.7 reshape.116.slot_ref
  8.3 1.5 reshape.117.rope_ref
  9.8 2.4 %pack.1 = bf16[32,72,128]{2,1,0:T(8,128)(2,1)} custom-call(s32[32]{0:T(128)} %reshape.116.slot_ref, bf16[32,8,512]{2,1,0:T(8,128)(2,1)} %pool_ref.1, bf16[32,8,64]{2,1,0:T(8,128)(2,1)} %reshape.117.rope_ref), custom_call_target="tpu_custom_call" | custom-call | tf_op jit(solution)/shard_map/pack/pallas_call | solution.py:75
  12.1 12.0 %all-to-all-start = ((bf16[32,72,128]{2,1,0:T(8,128)(2,1)}), bf16[32,72,128]{2,1,0:T(8,128)(2,1)S(1)}, u32[]{:S(2)}, u32[]{:S(2)}) async-start(bf16[32,72,128]{2,1,0:T(8,128)(2,1)} %pack.1), calls=%async_computation | async-start | bytes 1179648 | tf_op jit(solution)/shard_map/all_to_all | solution.py:334
  24.2 0.0 all-gather.3.cloned.1.call-start
  24.2 0.1 dynamic-slice_bitcast_fusion.1
  24.3 1.0 collective-permute-start.2
  25.4 3.0 %collective-permute-start = (bf16[1,12,512]{2,1,0:T(8,128)(2,1)S(1)}, bf16[1,12,512]{2,1,0:T(8,128)(2,1)S(1)}, u32[]{:S(2)}, u32[]{:S(2)}) collective-permute-start(bf16[1,12,512]{2,1,0:T(8,128)(2,1)S(1)} %copy-done.16), channel_id=1, source_target_pairs={{0,2},{2,0},{1,3},{3,1},{4,6},{6,4},{5,7},{7,5},{8,10},{10,8},{9,1... | collective-permute-start | bytes 36872 | tf_op jit(solution)/shard_map/ppermute | solution.py:27
  28.4 0.1 collective-permute-start.1
  28.5 2.1 %split_queries.1 = bf16[16,12,1536]{2,1,0:T(8,128)(2,1)} custom-call(bf16[12,24576]{1,0:T(8,128)(2,1)} %bitcast.16), custom_call_target="tpu_custom_call" | custom-call | tf_op jit(solution)/shard_map/split_queries/pallas_call | solution.py:39
  30.6 2.2 %collective-permute-done.1.pair_rope_ref = bf16[1,12,64]{2,1,0:T(8,128)(2,1)S(1)} collective-permute-done((bf16[1,12,64]{2,1,0:T(8,128)(2,1)S(1)}, bf16[1,12,64]{2,1,0:T(8,128)(2,1)S(1)}, u32[]{:S(2)}, u32[]{:S(2)}) %collective-permute-start.1) | collective-permute-done | bytes 1568 | tf_op jit(solution)/shard_map/ppermute | solution.py:27
  32.8 0.0 collective-permute-done.pair_ref
  32.8 0.6 copy-done.19
  33.4 0.6 copy-done.17
  34.0 1.4 pack_fresh.1
  35.5 0.0 copy-start.21
  35.5 1.1 pad_maximum_fusion
  36.5 5.1 %all-to-all-done = bf16[32,72,128]{2,1,0:T(8,128)(2,1)S(1)} async-done(((bf16[32,72,128]{2,1,0:T(8,128)(2,1)}), bf16[32,72,128]{2,1,0:T(8,128)(2,1)S(1)}, u32[]{:S(2)}, u32[]{:S(2)}) %all-to-all-start) | async-done | bytes 589856 | tf_op jit(solution)/shard_map/all_to_all | solution.py:334
  41.7 0.0 all-gather.3.cloned.1.call-update
  41.8 1.3 collective-permute-start.3
  43.1 1.5 collective-permute-start.4
  44.5 0.6 dynamic_slice.18
  45.1 0.6 dynamic_slice.17
  45.7 0.7 and_select_fusion
  46.4 3.1 %collective-permute-start.7 = (bf16[34,72,128]{2,1,0:T(8,128)(2,1)S(1)}, bf16[34,72,128]{2,1,0:T(8,128)(2,1)S(1)}, u32[]{:S(2)}, u32[]{:S(2)}) collective-permute-start(bf16[34,72,128]{2,1,0:T(8,128)(2,1)S(1)} %constant_dynamic-update-slice_fusion.rest_0_), channel_id=1, source_target_pairs={{0,1},{1,0},{2,3},{3,2},{4,5},{5,4},{6,7},{7,6},{8,9},{9,8},{10,11... | collective-permute-start | bytes 1880072 | tf_op jit(solution)/shard_map/ppermute | solution.py:27
  49.5 6.8 %collective-permute-done.3.rest_1_ = bf16[34,72,128]{2,1,0:T(8,128)(2,1)S(1)} collective-permute-done((bf16[34,72,128]{2,1,0:T(8,128)(2,1)S(1)}, bf16[34,72,128]{2,1,0:T(8,128)(2,1)S(1)}, u32[]{:S(2)}, u32[]{:S(2)}) %collective-permute-start.3) | collective-permute-done | bytes 626720 | tf_op jit(solution)/shard_map/ppermute | solution.py:27
  56.3 0.8 slice.8
  57.1 0.7 slice.9
  57.8 2.7 %collective-permute-start.6 = (bf16[17,72,128]{2,1,0:T(8,128)(2,1)}, bf16[17,72,128]{2,1,0:T(8,128)(2,1)}, u32[]{:S(2)}, u32[]{:S(2)}) collective-permute-start(bf16[17,72,128]{2,1,0:T(8,128)(2,1)} %slice.9), channel_id=1, source_target_pairs={{0,12},{4,0},{8,4},{12,8},{1,13},{5,1},{9,5},{13,9},{2,14},{6,2},{... | collective-permute-start | bytes 940040 | tf_op jit(solution)/shard_map/ppermute | solution.py:27
  60.5 3.8 %collective-permute-start.8 = (bf16[34,72,128]{2,1,0:T(8,128)(2,1)S(1)}, bf16[34,72,128]{2,1,0:T(8,128)(2,1)S(1)}, u32[]{:S(2)}, u32[]{:S(2)}) collective-permute-start(bf16[34,72,128]{2,1,0:T(8,128)(2,1)S(1)} %collective-permute-done.3.rest_1_), channel_id=1, source_target_pairs={{0,1},{1,0},{2,3},{3,2},{4,5},{5,4},{6,7},{7,6},{8,9},{9,8},{10,11... | collective-permute-start | bytes 1880072 | tf_op jit(solution)/shard_map/ppermute | solution.py:27
  64.4 4.5 %all-to-all-start.1 = ((bf16[16,12,1536]{2,1,0:T(8,128)(2,1)}), bf16[16,12,1536]{2,1,0:T(8,128)(2,1)}, u32[]{:S(2)}, u32[]{:S(2)}) async-start(bf16[16,12,1536]{2,1,0:T(8,128)(2,1)} %split_queries.1), calls=%async_computation.1 | async-start | bytes 1572864 | tf_op jit(solution)/shard_map/all_to_all | solution.py:347
  68.9 1.3 pad_add_fusion.3.lens_ref
  70.2 0.2 convert_reduce_fusion
  70.4 0.4 collective-permute-start.10
  70.7 0.3 collective-permute-start.11
  71.1 12.2 %all-to-all-done.1 = bf16[16,12,1536]{2,1,0:T(8,128)(2,1)} async-done(((bf16[16,12,1536]{2,1,0:T(8,128)(2,1)}), bf16[16,12,1536]{2,1,0:T(8,128)(2,1)}, u32[]{:S(2)}, u32[]{:S(2)}) %all-to-all-start.1) | async-done | bytes 589856 | tf_op jit(solution)/shard_map/all_to_all | solution.py:347
  83.3 2.1 %reshape.118.q_ref = bf16[192,1536]{1,0:T(8,128)(2,1)} reshape(bf16[16,12,1536]{2,1,0:T(8,128)(2,1)} %all-to-all-done.1) | data formatting | bytes 1179648 | tf_op jit(solution)/shard_map/reshape | solution.py:348
  85.4 5.6 %assemble.1.keys = bf16[2304,640]{1,0:T(8,128)(2,1)S(1)} custom-call(s32[288]{0:T(512)S(1)} %pad_add_fusion.index_ref, bf16[34,72,128]{2,1,0:T(8,128)(2,1)S(1)} %constant_dynamic-update-slice_fusion.rest_0_, bf16[34,72,128]{2,1,0:T(8,128)(2,1)S(1)} %collective-permute-done.3.rest_1_, bf16[34,72,128]{2,1,0:T(8,128)(2,1)S(1)} %collective-permute-done.4.rest_2_, ...), custom_call_target="tpu_custom_call" | custom-call | bytes 16000000 | tf_op jit(solution)/shard_map/assemble/pallas_call | solution.py:141
  91.1 7.8 %attend.2.refs_0_ = bf16[192,512]{1,0:T(8,128)(2,1)S(1)} custom-call(s32[2]{0:T(128)S(1)} %pad_add_fusion.3.lens_ref, bf16[192,1536]{1,0:T(8,128)(2,1)S(1)} %copy-done, bf16[512,2048]{1,0:T(8,128)(2,1)S(1)} %copy-done.3, bf16[2304,640]{1,0:T(8,128)(2,1)S(1)} %assemble.1.keys), custom_call_target="tpu_custom_call" | custom-call | flops 5000000000 | bytes 4000000 | tf_op jit(solution)/shard_map/attend/pallas_call | solution.py:198
  98.9 0.0 copy-start.1
  98.9 1.0 collective-permute-start.12
  99.9 7.8 %attend.3.refs_1_ = bf16[192,512]{1,0:T(8,128)(2,1)S(1)} custom-call(s32[2]{0:T(128)S(1)} %pad_add_fusion.3.lens_ref, bf16[192,1536]{1,0:T(8,128)(2,1)S(1)} %copy-done, bf16[512,2048]{1,0:T(8,128)(2,1)S(1)} %copy-done.3, bf16[2304,640]{1,0:T(8,128)(2,1)S(1)} %assemble.1.keys), custom_call_target="tpu_custom_call" | custom-call | flops 5000000000 | bytes 4000000 | tf_op jit(solution)/shard_map/attend/pallas_call | solution.py:198
  107.7 0.7 collective-permute-start.13
  108.4 1.7 collective-permute-start.14
  110.1 0.5 collective-permute-start.16
  110.6 2.4 %collective-permute-done.13.refs_3_ = bf16[192,512]{1,0:T(8,128)(2,1)S(1)} collective-permute-done((bf16[192,512]{1,0:T(8,128)(2,1)S(1)}, bf16[192,512]{1,0:T(8,128)(2,1)S(1)}, u32[]{:S(2)}, u32[]{:S(2)}) %collective-permute-start.13) | collective-permute-done | bytes 196640 | tf_op jit(solution)/shard_map/ppermute | solution.py:27
  113.0 2.2 %collective-permute-start.17 = (bf16[192,512]{1,0:T(8,128)(2,1)S(1)}, bf16[192,512]{1,0:T(8,128)(2,1)S(1)}, u32[]{:S(2)}, u32[]{:S(2)}) collective-permute-start(bf16[192,512]{1,0:T(8,128)(2,1)S(1)} %collective-permute-done.13.refs_3_), channel_id=1, source_target_pairs={{0,1},{1,0},{2,3},{3,2},{4,5},{5,4},{6,7},{7,6},{8,9},{9,8},{10,11... | collective-permute-start | bytes 589832 | tf_op jit(solution)/shard_map/ppermute | solution.py:27
  115.2 1.0 collective-permute-done.17.refs_7_
  116.2 7.9 %all-gather.3.cloned.1.call-done = bf16[3584,1024]{1,0:T(8,128)(2,1)} async-done(((bf16[448,1024]{1,0:T(8,128)(2,1)}), bf16[3584,1024]{1,0:T(8,128)(2,1)}) %all-gather.3.cloned.1.call-update) | async-done | bytes 7340048 | tf_op jit(solution)/shard_map/all_gather | solution.py:342
  124.1 7.1 %project.1 = bf16[8,2,24,1792]{3,2,1,0:T(8,128)(2,1)} custom-call(bf16[192,512]{1,0:T(8,128)(2,1)} %copy-done.1, bf16[192,512]{1,0:T(8,128)(2,1)} %copy-done.2, bf16[192,512]{1,0:T(8,128)(2,1)} %copy-done.6, bf16[192,512]{1,0:T(8,128)(2,1)} %copy-done.7, bf16[192,512]{1,0:T(8,128)(2,1)} %copy-done.8, bf16[192,512]{1,0:T(8,128)(2,1)} %copy-done.9, ...), custom_call_target="tpu_custom_call" | custom-call | tf_op jit(solution)/shard_map/project/pallas_call | solution.py:246
  131.2 6.4 %all-to-all-start.2 = ((bf16[8,2,24,1792]{3,2,1,0:T(8,128)(2,1)}), bf16[8,2,24,1792]{3,2,1,0:T(8,128)(2,1)S(1)}, u32[]{:S(2)}, u32[]{:S(2)}) async-start(bf16[8,2,24,1792]{3,2,1,0:T(8,128)(2,1)} %project.1), calls=%async_computation.2 | async-start | bytes 2752512 | tf_op jit(solution)/shard_map/all_to_all | solution.py:382
  137.6 0.6 pad_add_fusion.2.where_ref
  138.2 19.6 %all-to-all-done.2.x_ref = bf16[8,2,24,1792]{3,2,1,0:T(8,128)(2,1)S(1)} async-done(((bf16[8,2,24,1792]{3,2,1,0:T(8,128)(2,1)}), bf16[8,2,24,1792]{3,2,1,0:T(8,128)(2,1)S(1)}, u32[]{:S(2)}, u32[]{:S(2)}) %all-to-all-start.2) | async-done | bytes 1376288 | tf_op jit(solution)/shard_map/all_to_all | solution.py:382
  157.9 1.1 copy-done.4
  159.0 2.2 %total_parts.1 = (bf16[12,1792]{1,0:T(8,128)(2,1)}, bf16[12,1792]{1,0:T(8,128)(2,1)}, bf16[12,1792]{1,0:T(8,128)(2,1)}, bf16[12,1792]{1,0:T(8,128)(2,1)}) custom-call(s32[2]{0:T(128)} %pad_add_fusion.2.where_ref, bf16[8,2,24,1792]{3,2,1,0:T(8,128)(2,1)} %copy-done.4), custom_call_target="tpu_custom_call" | custom-call | tf_op jit(solution)/shard_map/total_parts/pallas_call | solution.py:269
  161.2 1.6 collective-permute-start.18
  162.8 0.3 collective-permute-start.19
  163.1 1.3 collective-permute-start.20
  164.5 2.1 %collective-permute-done.19.y_ref = bf16[12,1792]{1,0:T(8,128)(2,1)S(1)} collective-permute-done((bf16[12,1792]{1,0:T(8,128)(2,1)}, bf16[12,1792]{1,0:T(8,128)(2,1)S(1)}, u32[]{:S(2)}, u32[]{:S(2)}) %collective-permute-start.19) | collective-permute-done | bytes 43040 | tf_op jit(solution)/shard_map/ppermute | solution.py:27
  166.6 1.3 collective-permute-done.20.both_ref
  167.9 0.6 copy-done.15
  168.5 1.7 arrange.1
  (64 shorter events, 0.3 us)
Async XLA Ops:
  6.5 17.7 %copy-start.5 = (bf16[1024,448]{0,1:T(8,128)(2,1)S(1)}, bf16[1024,448]{0,1:T(8,128)(2,1)}, u32[]{:S(2)}) copy-start(bf16[1024,448]{0,1:T(8,128)(2,1)} %param.19) | copy-start | bytes 2752516
  9.8 15.6 %copy-start.16 = (bf16[1,12,512]{2,1,0:T(8,128)(2,1)S(1)}, bf16[1,12,512]{2,1,0:T(8,128)(2,1)}, u32[]{:S(2)}) copy-start(bf16[1,12,512]{2,1,0:T(8,128)(2,1)} %span_ref.1) | copy-start | bytes 36868
  9.8 18.7 %copy-start.18 = (bf16[1,12,64]{2,1,0:T(8,128)(2,1)S(1)}, bf16[1,12,64]{2,1,0:T(8,128)(2,1)}, u32[]{:S(2)}) copy-start(bf16[1,12,64]{2,1,0:T(8,128)(2,1)} %span_rope_ref.1) | copy-start | bytes 4612
  12.1 29.5 %all-to-all-start = ((bf16[32,72,128]{2,1,0:T(8,128)(2,1)}), bf16[32,72,128]{2,1,0:T(8,128)(2,1)S(1)}, u32[]{:S(2)}, u32[]{:S(2)}) async-start(bf16[32,72,128]{2,1,0:T(8,128)(2,1)} %pack.1), calls=%async_computation | async-start | bytes 1179648 | tf_op jit(solution)/shard_map/all_to_all | solution.py:334
  24.2 99.9 %all-gather.3.cloned.1.call-start = ((), (), s32[]{:S(2)}) async-start(), calls=%async_computation.3 | async-start | bytes 8257536 | tf_op jit(solution)/shard_map/all_gather | solution.py:342
  24.3 11.1 %collective-permute-start.2 = (bf16[224,1024]{1,0:T(8,128)(2,1)S(1)}, bf16[224,1024]{1,0:T(8,128)(2,1)S(1)}, u32[]{:S(2)}, u32[]{:S(2)}) collective-permute-start(bf16[224,1024]{1,0:T(8,128)(2,1)S(1)} %get-tuple-element.26), channel_id=1, source_target_pairs={{0,1},{1,0},{2,3},{3,2},{4,5},{5,4},{6,7},{7,6},{8,9},{9,8},{10,11... | collective-permute-start | bytes 1376264 | tf_op jit(solution)/shard_map/ppermute | solution.py:27
  25.4 7.5 %collective-permute-start = (bf16[1,12,512]{2,1,0:T(8,128)(2,1)S(1)}, bf16[1,12,512]{2,1,0:T(8,128)(2,1)S(1)}, u32[]{:S(2)}, u32[]{:S(2)}) collective-permute-start(bf16[1,12,512]{2,1,0:T(8,128)(2,1)S(1)} %copy-done.16), channel_id=1, source_target_pairs={{0,2},{2,0},{1,3},{3,1},{4,6},{6,4},{5,7},{7,5},{8,10},{10,8},{9,1... | collective-permute-start | bytes 36872 | tf_op jit(solution)/shard_map/ppermute | solution.py:27
  28.4 4.4 %collective-permute-start.1 = (bf16[1,12,64]{2,1,0:T(8,128)(2,1)S(1)}, bf16[1,12,64]{2,1,0:T(8,128)(2,1)S(1)}, u32[]{:S(2)}, u32[]{:S(2)}) collective-permute-start(bf16[1,12,64]{2,1,0:T(8,128)(2,1)S(1)} %copy-done.18), channel_id=1, source_target_pairs={{0,2},{2,0},{1,3},{3,1},{4,6},{6,4},{5,7},{7,5},{8,10},{10,8},{9,1... | collective-permute-start | bytes 4616 | tf_op jit(solution)/shard_map/ppermute | solution.py:27
  32.8 0.6 copy-start.19
  33.4 0.6 copy-start.17
  35.5 6.3 %copy-start.12 = (bf16[2,72,128]{2,1,0:T(8,128)(2,1)S(1)}, bf16[2,72,128]{2,1,0:T(8,128)(2,1)}, u32[]{:S(2)}) copy-start(bf16[2,72,128]{2,1,0:T(8,128)(2,1)} %pack_fresh.1) | copy-start | bytes 110596
  35.5 9.1 %copy-start.20 = (s32[16]{0:T(128)S(1)}, s32[16]{0:T(128)}, u32[]{:S(2)}) copy-start(s32[16]{0:T(128)} %param.17) | copy-start | bytes 196
  35.5 9.7 %copy-start.21 = (s32[16]{0:T(128)S(1)}, s32[16]{0:T(128)}, u32[]{:S(2)}) copy-start(s32[16]{0:T(128)} %param.16) | copy-start | bytes 196
  41.8 14.5 %collective-permute-start.3 = (bf16[34,72,128]{2,1,0:T(8,128)(2,1)S(1)}, bf16[34,72,128]{2,1,0:T(8,128)(2,1)S(1)}, u32[]{:S(2)}, u32[]{:S(2)}) collective-permute-start(bf16[34,72,128]{2,1,0:T(8,128)(2,1)S(1)} %constant_dynamic-update-slice_fusion.rest_0_), channel_id=1, source_target_pairs={{0,4},{4,8},{8,12},{12,0},{1,5},{5,9},{9,13},{13,1},{2,6},{6,10},{... | collective-permute-start | bytes 1880072 | tf_op jit(solution)/shard_map/ppermute | solution.py:27
  43.1 14.0 %collective-permute-start.4 = (bf16[34,72,128]{2,1,0:T(8,128)(2,1)S(1)}, bf16[34,72,128]{2,1,0:T(8,128)(2,1)S(1)}, u32[]{:S(2)}, u32[]{:S(2)}) collective-permute-start(bf16[34,72,128]{2,1,0:T(8,128)(2,1)S(1)} %constant_dynamic-update-slice_fusion.rest_0_), channel_id=1, source_target_pairs={{0,12},{4,0},{8,4},{12,8},{1,13},{5,1},{9,5},{13,9},{2,14},{6,2},{... | collective-permute-start | bytes 1880072 | tf_op jit(solution)/shard_map/ppermute | solution.py:27
  46.4 39.0 %collective-permute-start.7 = (bf16[34,72,128]{2,1,0:T(8,128)(2,1)S(1)}, bf16[34,72,128]{2,1,0:T(8,128)(2,1)S(1)}, u32[]{:S(2)}, u32[]{:S(2)}) collective-permute-start(bf16[34,72,128]{2,1,0:T(8,128)(2,1)S(1)} %constant_dynamic-update-slice_fusion.rest_0_), channel_id=1, source_target_pairs={{0,1},{1,0},{2,3},{3,2},{4,5},{5,4},{6,7},{7,6},{8,9},{9,8},{10,11... | collective-permute-start | bytes 1880072 | tf_op jit(solution)/shard_map/ppermute | solution.py:27
  57.1 13.3 %collective-permute-start.5 = (bf16[17,72,128]{2,1,0:T(8,128)(2,1)}, bf16[17,72,128]{2,1,0:T(8,128)(2,1)S(1)}, u32[]{:S(2)}, u32[]{:S(2)}) collective-permute-start(bf16[17,72,128]{2,1,0:T(8,128)(2,1)} %slice.8), channel_id=1, source_target_pairs={{0,4},{4,8},{8,12},{12,0},{1,5},{5,9},{9,13},{13,1},{2,6},{6,10},{... | collective-permute-start | bytes 940040 | tf_op jit(solution)/shard_map/ppermute | solution.py:27
  57.8 12.9 %collective-permute-start.6 = (bf16[17,72,128]{2,1,0:T(8,128)(2,1)}, bf16[17,72,128]{2,1,0:T(8,128)(2,1)}, u32[]{:S(2)}, u32[]{:S(2)}) collective-permute-start(bf16[17,72,128]{2,1,0:T(8,128)(2,1)} %slice.9), channel_id=1, source_target_pairs={{0,12},{4,0},{8,4},{12,8},{1,13},{5,1},{9,5},{13,9},{2,14},{6,2},{... | collective-permute-start | bytes 940040 | tf_op jit(solution)/shard_map/ppermute | solution.py:27
  60.5 24.9 %collective-permute-start.8 = (bf16[34,72,128]{2,1,0:T(8,128)(2,1)S(1)}, bf16[34,72,128]{2,1,0:T(8,128)(2,1)S(1)}, u32[]{:S(2)}, u32[]{:S(2)}) collective-permute-start(bf16[34,72,128]{2,1,0:T(8,128)(2,1)S(1)} %collective-permute-done.3.rest_1_), channel_id=1, source_target_pairs={{0,1},{1,0},{2,3},{3,2},{4,5},{5,4},{6,7},{7,6},{8,9},{9,8},{10,11... | collective-permute-start | bytes 1880072 | tf_op jit(solution)/shard_map/ppermute | solution.py:27
  64.3 21.1 %collective-permute-start.9 = (bf16[34,72,128]{2,1,0:T(8,128)(2,1)S(1)}, bf16[34,72,128]{2,1,0:T(8,128)(2,1)}, u32[]{:S(2)}, u32[]{:S(2)}) collective-permute-start(bf16[34,72,128]{2,1,0:T(8,128)(2,1)S(1)} %collective-permute-done.4.rest_2_), channel_id=1, source_target_pairs={{0,1},{1,0},{2,3},{3,2},{4,5},{5,4},{6,7},{7,6},{8,9},{9,8},{10,11... | collective-permute-start | bytes 1880072 | tf_op jit(solution)/shard_map/ppermute | solution.py:27
  64.4 18.9 %all-to-all-start.1 = ((bf16[16,12,1536]{2,1,0:T(8,128)(2,1)}), bf16[16,12,1536]{2,1,0:T(8,128)(2,1)}, u32[]{:S(2)}, u32[]{:S(2)}) async-start(bf16[16,12,1536]{2,1,0:T(8,128)(2,1)} %split_queries.1), calls=%async_computation.1 | async-start | bytes 1572864 | tf_op jit(solution)/shard_map/all_to_all | solution.py:347
  70.4 15.0 %collective-permute-start.10 = (bf16[17,72,128]{2,1,0:T(8,128)(2,1)S(1)}, bf16[17,72,128]{2,1,0:T(8,128)(2,1)}, u32[]{:S(2)}, u32[]{:S(2)}) collective-permute-start(bf16[17,72,128]{2,1,0:T(8,128)(2,1)S(1)} %collective-permute-done.5.rest_3_), channel_id=1, source_target_pairs={{0,1},{1,0},{2,3},{3,2},{4,5},{5,4},{6,7},{7,6},{8,9},{9,8},{10,11... | collective-permute-start | bytes 940040 | tf_op jit(solution)/shard_map/ppermute | solution.py:27
  70.7 14.7 %collective-permute-start.11 = (bf16[17,72,128]{2,1,0:T(8,128)(2,1)}, bf16[17,72,128]{2,1,0:T(8,128)(2,1)}, u32[]{:S(2)}, u32[]{:S(2)}) collective-permute-start(bf16[17,72,128]{2,1,0:T(8,128)(2,1)} %collective-permute-done.6.rest_4_), channel_id=1, source_target_pairs={{0,1},{1,0},{2,3},{3,2},{4,5},{5,4},{6,7},{7,6},{8,9},{9,8},{10,11... | collective-permute-start | bytes 940040 | tf_op jit(solution)/shard_map/ppermute | solution.py:27
  85.4 5.7 %copy-start = (bf16[192,1536]{1,0:T(8,128)(2,1)S(1)}, bf16[192,1536]{1,0:T(8,128)(2,1)}, u32[]{:S(2)}) copy-start(bf16[192,1536]{1,0:T(8,128)(2,1)} %reshape.118.q_ref) | copy-start | bytes 1769476
  85.4 5.7 %copy-start.3 = (bf16[512,2048]{1,0:T(8,128)(2,1)S(1)}, bf16[512,2048]{1,0:T(8,128)(2,1)}, u32[]{:S(2)}) copy-start(bf16[512,2048]{1,0:T(8,128)(2,1)} %up_ref.3) | copy-start | bytes 6291460
  98.9 9.5 %copy-start.1 = (bf16[192,512]{1,0:T(8,128)(2,1)}, bf16[192,512]{1,0:T(8,128)(2,1)S(1)}, u32[]{:S(2)}) copy-start(bf16[192,512]{1,0:T(8,128)(2,1)S(1)} %attend.2.refs_0_) | copy-start | bytes 589828
  98.9 11.1 %collective-permute-start.12 = (bf16[192,512]{1,0:T(8,128)(2,1)S(1)}, bf16[192,512]{1,0:T(8,128)(2,1)S(1)}, u32[]{:S(2)}, u32[]{:S(2)}) collective-permute-start(bf16[192,512]{1,0:T(8,128)(2,1)S(1)} %attend.2.refs_0_), channel_id=1, source_target_pairs={{0,16},{16,0},{1,17},{17,1},{2,18},{18,2},{3,19},{19,3},{4,20},{20... | collective-permute-start | bytes 589832 | tf_op jit(solution)/shard_map/ppermute | solution.py:27
  107.7 16.4 %copy-start.2 = (bf16[192,512]{1,0:T(8,128)(2,1)}, bf16[192,512]{1,0:T(8,128)(2,1)S(1)}, u32[]{:S(2)}) copy-start(bf16[192,512]{1,0:T(8,128)(2,1)S(1)} %attend.3.refs_1_) | copy-start | bytes 589828
  107.7 5.2 %collective-permute-start.13 = (bf16[192,512]{1,0:T(8,128)(2,1)S(1)}, bf16[192,512]{1,0:T(8,128)(2,1)S(1)}, u32[]{:S(2)}, u32[]{:S(2)}) collective-permute-start(bf16[192,512]{1,0:T(8,128)(2,1)S(1)} %attend.3.refs_1_), channel_id=1, source_target_pairs={{0,16},{16,0},{1,17},{17,1},{2,18},{18,2},{3,19},{19,3},{4,20},{20... | collective-permute-start | bytes 589832 | tf_op jit(solution)/shard_map/ppermute | solution.py:27
  108.4 6.7 %collective-permute-start.14 = (bf16[192,512]{1,0:T(8,128)(2,1)S(1)}, bf16[192,512]{1,0:T(8,128)(2,1)S(1)}, u32[]{:S(2)}, u32[]{:S(2)}) collective-permute-start(bf16[192,512]{1,0:T(8,128)(2,1)S(1)} %attend.2.refs_0_), channel_id=1, source_target_pairs={{0,1},{1,0},{2,3},{3,2},{4,5},{5,4},{6,7},{7,6},{8,9},{9,8},{10,11... | collective-permute-start | bytes 589832 | tf_op jit(solution)/shard_map/ppermute | solution.py:27
  110.1 5.1 %collective-permute-start.15 = (bf16[192,512]{1,0:T(8,128)(2,1)S(1)}, bf16[192,512]{1,0:T(8,128)(2,1)S(1)}, u32[]{:S(2)}, u32[]{:S(2)}) collective-permute-start(bf16[192,512]{1,0:T(8,128)(2,1)S(1)} %attend.3.refs_1_), channel_id=1, source_target_pairs={{0,1},{1,0},{2,3},{3,2},{4,5},{5,4},{6,7},{7,6},{8,9},{9,8},{10,11... | collective-permute-start | bytes 589832 | tf_op jit(solution)/shard_map/ppermute | solution.py:27
  110.1 14.0 %copy-start.6 = (bf16[192,512]{1,0:T(8,128)(2,1)}, bf16[192,512]{1,0:T(8,128)(2,1)S(1)}, u32[]{:S(2)}) copy-start(bf16[192,512]{1,0:T(8,128)(2,1)S(1)} %collective-permute-done.12.refs_2_) | copy-start | bytes 589828
  110.1 5.1 %collective-permute-start.16 = (bf16[192,512]{1,0:T(8,128)(2,1)S(1)}, bf16[192,512]{1,0:T(8,128)(2,1)S(1)}, u32[]{:S(2)}, u32[]{:S(2)}) collective-permute-start(bf16[192,512]{1,0:T(8,128)(2,1)S(1)} %collective-permute-done.12.refs_2_), channel_id=1, source_target_pairs={{0,1},{1,0},{2,3},{3,2},{4,5},{5,4},{6,7},{7,6},{8,9},{9,8},{10,11... | collective-permute-start | bytes 589832 | tf_op jit(solution)/shard_map/ppermute | solution.py:27
  113.0 11.1 %copy-start.7 = (bf16[192,512]{1,0:T(8,128)(2,1)}, bf16[192,512]{1,0:T(8,128)(2,1)S(1)}, u32[]{:S(2)}) copy-start(bf16[192,512]{1,0:T(8,128)(2,1)S(1)} %collective-permute-done.13.refs_3_) | copy-start | bytes 589828
  113.0 3.3 %collective-permute-start.17 = (bf16[192,512]{1,0:T(8,128)(2,1)S(1)}, bf16[192,512]{1,0:T(8,128)(2,1)S(1)}, u32[]{:S(2)}, u32[]{:S(2)}) collective-permute-start(bf16[192,512]{1,0:T(8,128)(2,1)S(1)} %collective-permute-done.13.refs_3_), channel_id=1, source_target_pairs={{0,1},{1,0},{2,3},{3,2},{4,5},{5,4},{6,7},{7,6},{8,9},{9,8},{10,11... | collective-permute-start | bytes 589832 | tf_op jit(solution)/shard_map/ppermute | solution.py:27
  115.2 8.9 %copy-start.8 = (bf16[192,512]{1,0:T(8,128)(2,1)}, bf16[192,512]{1,0:T(8,128)(2,1)S(1)}, u32[]{:S(2)}) copy-start(bf16[192,512]{1,0:T(8,128)(2,1)S(1)} %collective-permute-done.14.refs_4_) | copy-start | bytes 589828
  115.2 8.9 %copy-start.9 = (bf16[192,512]{1,0:T(8,128)(2,1)}, bf16[192,512]{1,0:T(8,128)(2,1)S(1)}, u32[]{:S(2)}) copy-start(bf16[192,512]{1,0:T(8,128)(2,1)S(1)} %collective-permute-done.15.refs_5_) | copy-start | bytes 589828
  115.2 8.9 %copy-start.10 = (bf16[192,512]{1,0:T(8,128)(2,1)}, bf16[192,512]{1,0:T(8,128)(2,1)S(1)}, u32[]{:S(2)}) copy-start(bf16[192,512]{1,0:T(8,128)(2,1)S(1)} %collective-permute-done.16.refs_6_) | copy-start | bytes 589828
  116.2 7.9 %copy-start.11 = (bf16[192,512]{1,0:T(8,128)(2,1)}, bf16[192,512]{1,0:T(8,128)(2,1)S(1)}, u32[]{:S(2)}) copy-start(bf16[192,512]{1,0:T(8,128)(2,1)S(1)} %collective-permute-done.17.refs_7_) | copy-start | bytes 589828
  131.2 26.7 %all-to-all-start.2 = ((bf16[8,2,24,1792]{3,2,1,0:T(8,128)(2,1)}), bf16[8,2,24,1792]{3,2,1,0:T(8,128)(2,1)S(1)}, u32[]{:S(2)}, u32[]{:S(2)}) async-start(bf16[8,2,24,1792]{3,2,1,0:T(8,128)(2,1)} %project.1), calls=%async_computation.2 | async-start | bytes 2752512 | tf_op jit(solution)/shard_map/all_to_all | solution.py:382
  157.9 1.1 copy-start.4
  161.2 3.3 %collective-permute-start.18 = (bf16[12,1792]{1,0:T(8,128)(2,1)}, bf16[12,1792]{1,0:T(8,128)(2,1)S(1)}, u32[]{:S(2)}, u32[]{:S(2)}) collective-permute-start(bf16[12,1792]{1,0:T(8,128)(2,1)} %get-tuple-element.18), channel_id=1, source_target_pairs={{0,1},{1,0},{2,3},{3,2},{4,5},{5,4},{6,7},{7,6},{8,9},{9,8},{10,11... | collective-permute-start | bytes 129032 | tf_op jit(solution)/shard_map/ppermute | solution.py:27
  162.8 3.8 %collective-permute-start.19 = (bf16[12,1792]{1,0:T(8,128)(2,1)}, bf16[12,1792]{1,0:T(8,128)(2,1)S(1)}, u32[]{:S(2)}, u32[]{:S(2)}) collective-permute-start(bf16[12,1792]{1,0:T(8,128)(2,1)} %get-tuple-element.19), channel_id=1, source_target_pairs={{0,16},{16,0},{1,17},{17,1},{2,18},{18,2},{3,19},{19,3},{4,20},{20... | collective-permute-start | bytes 129032 | tf_op jit(solution)/shard_map/ppermute | solution.py:27
  163.1 4.8 %collective-permute-start.20 = (bf16[12,1792]{1,0:T(8,128)(2,1)}, bf16[12,1792]{1,0:T(8,128)(2,1)S(1)}, u32[]{:S(2)}, u32[]{:S(2)}) collective-permute-start(bf16[12,1792]{1,0:T(8,128)(2,1)} %get-tuple-element.20), channel_id=1, source_target_pairs={{0,17},{1,16},{16,1},{17,0},{2,19},{3,18},{18,3},{19,2},{4,21},{5,... | collective-permute-start | bytes 129032 | tf_op jit(solution)/shard_map/ppermute | solution.py:385
  164.5 3.4 %copy-start.13 = (bf16[12,1792]{1,0:T(8,128)(2,1)}, bf16[12,1792]{1,0:T(8,128)(2,1)S(1)}, u32[]{:S(2)}) copy-start(bf16[12,1792]{1,0:T(8,128)(2,1)S(1)} %collective-permute-done.18.c_ref) | copy-start | bytes 129028
  166.6 1.3 copy-start.14
  167.9 0.6 copy-start.15
Sparse Core Ops, SparseCore 0:
  41.8 82.2 all-gather.2

commit v4 on v3

--- a/solution.py
+++ b/solution.py
@@ -62,9 +62,8 @@
         second = slot_ref[2 * dest + 1]
         tiles = jnp.concatenate([tiles_of(pool_ref[first]), tiles_of(pool_ref[second])], 0)
         rope = jnp.concatenate([rope_ref[first], rope_ref[second]], 1)
-        for copy in range(2):
-            o_ref[2 * dest + copy, :64] = tiles
-            o_ref[2 * dest + copy, 64:] = rope
+        o_ref[dest, :64] = tiles
+        o_ref[dest, 64:] = rope
         return carry
 
     lax.fori_loop(0, 16, one, 0, unroll=2)
@@ -76,7 +75,7 @@
         pack_body,
         in_specs=[pl.BlockSpec(memory_space=pltpu.SMEM), vmem, vmem],
         out_specs=vmem,
-        out_shape=jax.ShapeDtypeStruct((32, 72, 128), BF),
+        out_shape=jax.ShapeDtypeStruct((16, 72, 128), BF),
         name="pack",
     )(slots, pool, rope)
 
@@ -255,26 +254,6 @@
     )(*parts, weight)
 
 
-def total_body(where_ref, x_ref, *outs):
-    core = where_ref[1]
-    for request in range(2):
-        value = jnp.sum(x_ref[:, request].astype(F32), axis=0)
-        low, high = value[:OWN], value[OWN:]
-        outs[2 * request][...] = jnp.where(core == 0, low, high).astype(BF)
-        outs[2 * request + 1][...] = jnp.where(core == 0, high, low).astype(BF)
-
-
-def total_parts(where, shared):
-    vmem = pl.BlockSpec(memory_space=pltpu.VMEM)
-    return pl.pallas_call(
-        total_body,
-        in_specs=[pl.BlockSpec(memory_space=pltpu.SMEM), vmem],
-        out_specs=[vmem] * 4,
-        out_shape=[jax.ShapeDtypeStruct((OWN, 1792), BF)] * 4,
-        name="total_parts",
-    )(where, shared)
-
-
 def arrange_body(where_ref, here_ref, c_ref, y_ref, both_ref, o_ref):
     yl, core = where_ref[0], where_ref[1]
     here, mate, near, far = (r[...].astype(F32) for r in (here_ref, c_ref, y_ref, both_ref))
@@ -331,21 +310,26 @@
     high = jnp.max(jnp.where(owned, marked, 0), axis=1)
     picked = jnp.stack([low % slots, high % slots], 1).reshape(32)
     sent_pages = pack(picked, pool_latent, pool_rope.reshape(slots, PAGE, ROPE))
-    back = lax.all_to_all(sent_pages, ("z", "yl", "yh"), split_axis=0, concat_axis=0, tiled=True)
+    back = lax.all_to_all(sent_pages, ("z", "yl"), split_axis=0, concat_axis=0, tiled=True)
     fresh = pack_fresh(span_latent, span_rope, pair_latent, pair_rope)
     sent = split_queries(queries[0])
+    lens = jnp.stack(
+        [
+            lax.dynamic_index_in_dim(cache_len, group, 0, keepdims=False),
+            lax.dynamic_index_in_dim(span_len, group, 0, keepdims=False),
+        ]
+    )
     turned = out_weight.T
     kept = lax.dynamic_slice_in_dim(turned, ci * 224, 224, 0)
     given = lax.dynamic_slice_in_dim(turned, (1 - ci) * 224, 224, 0)
     columns = jnp.concatenate([kept, swap_c(given)], 0)
-    back, fresh, sent, columns = lax.optimization_barrier((back, fresh, sent, columns))
+    back, fresh, sent, lens, columns = lax.optimization_barrier((back, fresh, sent, lens, columns))
     weight = lax.all_gather(columns, "z", axis=0, tiled=False)
-    mine = jnp.concatenate([back, fresh], 0)
+    mine = jnp.concatenate([back, swap_yh(back), fresh], 0)
     half = PIECE // 2
     left = step("x", 4, 1)(mine)
     right = step("x", 4, -1)(mine)
     exchanged = lax.all_to_all(sent, ("x", "yh", "c"), split_axis=0, concat_axis=0, tiled=True)
-    q = exchanged.reshape(SPAN, HEADS_HERE * QHEAD)
     mine_c = swap_c(mine)
     far_a = step("x", 4, 1)(left[:half])
     far_b = step("x", 4, -1)(right[half:])
@@ -364,24 +348,23 @@
         number = jnp.where(apart == 0, 0, jnp.where(apart == 3, 1, jnp.where(apart == 1, 2, 3)))
         return (jnp.where(of_member % 2 == ci, 0, 4) + number) * PIECE
 
-    block = piece_index(from_member) + from_group * 2 + (from_member // 2) % 2
+    block = piece_index(from_member) + from_group + jnp.where((from_member // 2) % 2 == yh, 0, 16)
     members = jnp.arange(32, dtype=jnp.int32) // 2
     block_new = piece_index(members) + 32 + jnp.where((members // 2) % 2 == yh, 0, 1)
     index = jnp.concatenate([block * 2 + place, block_new * 2 + jnp.arange(32, dtype=jnp.int32) % 2])
 
-    lens = jnp.stack(
-        [
-            lax.dynamic_index_in_dim(cache_len, group, 0, keepdims=False),
-            lax.dynamic_index_in_dim(span_len, group, 0, keepdims=False),
-        ]
-    )
     keys = assemble(index, pieces)
+    exchanged, keys = lax.optimization_barrier((exchanged, keys))
+    q = exchanged.reshape(SPAN, HEADS_HERE * QHEAD)
     own = [attend(half, lens, q, kv_up, keys) for half in range(2)]
     near = [swap_yl(x) for x in own]
     partial = project([*own, *near, *[swap_c(x) for x in own], *[swap_c(x) for x in near]], weight)
     shared = lax.all_to_all(partial, ("x", "yh"), split_axis=0, concat_axis=0, tiled=True)
     where = jnp.stack([yl, ci]).astype(jnp.int32)
-    here, to_c, to_yl, to_both = total_parts(where, shared)
+    summed = jnp.sum(shared.astype(F32), axis=0).astype(BF).reshape(2, 2, OWN, 1792)
+    own_rows = lax.dynamic_index_in_dim(summed, ci, 1, keepdims=False)
+    mate_rows = lax.dynamic_index_in_dim(summed, 1 - ci, 1, keepdims=False)
+    here, to_c, to_yl, to_both = own_rows[0], mate_rows[0], own_rows[1], mate_rows[1]
     from_both = lax.ppermute(to_both, ("yl", "c"), [(i, 3 - i) for i in range(4)])
     out = arrange(where, here, swap_c(to_c), swap_yl(to_yl), from_both)
     return out[None]

time: 178 us -> 171 us (0.961)
  waiting for transfers between devices: 60.7 us -> 48 us
  local copies, waits for them, and re-layouts: 10.1 us -> 18.5 us
  Pallas kernels: 38.2 us -> 35.5 us
    all_to_all x1, waiting for transfers between devices: 12.2 us -> 0.09 us  [shards(): lax.all_to_all(sent, ('x', 'yh', 'c'), split_axis=0, concat_axis=0, tiled...]
    unnamed x45 -> x68, local copies, waits for them, and re-layouts: 3.04 us -> 11.3 us
    ppermute x20 -> x21, starting transfers between devices: 25.1 us -> 30.7 us  [send(): lax.ppermute(value, axis, [(i, (i + by) % count) for i in range(count)])]
    all_to_all x1, waiting for transfers between devices: 5.13 us -> 0.63 us  [shards(): lax.all_to_all(sent_pages, ('z', 'yl'), split_axis=0, concat_axis=0, tile...]
    all_to_all x1, starting transfers between devices: 12 us -> 7.57 us  [shards(): lax.all_to_all(sent_pages, ('z', 'yl'), split_axis=0, concat_axis=0, tile...]
    ppermute x20 -> x21, waiting for transfers between devices: 14.6 us -> 18.6 us  [send(): lax.ppermute(value, axis, [(i, (i + by) % count) for i in range(count)])]
    pallas_call x1 -> x0, Pallas kernels: 2.2 us -> none  [total_parts(): pl.pallas_call(total_body, in_specs=[pl.BlockSpec(memory_space=pltpu.SMEM...]
  transfers between devices with their start and end apart: 25 -> 26, of which waited for: 10 -> 12; matrix products, arithmetic and copies ran while one was open for 5% -> 6% of each run, Pallas kernels for 14% -> 16%
where the time goes in v4:
time: 171 us; the launch traced here: 170 us
  starting transfers between devices  50.9 us (30%)
  waiting for transfers between devices  48 us (28%)
  Pallas kernels  35.5 us (21%)
  local copies, waits for them, and re-layouts  18.5 us (11%)
  between operations  13.7 us (8%)
  other arithmetic  3.66 us (2%)
    ppermute x21, starting transfers between devices, send(): lax.ppermute(value, axis, [(i, (i + by) % count) for i in range(count)])  30.7 us
    all_to_all x1, waiting for transfers between devices, shards(): lax.all_to_all(partial, ('x', 'yh'), split_axis=0, concat_axis=0, tiled=T...  20.2 us
    ppermute x21, waiting for transfers between devices, send(): lax.ppermute(value, axis, [(i, (i + by) % count) for i in range(count)])  18.6 us
    pallas_call x2, Pallas kernels, attend(): pl.pallas_call(attend_body, grid_spec=pltpu.PrefetchScalarGridSpec(num_sc...  15.7 us
    unnamed x68, local copies, waits for them, and re-layouts  11.3 us
    all_to_all x1, starting transfers between devices, shards(): lax.all_to_all(sent_pages, ('z', 'yl'), split_axis=0, concat_axis=0, tile...  7.57 us
    all_gather x1, waiting for transfers between devices, shards(): weight = lax.all_gather(columns, 'z', axis=0, tiled=False)  7.1 us
    pallas_call x1, Pallas kernels, project(): pl.pallas_call(project_body, grid=(2,), in_specs=[pl.BlockSpec((SPAN, 512...  7.05 us
  transfers between devices with their start and end apart: 26, of which 12 were waited for; matrix products, arithmetic and copies ran while one was open for 6% of the time, Pallas kernels for 16%

profile of v4, /device:TPU:1, one launch (start us, length us, event | category | flops | bytes accessed | tf_op | source)
XLA Modules:
  0.0 170.4 jit_solution(9611938148785608630)
XLA Ops:
  6.6 1.3 dynamic-slice_bitcast_fusion.1
  7.8 3.3 %collective-permute-start.2 = (bf16[224,1024]{1,0:T(8,128)(2,1)S(1)}, bf16[224,1024]{1,0:T(8,128)(2,1)S(1)}, u32[]{:S(2)}, u32[]{:S(2)}) collective-permute-start(bf16[224,1024]{1,0:T(8,128)(2,1)S(1)} %get-tuple-element.24), channel_id=1, source_target_pairs={{0,1},{1,0},{2,3},{3,2},{4,5},{5,4},{6,7},{7,6},{8,9},{9,8},{10,11... | collective-permute-start | bytes 1376264 | tf_op jit(solution)/shard_map/ppermute | solution.py:27
  11.4 0.6 reshape.127.slot_ref
  12.1 0.7 reshape.128.rope_ref
  12.8 2.2 %pack.1 = bf16[16,72,128]{2,1,0:T(8,128)(2,1)} custom-call(s32[32]{0:T(128)} %reshape.127.slot_ref, bf16[32,8,512]{2,1,0:T(8,128)(2,1)} %pool_ref.1, bf16[32,8,64]{2,1,0:T(8,128)(2,1)} %reshape.128.rope_ref), custom_call_target="tpu_custom_call" | custom-call | tf_op jit(solution)/shard_map/pack/pallas_call | solution.py:74
  15.0 7.6 %all-to-all-start = ((bf16[16,72,128]{2,1,0:T(8,128)(2,1)}), bf16[16,72,128]{2,1,0:T(8,128)(2,1)S(1)}, u32[]{:S(2)}, u32[]{:S(2)}) async-start(bf16[16,72,128]{2,1,0:T(8,128)(2,1)} %pack.1), calls=%async_computation | async-start | bytes 589824 | tf_op jit(solution)/shard_map/all_to_all | solution.py:313
  22.7 2.7 %collective-permute-start = (bf16[1,12,512]{2,1,0:T(8,128)(2,1)S(1)}, bf16[1,12,512]{2,1,0:T(8,128)(2,1)S(1)}, u32[]{:S(2)}, u32[]{:S(2)}) collective-permute-start(bf16[1,12,512]{2,1,0:T(8,128)(2,1)S(1)} %copy-done.25), channel_id=1, source_target_pairs={{0,2},{2,0},{1,3},{3,1},{4,6},{6,4},{5,7},{7,5},{8,10},{10,8},{9,1... | collective-permute-start | bytes 36872 | tf_op jit(solution)/shard_map/ppermute | solution.py:27
  25.4 0.3 collective-permute-start.1
  25.7 0.6 dynamic_slice.24
  26.4 0.6 dynamic_slice.25
  26.9 1.3 pad_add_fusion.3.lens_ref
  28.3 2.1 %split_queries.1 = bf16[16,12,1536]{2,1,0:T(8,128)(2,1)} custom-call(bf16[12,24576]{1,0:T(8,128)(2,1)} %bitcast.30), custom_call_target="tpu_custom_call" | custom-call | tf_op jit(solution)/shard_map/split_queries/pallas_call | solution.py:39
  30.3 0.6 copy-done.28
  30.9 0.6 copy-done.26
  31.5 1.4 pack_fresh.1
  33.0 1.0 pad_maximum_fusion
  34.0 0.6 all-to-all-done
  34.7 2.7 %collective-permute-start.3 = (bf16[16,72,128]{2,1,0:T(8,128)(2,1)S(1)}, bf16[16,72,128]{2,1,0:T(8,128)(2,1)S(1)}, u32[]{:S(2)}, u32[]{:S(2)}) collective-permute-start(bf16[16,72,128]{2,1,0:T(8,128)(2,1)S(1)} %all-to-all-done), channel_id=1, source_target_pairs={{0,2},{2,0},{1,3},{3,1},{4,6},{6,4},{5,7},{7,5},{8,10},{10,8},{9,1... | collective-permute-start | bytes 884744 | tf_op jit(solution)/shard_map/ppermute | solution.py:27
  37.4 5.5 %collective-permute-done.3 = bf16[16,72,128]{2,1,0:T(8,128)(2,1)S(1)} collective-permute-done((bf16[16,72,128]{2,1,0:T(8,128)(2,1)S(1)}, bf16[16,72,128]{2,1,0:T(8,128)(2,1)S(1)}, u32[]{:S(2)}, u32[]{:S(2)}) %collective-permute-start.3) | collective-permute-done | bytes 294944 | tf_op jit(solution)/shard_map/ppermute | solution.py:27
  43.0 1.3 collective-permute-start.4
  44.3 1.5 collective-permute-start.5
  45.8 3.4 %collective-permute-start.8 = (bf16[34,72,128]{2,1,0:T(8,128)(2,1)S(1)}, bf16[34,72,128]{2,1,0:T(8,128)(2,1)S(1)}, u32[]{:S(2)}, u32[]{:S(2)}) collective-permute-start(bf16[34,72,128]{2,1,0:T(8,128)(2,1)S(1)} %constant_dynamic-update-slice_fusion.rest_0_), channel_id=1, source_target_pairs={{0,1},{1,0},{2,3},{3,2},{4,5},{5,4},{6,7},{7,6},{8,9},{9,8},{10,11... | collective-permute-start | bytes 1880072 | tf_op jit(solution)/shard_map/ppermute | solution.py:27
  49.2 8.1 %collective-permute-done.4.rest_1_ = bf16[34,72,128]{2,1,0:T(8,128)(2,1)S(1)} collective-permute-done((bf16[34,72,128]{2,1,0:T(8,128)(2,1)S(1)}, bf16[34,72,128]{2,1,0:T(8,128)(2,1)S(1)}, u32[]{:S(2)}, u32[]{:S(2)}) %collective-permute-start.4) | collective-permute-done | bytes 626720 | tf_op jit(solution)/shard_map/ppermute | solution.py:27
  57.3 0.8 slice.28
  58.1 0.8 slice.29
  58.9 2.7 %collective-permute-start.7 = (bf16[17,72,128]{2,1,0:T(8,128)(2,1)}, bf16[17,72,128]{2,1,0:T(8,128)(2,1)}, u32[]{:S(2)}, u32[]{:S(2)}) collective-permute-start(bf16[17,72,128]{2,1,0:T(8,128)(2,1)} %slice.29), channel_id=1, source_target_pairs={{0,12},{4,0},{8,4},{12,8},{1,13},{5,1},{9,5},{13,9},{2,14},{6,2},{... | collective-permute-start | bytes 940040 | tf_op jit(solution)/shard_map/ppermute | solution.py:27
  61.6 4.1 %collective-permute-start.10 = (bf16[34,72,128]{2,1,0:T(8,128)(2,1)S(1)}, bf16[34,72,128]{2,1,0:T(8,128)(2,1)S(1)}, u32[]{:S(2)}, u32[]{:S(2)}) collective-permute-start(bf16[34,72,128]{2,1,0:T(8,128)(2,1)S(1)} %collective-permute-done.5.rest_2_), channel_id=1, source_target_pairs={{0,1},{1,0},{2,3},{3,2},{4,5},{5,4},{6,7},{7,6},{8,9},{9,8},{10,11... | collective-permute-start | bytes 1880072 | tf_op jit(solution)/shard_map/ppermute | solution.py:27
  65.7 4.7 %all-to-all-start.1 = ((bf16[16,12,1536]{2,1,0:T(8,128)(2,1)}), bf16[16,12,1536]{2,1,0:T(8,128)(2,1)}, u32[]{:S(2)}, u32[]{:S(2)}) async-start(bf16[16,12,1536]{2,1,0:T(8,128)(2,1)} %split_queries.1), calls=%async_computation.1 | async-start | bytes 1572864 | tf_op jit(solution)/shard_map/all_to_all | solution.py:332
  70.7 0.2 collective-permute-start.11
  70.9 0.4 collective-permute-start.12
  71.4 0.8 copy-done.6
  72.4 0.7 collective-permute-done.12.rest_9_
  73.1 0.8 copy-done.8
  73.9 1.1 copy-done.1
  75.0 1.1 copy-done.3
  76.1 1.1 copy-done.5
  77.2 1.1 copy-done.7
  78.2 1.1 copy-done.9
  79.3 5.3 %assemble.1.keys = bf16[2304,640]{1,0:T(8,128)(2,1)S(1)} custom-call(s32[288]{0:T(512)S(1)} %pad_add_fusion.index_ref, bf16[34,72,128]{2,1,0:T(8,128)(2,1)S(1)} %copy-done.5, bf16[34,72,128]{2,1,0:T(8,128)(2,1)S(1)} %copy-done.1, bf16[34,72,128]{2,1,0:T(8,128)(2,1)S(1)} %copy-done.3, bf16[17,72,128]{2,1,0:T(8,128)(2,1)S(1)} %collective-permute-done.6.rest_3_, ...), custom_call_target="tpu_custom_call" | custom-call | bytes 16000000 | tf_op jit(solution)/shard_map/assemble/pallas_call | solution.py:140
  84.7 1.3 reshape.129.q_ref
  86.0 1.6 copy-done.12
  87.7 7.8 %attend.3.refs_1_ = bf16[192,512]{1,0:T(8,128)(2,1)S(1)} custom-call(s32[2]{0:T(128)S(1)} %pad_add_fusion.3.lens_ref, bf16[192,1536]{1,0:T(8,128)(2,1)S(1)} %reshape.129.q_ref, bf16[512,2048]{1,0:T(8,128)(2,1)S(1)} %copy-done.12, bf16[2304,640]{1,0:T(8,128)(2,1)S(1)} %assemble.1.keys), custom_call_target="tpu_custom_call" | custom-call | flops 5000000000 | bytes 4000000 | tf_op jit(solution)/shard_map/attend/pallas_call | solution.py:197
  95.5 1.1 collective-permute-start.14
  96.6 7.8 %attend.2.refs_0_ = bf16[192,512]{1,0:T(8,128)(2,1)S(1)} custom-call(s32[2]{0:T(128)S(1)} %pad_add_fusion.3.lens_ref, bf16[192,1536]{1,0:T(8,128)(2,1)S(1)} %reshape.129.q_ref, bf16[512,2048]{1,0:T(8,128)(2,1)S(1)} %copy-done.12, bf16[2304,640]{1,0:T(8,128)(2,1)S(1)} %assemble.1.keys), custom_call_target="tpu_custom_call" | custom-call | flops 5000000000 | bytes 4000000 | tf_op jit(solution)/shard_map/attend/pallas_call | solution.py:197
  104.5 0.5 collective-permute-start.13
  105.0 1.7 collective-permute-start.16
  106.7 0.5 collective-permute-start.18
  107.2 2.6 %collective-permute-done.13.refs_2_ = bf16[192,512]{1,0:T(8,128)(2,1)S(1)} collective-permute-done((bf16[192,512]{1,0:T(8,128)(2,1)S(1)}, bf16[192,512]{1,0:T(8,128)(2,1)S(1)}, u32[]{:S(2)}, u32[]{:S(2)}) %collective-permute-start.13) | collective-permute-done | bytes 196640 | tf_op jit(solution)/shard_map/ppermute | solution.py:27
  109.7 2.2 %collective-permute-start.17 = (bf16[192,512]{1,0:T(8,128)(2,1)S(1)}, bf16[192,512]{1,0:T(8,128)(2,1)S(1)}, u32[]{:S(2)}, u32[]{:S(2)}) collective-permute-start(bf16[192,512]{1,0:T(8,128)(2,1)S(1)} %collective-permute-done.13.refs_2_), channel_id=1, source_target_pairs={{0,1},{1,0},{2,3},{3,2},{4,5},{5,4},{6,7},{7,6},{8,9},{9,8},{10,11... | collective-permute-start | bytes 589832 | tf_op jit(solution)/shard_map/ppermute | solution.py:27
  111.9 1.0 collective-permute-done.17.refs_6_
  113.0 7.1 %all-gather.3.cloned.1.call-done = bf16[3584,1024]{1,0:T(8,128)(2,1)} async-done(((bf16[448,1024]{1,0:T(8,128)(2,1)}), bf16[3584,1024]{1,0:T(8,128)(2,1)}) %all-gather.3.cloned.1.call-update) | async-done | bytes 7340048 | tf_op jit(solution)/shard_map/all_gather | solution.py:327
  120.1 7.0 %project.1 = bf16[8,2,24,1792]{3,2,1,0:T(8,128)(2,1)} custom-call(bf16[192,512]{1,0:T(8,128)(2,1)} %copy-done.11, bf16[192,512]{1,0:T(8,128)(2,1)} %copy-done.10, bf16[192,512]{1,0:T(8,128)(2,1)} %copy-done.14, bf16[192,512]{1,0:T(8,128)(2,1)} %copy-done.13, bf16[192,512]{1,0:T(8,128)(2,1)} %copy-done.16, bf16[192,512]{1,0:T(8,128)(2,1)} %copy-done.15, ...), custom_call_target="tpu_custom_call" | custom-call | tf_op jit(solution)/shard_map/project/pallas_call | solution.py:245
  127.1 6.4 %all-to-all-start.2 = ((bf16[8,2,24,1792]{3,2,1,0:T(8,128)(2,1)}), bf16[8,2,24,1792]{3,2,1,0:T(8,128)(2,1)S(1)}, u32[]{:S(2)}, u32[]{:S(2)}) async-start(bf16[8,2,24,1792]{3,2,1,0:T(8,128)(2,1)} %project.1), calls=%async_computation.2 | async-start | bytes 2752512 | tf_op jit(solution)/shard_map/all_to_all | solution.py:362
  133.6 20.2 %all-to-all-done.2 = bf16[8,2,24,1792]{3,2,1,0:T(8,128)(2,1)S(1)} async-done(((bf16[8,2,24,1792]{3,2,1,0:T(8,128)(2,1)}), bf16[8,2,24,1792]{3,2,1,0:T(8,128)(2,1)S(1)}, u32[]{:S(2)}, u32[]{:S(2)}) %all-to-all-start.2) | async-done | bytes 1376288 | tf_op jit(solution)/shard_map/all_to_all | solution.py:362
  154.1 0.3 constant_dynamic-slice_fusion.2
  154.5 1.7 %collective-permute-start.19 = (bf16[12,1792]{1,0:T(8,128)(2,1)S(1)}, bf16[12,1792]{1,0:T(8,128)(2,1)S(1)}, u32[]{:S(2)}, u32[]{:S(2)}) collective-permute-start(bf16[12,1792]{1,0:T(8,128)(2,1)S(1)} %bitcast.32), channel_id=1, source_target_pairs={{0,1},{1,0},{2,3},{3,2},{4,5},{5,4},{6,7},{7,6},{8,9},{9,8},{10,11... | collective-permute-start | bytes 129032 | tf_op jit(solution)/shard_map/ppermute | solution.py:27
  156.2 0.4 collective-permute-start.20
  156.6 1.4 collective-permute-start.21
  158.0 0.6 pad_add_fusion.2.where_ref
  158.7 0.6 copy.36
  159.3 0.5 collective-permute-done.20.y_ref
  159.8 1.3 collective-permute-done.21.both_ref
  161.2 0.6 copy-done.22
  161.8 1.7 %arrange.1 = bf16[12,7168]{1,0:T(8,128)(2,1)} custom-call(s32[2]{0:T(128)} %pad_add_fusion.2.where_ref, bf16[12,1792]{1,0:T(8,128)(2,1)} %bitcast.31, bf16[12,1792]{1,0:T(8,128)(2,1)} %copy-done.20, bf16[12,1792]{1,0:T(8,128)(2,1)} %copy-done.21, bf16[12,1792]{1,0:T(8,128)(2,1)} %copy-done.22), custom_call_target="tpu_custom_call" | custom-call | tf_op jit(solution)/shard_map/arrange/pallas_call | solution.py:272
  (91 shorter events, 1.5 us)
Async XLA Ops:
  6.5 4.6 %copy-start.24 = (s32[16,256]{1,0:T(8,128)S(1)}, s32[16,256]{1,0:T(8,128)}, u32[]{:S(2)}) copy-start(s32[16,256]{1,0:T(8,128)} %param.15) | copy-start | bytes 49156
  6.5 5.5 %copy-start.23 = (bf16[32,512]{1,0:T(8,128)(2,1)S(1)}, bf16[32,512]{1,0:T(8,128)(2,1)}, u32[]{:S(2)}) copy-start(bf16[32,512]{1,0:T(8,128)(2,1)} %param.14) | copy-start | bytes 98308
  6.5 16.1 %copy-start.25 = (bf16[1,12,512]{2,1,0:T(8,128)(2,1)S(1)}, bf16[1,12,512]{2,1,0:T(8,128)(2,1)}, u32[]{:S(2)}) copy-start(bf16[1,12,512]{2,1,0:T(8,128)(2,1)} %span_ref.1) | copy-start | bytes 36868
  6.5 18.8 %copy-start.27 = (bf16[1,12,64]{2,1,0:T(8,128)(2,1)S(1)}, bf16[1,12,64]{2,1,0:T(8,128)(2,1)}, u32[]{:S(2)}) copy-start(bf16[1,12,64]{2,1,0:T(8,128)(2,1)} %span_rope_ref.1) | copy-start | bytes 4612
  6.5 19.2 %copy-start.29 = (s32[16]{0:T(128)S(1)}, s32[16]{0:T(128)}, u32[]{:S(2)}) copy-start(s32[16]{0:T(128)} %param.16) | copy-start | bytes 196
  6.5 19.8 %copy-start.30 = (s32[16]{0:T(128)S(1)}, s32[16]{0:T(128)}, u32[]{:S(2)}) copy-start(s32[16]{0:T(128)} %param.17) | copy-start | bytes 196
  7.8 25.1 %collective-permute-start.2 = (bf16[224,1024]{1,0:T(8,128)(2,1)S(1)}, bf16[224,1024]{1,0:T(8,128)(2,1)S(1)}, u32[]{:S(2)}, u32[]{:S(2)}) collective-permute-start(bf16[224,1024]{1,0:T(8,128)(2,1)S(1)} %get-tuple-element.24), channel_id=1, source_target_pairs={{0,1},{1,0},{2,3},{3,2},{4,5},{5,4},{6,7},{7,6},{8,9},{9,8},{10,11... | collective-permute-start | bytes 1376264 | tf_op jit(solution)/shard_map/ppermute | solution.py:27
  15.0 19.6 %all-to-all-start = ((bf16[16,72,128]{2,1,0:T(8,128)(2,1)}), bf16[16,72,128]{2,1,0:T(8,128)(2,1)S(1)}, u32[]{:S(2)}, u32[]{:S(2)}) async-start(bf16[16,72,128]{2,1,0:T(8,128)(2,1)} %pack.1), calls=%async_computation | async-start | bytes 589824 | tf_op jit(solution)/shard_map/all_to_all | solution.py:313
  22.6 97.4 %all-gather.3.cloned.1.call-start = ((), (), s32[]{:S(2)}) async-start(), calls=%async_computation.3 | async-start | bytes 8257536 | tf_op jit(solution)/shard_map/all_gather | solution.py:327
  22.7 7.7 %collective-permute-start = (bf16[1,12,512]{2,1,0:T(8,128)(2,1)S(1)}, bf16[1,12,512]{2,1,0:T(8,128)(2,1)S(1)}, u32[]{:S(2)}, u32[]{:S(2)}) collective-permute-start(bf16[1,12,512]{2,1,0:T(8,128)(2,1)S(1)} %copy-done.25), channel_id=1, source_target_pairs={{0,2},{2,0},{1,3},{3,1},{4,6},{6,4},{5,7},{7,5},{8,10},{10,8},{9,1... | collective-permute-start | bytes 36872 | tf_op jit(solution)/shard_map/ppermute | solution.py:27
  25.4 5.0 %collective-permute-start.1 = (bf16[1,12,64]{2,1,0:T(8,128)(2,1)S(1)}, bf16[1,12,64]{2,1,0:T(8,128)(2,1)S(1)}, u32[]{:S(2)}, u32[]{:S(2)}) collective-permute-start(bf16[1,12,64]{2,1,0:T(8,128)(2,1)S(1)} %copy-done.27), channel_id=1, source_target_pairs={{0,2},{2,0},{1,3},{3,1},{4,6},{6,4},{5,7},{7,5},{8,10},{10,8},{9,1... | collective-permute-start | bytes 4616 | tf_op jit(solution)/shard_map/ppermute | solution.py:27
  30.3 0.6 copy-start.28
  30.9 0.6 copy-start.26
  33.0 10.0 %copy-start.19 = (bf16[2,72,128]{2,1,0:T(8,128)(2,1)S(1)}, bf16[2,72,128]{2,1,0:T(8,128)(2,1)}, u32[]{:S(2)}) copy-start(bf16[2,72,128]{2,1,0:T(8,128)(2,1)} %pack_fresh.1) | copy-start | bytes 110596
  34.7 8.3 %collective-permute-start.3 = (bf16[16,72,128]{2,1,0:T(8,128)(2,1)S(1)}, bf16[16,72,128]{2,1,0:T(8,128)(2,1)S(1)}, u32[]{:S(2)}, u32[]{:S(2)}) collective-permute-start(bf16[16,72,128]{2,1,0:T(8,128)(2,1)S(1)} %all-to-all-done), channel_id=1, source_target_pairs={{0,2},{2,0},{1,3},{3,1},{4,6},{6,4},{5,7},{7,5},{8,10},{10,8},{9,1... | collective-permute-start | bytes 884744 | tf_op jit(solution)/shard_map/ppermute | solution.py:27
  43.0 30.0 %copy-start.4 = (bf16[34,72,128]{2,1,0:T(8,128)(2,1)}, bf16[34,72,128]{2,1,0:T(8,128)(2,1)S(1)}, u32[]{:S(2)}) copy-start(bf16[34,72,128]{2,1,0:T(8,128)(2,1)S(1)} %constant_dynamic-update-slice_fusion.rest_0_) | copy-start | bytes 1880068
  43.0 14.3 %collective-permute-start.4 = (bf16[34,72,128]{2,1,0:T(8,128)(2,1)S(1)}, bf16[34,72,128]{2,1,0:T(8,128)(2,1)S(1)}, u32[]{:S(2)}, u32[]{:S(2)}) collective-permute-start(bf16[34,72,128]{2,1,0:T(8,128)(2,1)S(1)} %constant_dynamic-update-slice_fusion.rest_0_), channel_id=1, source_target_pairs={{0,4},{4,8},{8,12},{12,0},{1,5},{5,9},{9,13},{13,1},{2,6},{6,10},{... | collective-permute-start | bytes 1880072 | tf_op jit(solution)/shard_map/ppermute | solution.py:27
  44.3 13.8 %collective-permute-start.5 = (bf16[34,72,128]{2,1,0:T(8,128)(2,1)S(1)}, bf16[34,72,128]{2,1,0:T(8,128)(2,1)S(1)}, u32[]{:S(2)}, u32[]{:S(2)}) collective-permute-start(bf16[34,72,128]{2,1,0:T(8,128)(2,1)S(1)} %constant_dynamic-update-slice_fusion.rest_0_), channel_id=1, source_target_pairs={{0,12},{4,0},{8,4},{12,8},{1,13},{5,1},{9,5},{13,9},{2,14},{6,2},{... | collective-permute-start | bytes 1880072 | tf_op jit(solution)/shard_map/ppermute | solution.py:27
  45.8 25.5 %collective-permute-start.8 = (bf16[34,72,128]{2,1,0:T(8,128)(2,1)S(1)}, bf16[34,72,128]{2,1,0:T(8,128)(2,1)S(1)}, u32[]{:S(2)}, u32[]{:S(2)}) collective-permute-start(bf16[34,72,128]{2,1,0:T(8,128)(2,1)S(1)} %constant_dynamic-update-slice_fusion.rest_0_), channel_id=1, source_target_pairs={{0,1},{1,0},{2,3},{3,2},{4,5},{5,4},{6,7},{7,6},{8,9},{9,8},{10,11... | collective-permute-start | bytes 1880072 | tf_op jit(solution)/shard_map/ppermute | solution.py:27
  57.3 15.7 %copy-start = (bf16[34,72,128]{2,1,0:T(8,128)(2,1)}, bf16[34,72,128]{2,1,0:T(8,128)(2,1)S(1)}, u32[]{:S(2)}) copy-start(bf16[34,72,128]{2,1,0:T(8,128)(2,1)S(1)} %collective-permute-done.4.rest_1_) | copy-start | bytes 1880068
  58.1 12.5 %collective-permute-start.6 = (bf16[17,72,128]{2,1,0:T(8,128)(2,1)}, bf16[17,72,128]{2,1,0:T(8,128)(2,1)S(1)}, u32[]{:S(2)}, u32[]{:S(2)}) collective-permute-start(bf16[17,72,128]{2,1,0:T(8,128)(2,1)} %slice.28), channel_id=1, source_target_pairs={{0,4},{4,8},{8,12},{12,0},{1,5},{5,9},{9,13},{13,1},{2,6},{6,10},{... | collective-permute-start | bytes 940040 | tf_op jit(solution)/shard_map/ppermute | solution.py:27
  58.1 14.9 %copy-start.2 = (bf16[34,72,128]{2,1,0:T(8,128)(2,1)}, bf16[34,72,128]{2,1,0:T(8,128)(2,1)S(1)}, u32[]{:S(2)}) copy-start(bf16[34,72,128]{2,1,0:T(8,128)(2,1)S(1)} %collective-permute-done.5.rest_2_) | copy-start | bytes 1880068
  58.9 12.0 %collective-permute-start.7 = (bf16[17,72,128]{2,1,0:T(8,128)(2,1)}, bf16[17,72,128]{2,1,0:T(8,128)(2,1)}, u32[]{:S(2)}, u32[]{:S(2)}) collective-permute-start(bf16[17,72,128]{2,1,0:T(8,128)(2,1)} %slice.29), channel_id=1, source_target_pairs={{0,12},{4,0},{8,4},{12,8},{1,13},{5,1},{9,5},{13,9},{2,14},{6,2},{... | collective-permute-start | bytes 940040 | tf_op jit(solution)/shard_map/ppermute | solution.py:27
  61.6 11.4 %collective-permute-start.10 = (bf16[34,72,128]{2,1,0:T(8,128)(2,1)S(1)}, bf16[34,72,128]{2,1,0:T(8,128)(2,1)S(1)}, u32[]{:S(2)}, u32[]{:S(2)}) collective-permute-start(bf16[34,72,128]{2,1,0:T(8,128)(2,1)S(1)} %collective-permute-done.5.rest_2_), channel_id=1, source_target_pairs={{0,1},{1,0},{2,3},{3,2},{4,5},{5,4},{6,7},{7,6},{8,9},{9,8},{10,11... | collective-permute-start | bytes 1880072 | tf_op jit(solution)/shard_map/ppermute | solution.py:27
  65.7 8.2 %collective-permute-start.9 = (bf16[34,72,128]{2,1,0:T(8,128)(2,1)S(1)}, bf16[34,72,128]{2,1,0:T(8,128)(2,1)}, u32[]{:S(2)}, u32[]{:S(2)}) collective-permute-start(bf16[34,72,128]{2,1,0:T(8,128)(2,1)S(1)} %collective-permute-done.4.rest_1_), channel_id=1, source_target_pairs={{0,1},{1,0},{2,3},{3,2},{4,5},{5,4},{6,7},{7,6},{8,9},{9,8},{10,11... | collective-permute-start | bytes 1880072 | tf_op jit(solution)/shard_map/ppermute | solution.py:27
  65.7 19.0 %all-to-all-start.1 = ((bf16[16,12,1536]{2,1,0:T(8,128)(2,1)}), bf16[16,12,1536]{2,1,0:T(8,128)(2,1)}, u32[]{:S(2)}, u32[]{:S(2)}) async-start(bf16[16,12,1536]{2,1,0:T(8,128)(2,1)} %split_queries.1), calls=%async_computation.1 | async-start | bytes 1572864 | tf_op jit(solution)/shard_map/all_to_all | solution.py:332
  70.7 1.7 collective-permute-start.11
  70.9 2.1 %collective-permute-start.12 = (bf16[17,72,128]{2,1,0:T(8,128)(2,1)}, bf16[17,72,128]{2,1,0:T(8,128)(2,1)S(1)}, u32[]{:S(2)}, u32[]{:S(2)}) collective-permute-start(bf16[17,72,128]{2,1,0:T(8,128)(2,1)} %collective-permute-done.7.rest_4_), channel_id=1, source_target_pairs={{0,1},{1,0},{2,3},{3,2},{4,5},{5,4},{6,7},{7,6},{8,9},{9,8},{10,11... | collective-permute-start | bytes 940040 | tf_op jit(solution)/shard_map/ppermute | solution.py:27
  71.4 0.8 copy-start.6
  73.1 0.8 copy-start.8
  73.9 1.1 copy-start.1
  75.0 1.1 copy-start.3
  76.1 1.1 copy-start.5
  77.2 1.1 copy-start.7
  78.2 1.1 copy-start.9
  86.0 1.6 copy-start.12
  95.5 9.5 %copy-start.10 = (bf16[192,512]{1,0:T(8,128)(2,1)}, bf16[192,512]{1,0:T(8,128)(2,1)S(1)}, u32[]{:S(2)}) copy-start(bf16[192,512]{1,0:T(8,128)(2,1)S(1)} %attend.3.refs_1_) | copy-start | bytes 589828
  95.5 11.1 %collective-permute-start.14 = (bf16[192,512]{1,0:T(8,128)(2,1)S(1)}, bf16[192,512]{1,0:T(8,128)(2,1)S(1)}, u32[]{:S(2)}, u32[]{:S(2)}) collective-permute-start(bf16[192,512]{1,0:T(8,128)(2,1)S(1)} %attend.3.refs_1_), channel_id=1, source_target_pairs={{0,16},{16,0},{1,17},{17,1},{2,18},{18,2},{3,19},{19,3},{4,20},{20... | collective-permute-start | bytes 589832 | tf_op jit(solution)/shard_map/ppermute | solution.py:27
  104.5 7.4 %copy-start.11 = (bf16[192,512]{1,0:T(8,128)(2,1)}, bf16[192,512]{1,0:T(8,128)(2,1)S(1)}, u32[]{:S(2)}) copy-start(bf16[192,512]{1,0:T(8,128)(2,1)S(1)} %attend.2.refs_0_) | copy-start | bytes 589828
  104.5 5.2 %collective-permute-start.13 = (bf16[192,512]{1,0:T(8,128)(2,1)S(1)}, bf16[192,512]{1,0:T(8,128)(2,1)S(1)}, u32[]{:S(2)}, u32[]{:S(2)}) collective-permute-start(bf16[192,512]{1,0:T(8,128)(2,1)S(1)} %attend.2.refs_0_), channel_id=1, source_target_pairs={{0,16},{16,0},{1,17},{17,1},{2,18},{18,2},{3,19},{19,3},{4,20},{20... | collective-permute-start | bytes 589832 | tf_op jit(solution)/shard_map/ppermute | solution.py:27
  105.0 6.9 %collective-permute-start.16 = (bf16[192,512]{1,0:T(8,128)(2,1)S(1)}, bf16[192,512]{1,0:T(8,128)(2,1)S(1)}, u32[]{:S(2)}, u32[]{:S(2)}) collective-permute-start(bf16[192,512]{1,0:T(8,128)(2,1)S(1)} %attend.3.refs_1_), channel_id=1, source_target_pairs={{0,1},{1,0},{2,3},{3,2},{4,5},{5,4},{6,7},{7,6},{8,9},{9,8},{10,11... | collective-permute-start | bytes 589832 | tf_op jit(solution)/shard_map/ppermute | solution.py:27
  106.6 5.3 %collective-permute-start.15 = (bf16[192,512]{1,0:T(8,128)(2,1)S(1)}, bf16[192,512]{1,0:T(8,128)(2,1)S(1)}, u32[]{:S(2)}, u32[]{:S(2)}) collective-permute-start(bf16[192,512]{1,0:T(8,128)(2,1)S(1)} %attend.2.refs_0_), channel_id=1, source_target_pairs={{0,1},{1,0},{2,3},{3,2},{4,5},{5,4},{6,7},{7,6},{8,9},{9,8},{10,11... | collective-permute-start | bytes 589832 | tf_op jit(solution)/shard_map/ppermute | solution.py:27
  106.7 5.3 %copy-start.13 = (bf16[192,512]{1,0:T(8,128)(2,1)}, bf16[192,512]{1,0:T(8,128)(2,1)S(1)}, u32[]{:S(2)}) copy-start(bf16[192,512]{1,0:T(8,128)(2,1)S(1)} %collective-permute-done.14.refs_3_) | copy-start | bytes 589828
  106.7 5.3 %collective-permute-start.18 = (bf16[192,512]{1,0:T(8,128)(2,1)S(1)}, bf16[192,512]{1,0:T(8,128)(2,1)S(1)}, u32[]{:S(2)}, u32[]{:S(2)}) collective-permute-start(bf16[192,512]{1,0:T(8,128)(2,1)S(1)} %collective-permute-done.14.refs_3_), channel_id=1, source_target_pairs={{0,1},{1,0},{2,3},{3,2},{4,5},{5,4},{6,7},{7,6},{8,9},{9,8},{10,11... | collective-permute-start | bytes 589832 | tf_op jit(solution)/shard_map/ppermute | solution.py:27
  109.7 10.3 %copy-start.14 = (bf16[192,512]{1,0:T(8,128)(2,1)}, bf16[192,512]{1,0:T(8,128)(2,1)S(1)}, u32[]{:S(2)}) copy-start(bf16[192,512]{1,0:T(8,128)(2,1)S(1)} %collective-permute-done.13.refs_2_) | copy-start | bytes 589828
  109.7 3.2 %collective-permute-start.17 = (bf16[192,512]{1,0:T(8,128)(2,1)S(1)}, bf16[192,512]{1,0:T(8,128)(2,1)S(1)}, u32[]{:S(2)}, u32[]{:S(2)}) collective-permute-start(bf16[192,512]{1,0:T(8,128)(2,1)S(1)} %collective-permute-done.13.refs_2_), channel_id=1, source_target_pairs={{0,1},{1,0},{2,3},{3,2},{4,5},{5,4},{6,7},{7,6},{8,9},{9,8},{10,11... | collective-permute-start | bytes 589832 | tf_op jit(solution)/shard_map/ppermute | solution.py:27
  111.9 8.2 %copy-start.15 = (bf16[192,512]{1,0:T(8,128)(2,1)}, bf16[192,512]{1,0:T(8,128)(2,1)S(1)}, u32[]{:S(2)}) copy-start(bf16[192,512]{1,0:T(8,128)(2,1)S(1)} %collective-permute-done.16.refs_5_) | copy-start | bytes 589828
  111.9 8.2 %copy-start.16 = (bf16[192,512]{1,0:T(8,128)(2,1)}, bf16[192,512]{1,0:T(8,128)(2,1)S(1)}, u32[]{:S(2)}) copy-start(bf16[192,512]{1,0:T(8,128)(2,1)S(1)} %collective-permute-done.15.refs_4_) | copy-start | bytes 589828
  111.9 8.1 %copy-start.17 = (bf16[192,512]{1,0:T(8,128)(2,1)}, bf16[192,512]{1,0:T(8,128)(2,1)S(1)}, u32[]{:S(2)}) copy-start(bf16[192,512]{1,0:T(8,128)(2,1)S(1)} %collective-permute-done.18.refs_7_) | copy-start | bytes 589828
  113.0 7.1 %copy-start.18 = (bf16[192,512]{1,0:T(8,128)(2,1)}, bf16[192,512]{1,0:T(8,128)(2,1)S(1)}, u32[]{:S(2)}) copy-start(bf16[192,512]{1,0:T(8,128)(2,1)S(1)} %collective-permute-done.17.refs_6_) | copy-start | bytes 589828
  127.1 26.7 %all-to-all-start.2 = ((bf16[8,2,24,1792]{3,2,1,0:T(8,128)(2,1)}), bf16[8,2,24,1792]{3,2,1,0:T(8,128)(2,1)S(1)}, u32[]{:S(2)}, u32[]{:S(2)}) async-start(bf16[8,2,24,1792]{3,2,1,0:T(8,128)(2,1)} %project.1), calls=%async_computation.2 | async-start | bytes 2752512 | tf_op jit(solution)/shard_map/all_to_all | solution.py:362
  154.5 4.8 %collective-permute-start.19 = (bf16[12,1792]{1,0:T(8,128)(2,1)S(1)}, bf16[12,1792]{1,0:T(8,128)(2,1)S(1)}, u32[]{:S(2)}, u32[]{:S(2)}) collective-permute-start(bf16[12,1792]{1,0:T(8,128)(2,1)S(1)} %bitcast.32), channel_id=1, source_target_pairs={{0,1},{1,0},{2,3},{3,2},{4,5},{5,4},{6,7},{7,6},{8,9},{9,8},{10,11... | collective-permute-start | bytes 129032 | tf_op jit(solution)/shard_map/ppermute | solution.py:27
  156.2 3.6 %collective-permute-start.20 = (bf16[12,1792]{1,0:T(8,128)(2,1)S(1)}, bf16[12,1792]{1,0:T(8,128)(2,1)S(1)}, u32[]{:S(2)}, u32[]{:S(2)}) collective-permute-start(bf16[12,1792]{1,0:T(8,128)(2,1)S(1)} %bitcast.33), channel_id=1, source_target_pairs={{0,16},{16,0},{1,17},{17,1},{2,18},{18,2},{3,19},{19,3},{4,20},{20... | collective-permute-start | bytes 129032 | tf_op jit(solution)/shard_map/ppermute | solution.py:27
  156.6 4.6 %collective-permute-start.21 = (bf16[12,1792]{1,0:T(8,128)(2,1)S(1)}, bf16[12,1792]{1,0:T(8,128)(2,1)S(1)}, u32[]{:S(2)}, u32[]{:S(2)}) collective-permute-start(bf16[12,1792]{1,0:T(8,128)(2,1)S(1)} %bitcast.34), channel_id=1, source_target_pairs={{0,17},{1,16},{16,1},{17,0},{2,19},{3,18},{18,3},{19,2},{4,21},{5,... | collective-permute-start | bytes 129032 | tf_op jit(solution)/shard_map/ppermute | solution.py:368
  159.3 1.9 %copy-start.20 = (bf16[12,1792]{1,0:T(8,128)(2,1)}, bf16[12,1792]{1,0:T(8,128)(2,1)S(1)}, u32[]{:S(2)}) copy-start(bf16[12,1792]{1,0:T(8,128)(2,1)S(1)} %collective-permute-done.19.c_ref) | copy-start | bytes 129028
  159.8 1.3 copy-start.21
  161.2 0.6 copy-start.22
Sparse Core Ops, SparseCore 0:
  34.8 85.2 all-gather.2

commit v5 on v4

--- a/solution.py
+++ b/solution.py
@@ -310,6 +310,11 @@
     high = jnp.max(jnp.where(owned, marked, 0), axis=1)
     picked = jnp.stack([low % slots, high % slots], 1).reshape(32)
     sent_pages = pack(picked, pool_latent, pool_rope.reshape(slots, PAGE, ROPE))
+    out_weight, sent_pages = lax.optimization_barrier((out_weight, sent_pages))
+    turned = out_weight.T
+    kept = lax.dynamic_slice_in_dim(turned, ci * 224, 224, 0)
+    given = lax.dynamic_slice_in_dim(turned, (1 - ci) * 224, 224, 0)
+    columns = jnp.concatenate([kept, swap_c(given)], 0)
     back = lax.all_to_all(sent_pages, ("z", "yl"), split_axis=0, concat_axis=0, tiled=True)
     fresh = pack_fresh(span_latent, span_rope, pair_latent, pair_rope)
     sent = split_queries(queries[0])
@@ -319,11 +324,7 @@
             lax.dynamic_index_in_dim(span_len, group, 0, keepdims=False),
         ]
     )
-    turned = out_weight.T
-    kept = lax.dynamic_slice_in_dim(turned, ci * 224, 224, 0)
-    given = lax.dynamic_slice_in_dim(turned, (1 - ci) * 224, 224, 0)
-    columns = jnp.concatenate([kept, swap_c(given)], 0)
-    back, fresh, sent, lens, columns = lax.optimization_barrier((back, fresh, sent, lens, columns))
+    back, columns = lax.optimization_barrier((back, columns))
     weight = lax.all_gather(columns, "z", axis=0, tiled=False)
     mine = jnp.concatenate([back, swap_yh(back), fresh], 0)
     half = PIECE // 2

time: 171 us -> 170 us (level)
  local copies, waits for them, and re-layouts: 18.5 us -> 14.5 us
  starting transfers between devices: 50.9 us -> 53.6 us
  other arithmetic: 3.66 us -> 5.88 us
  waiting for transfers between devices: 48 us -> 46.1 us
    all_to_all x1, waiting for transfers between devices: 0.63 us -> 10.9 us  [shards(): lax.all_to_all(sent_pages, ('z', 'yl'), split_axis=0, concat_axis=0, tile...]
    all_gather x1, waiting for transfers between devices: 7.1 us -> 0.01 us  [shards(): weight = lax.all_gather(columns, 'z', axis=0, tiled=False)]
    ppermute x21, waiting for transfers between devices: 18.6 us -> 13.4 us  [send(): lax.ppermute(value, axis, [(i, (i + by) % count) for i in range(count)])]
    all_to_all x1, starting transfers between devices: 4.74 us -> 8.76 us  [shards(): lax.all_to_all(sent, ('x', 'yh', 'c'), split_axis=0, concat_axis=0, tiled...]
    unnamed x68 -> x52, local copies, waits for them, and re-layouts: 11.3 us -> 8.04 us
  transfers between devices with their start and end apart: 26 -> 26, of which waited for: 12 -> 10; matrix products, arithmetic and copies ran while one was open for 6% -> 5% of each run, Pallas kernels for 16% -> 14%
where the time goes in v5:
time: 170 us; the launch traced here: 169 us
  starting transfers between devices  53.6 us (32%)
  waiting for transfers between devices  46.1 us (27%)
  Pallas kernels  35 us (21%)
  local copies, waits for them, and re-layouts  14.5 us (9%)
  between operations  13.7 us (8%)
  other arithmetic  5.88 us (3%)
    ppermute x21, starting transfers between devices, send(): lax.ppermute(value, axis, [(i, (i + by) % count) for i in range(count)])  30.8 us
    all_to_all x1, waiting for transfers between devices, shards(): lax.all_to_all(partial, ('x', 'yh'), split_axis=0, concat_axis=0, tiled=T...  20.4 us
    pallas_call x2, Pallas kernels, attend(): pl.pallas_call(attend_body, grid_spec=pltpu.PrefetchScalarGridSpec(num_sc...  15.7 us
    ppermute x21, waiting for transfers between devices, send(): lax.ppermute(value, axis, [(i, (i + by) % count) for i in range(count)])  13.4 us
    all_to_all x1, waiting for transfers between devices, shards(): lax.all_to_all(sent_pages, ('z', 'yl'), split_axis=0, concat_axis=0, tile...  10.9 us
    all_to_all x1, starting transfers between devices, shards(): lax.all_to_all(sent, ('x', 'yh', 'c'), split_axis=0, concat_axis=0, tiled...  8.76 us
    unnamed x52, local copies, waits for them, and re-layouts  8.04 us
    all_to_all x1, starting transfers between devices, shards(): lax.all_to_all(sent_pages, ('z', 'yl'), split_axis=0, concat_axis=0, tile...  7.57 us
  transfers between devices with their start and end apart: 26, of which 10 were waited for; matrix products, arithmetic and copies ran while one was open for 5% of the time, Pallas kernels for 14%

profile of v5, /device:TPU:1, one launch (start us, length us, event | category | flops | bytes accessed | tf_op | source)
XLA Modules:
  0.0 168.8 jit_solution(16150096362167758132)
XLA Ops:
  6.5 0.8 select_reduce_fusion.1
  7.5 0.7 reshape.127.slot_ref
  8.2 1.5 reshape.128.rope_ref
  9.7 2.2 %pack.1 = bf16[16,72,128]{2,1,0:T(8,128)(2,1)} custom-call(s32[32]{0:T(128)} %reshape.127.slot_ref, bf16[32,8,512]{2,1,0:T(8,128)(2,1)} %pool_ref.1, bf16[32,8,64]{2,1,0:T(8,128)(2,1)} %reshape.128.rope_ref), custom_call_target="tpu_custom_call" | custom-call | tf_op jit(solution)/shard_map/pack/pallas_call | solution.py:74
  11.9 1.2 dynamic-slice_bitcast_fusion.1
  13.2 3.3 %collective-permute-start = (bf16[224,1024]{1,0:T(8,128)(2,1)S(1)}, bf16[224,1024]{1,0:T(8,128)(2,1)S(1)}, u32[]{:S(2)}, u32[]{:S(2)}) collective-permute-start(bf16[224,1024]{1,0:T(8,128)(2,1)S(1)} %get-tuple-element.22), channel_id=1, source_target_pairs={{0,1},{1,0},{2,3},{3,2},{4,5},{5,4},{6,7},{7,6},{8,9},{9,8},{10,11... | collective-permute-start | bytes 1376264 | tf_op jit(solution)/shard_map/ppermute | solution.py:27
  16.5 7.6 %all-to-all-start.1 = ((bf16[16,72,128]{2,1,0:T(8,128)(2,1)}), bf16[16,72,128]{2,1,0:T(8,128)(2,1)S(1)}, u32[]{:S(2)}, u32[]{:S(2)}) async-start(bf16[16,72,128]{2,1,0:T(8,128)(2,1)} %pack.1), calls=%async_computation.1 | async-start | bytes 589824 | tf_op jit(solution)/shard_map/all_to_all | solution.py:318
  24.1 1.1 pad_maximum_fusion
  25.2 10.9 %all-to-all-done.1 = bf16[16,72,128]{2,1,0:T(8,128)(2,1)S(1)} async-done(((bf16[16,72,128]{2,1,0:T(8,128)(2,1)}), bf16[16,72,128]{2,1,0:T(8,128)(2,1)S(1)}, u32[]{:S(2)}, u32[]{:S(2)}) %all-to-all-start.1) | async-done | bytes 294944 | tf_op jit(solution)/shard_map/all_to_all | solution.py:318
  36.2 2.7 %collective-permute-start.1 = (bf16[16,72,128]{2,1,0:T(8,128)(2,1)S(1)}, bf16[16,72,128]{2,1,0:T(8,128)(2,1)S(1)}, u32[]{:S(2)}, u32[]{:S(2)}) collective-permute-start(bf16[16,72,128]{2,1,0:T(8,128)(2,1)S(1)} %all-to-all-done.1), channel_id=1, source_target_pairs={{0,2},{2,0},{1,3},{3,1},{4,6},{6,4},{5,7},{7,5},{8,10},{10,8},{9,1... | collective-permute-start | bytes 884744 | tf_op jit(solution)/shard_map/ppermute | solution.py:27
  38.9 0.3 collective-permute-start.2
  39.2 2.6 %collective-permute-start.3 = (bf16[1,12,64]{2,1,0:T(8,128)(2,1)S(1)}, bf16[1,12,64]{2,1,0:T(8,128)(2,1)S(1)}, u32[]{:S(2)}, u32[]{:S(2)}) collective-permute-start(bf16[1,12,64]{2,1,0:T(8,128)(2,1)S(1)} %copy-done.20), channel_id=1, source_target_pairs={{0,2},{2,0},{1,3},{3,1},{4,6},{6,4},{5,7},{7,5},{8,10},{10,8},{9,1... | collective-permute-start | bytes 4616 | tf_op jit(solution)/shard_map/ppermute | solution.py:27
  41.8 3.0 %collective-permute-done.3.pair_rope_ref = bf16[1,12,64]{2,1,0:T(8,128)(2,1)S(1)} collective-permute-done((bf16[1,12,64]{2,1,0:T(8,128)(2,1)S(1)}, bf16[1,12,64]{2,1,0:T(8,128)(2,1)S(1)}, u32[]{:S(2)}, u32[]{:S(2)}) %collective-permute-start.3) | collective-permute-done | bytes 1568 | tf_op jit(solution)/shard_map/ppermute | solution.py:27
  44.9 0.6 copy-done.21
  45.5 0.6 copy-done.19
  46.0 1.4 pack_fresh.1
  47.5 0.8 pad_maximum_fusion.1.rest_0_
  48.4 1.3 collective-permute-start.4
  49.7 1.5 collective-permute-start.5
  51.1 2.1 %split_queries.1 = bf16[16,12,1536]{2,1,0:T(8,128)(2,1)} custom-call(bf16[12,24576]{1,0:T(8,128)(2,1)} %bitcast.30), custom_call_target="tpu_custom_call" | custom-call | tf_op jit(solution)/shard_map/split_queries/pallas_call | solution.py:39
  53.2 8.8 %all-to-all-start = ((bf16[16,12,1536]{2,1,0:T(8,128)(2,1)}), bf16[16,12,1536]{2,1,0:T(8,128)(2,1)}, u32[]{:S(2)}, u32[]{:S(2)}) async-start(bf16[16,12,1536]{2,1,0:T(8,128)(2,1)} %split_queries.1), calls=%async_computation | async-start | bytes 1572864 | tf_op jit(solution)/shard_map/all_to_all | solution.py:333
  62.0 0.6 dynamic_slice.24
  62.6 0.6 dynamic_slice.25
  63.2 0.7 and_select_fusion
  63.9 0.2 collective-permute-start.8
  64.2 1.7 collective-permute-start.6
  65.9 1.3 collective-permute-start.7
  67.2 8.2 %collective-permute-start.10 = (bf16[34,72,128]{2,1,0:T(8,128)(2,1)S(1)}, bf16[34,72,128]{2,1,0:T(8,128)(2,1)S(1)}, u32[]{:S(2)}, u32[]{:S(2)}) collective-permute-start(bf16[34,72,128]{2,1,0:T(8,128)(2,1)S(1)} %collective-permute-done.5.rest_2_), channel_id=1, source_target_pairs={{0,1},{1,0},{2,3},{3,2},{4,5},{5,4},{6,7},{7,6},{8,9},{9,8},{10,11... | collective-permute-start | bytes 1880072 | tf_op jit(solution)/shard_map/ppermute | solution.py:27
  75.4 1.3 pad_add_fusion.3.lens_ref
  76.7 0.2 convert_reduce_fusion
  76.9 3.9 %collective-permute-done.6.rest_3_ = bf16[17,72,128]{2,1,0:T(8,128)(2,1)S(1)} collective-permute-done((bf16[17,72,128]{2,1,0:T(8,128)(2,1)S(1)}, bf16[17,72,128]{2,1,0:T(8,128)(2,1)S(1)}, u32[]{:S(2)}, u32[]{:S(2)}) %collective-permute-start.6) | collective-permute-done | bytes 313376 | tf_op jit(solution)/shard_map/ppermute | solution.py:27
  80.8 0.8 collective-permute-start.11
  81.6 1.2 collective-permute-done.11.rest_8_
  82.8 0.4 collective-permute-done.12.rest_9_
  83.2 1.1 copy-done.1
  84.3 1.1 copy-done.3
  85.4 1.1 copy-done.5
  86.5 4.8 %assemble.1.keys = bf16[2304,640]{1,0:T(8,128)(2,1)S(1)} custom-call(s32[288]{0:T(512)S(1)} %pad_add_fusion.index_ref, bf16[34,72,128]{2,1,0:T(8,128)(2,1)S(1)} %copy-done.1, bf16[34,72,128]{2,1,0:T(8,128)(2,1)S(1)} %copy-done.3, bf16[34,72,128]{2,1,0:T(8,128)(2,1)S(1)} %copy-done.5, bf16[17,72,128]{2,1,0:T(8,128)(2,1)S(1)} %collective-permute-done.6.rest_3_, ...), custom_call_target="tpu_custom_call" | custom-call | bytes 16000000 | tf_op jit(solution)/shard_map/assemble/pallas_call | solution.py:140
  91.3 1.3 reshape.129.q_ref
  92.6 1.6 copy-done.8
  94.2 7.8 %attend.3.refs_1_ = bf16[192,512]{1,0:T(8,128)(2,1)S(1)} custom-call(s32[2]{0:T(128)S(1)} %pad_add_fusion.3.lens_ref, bf16[192,1536]{1,0:T(8,128)(2,1)S(1)} %reshape.129.q_ref, bf16[512,2048]{1,0:T(8,128)(2,1)S(1)} %copy-done.8, bf16[2304,640]{1,0:T(8,128)(2,1)S(1)} %assemble.1.keys), custom_call_target="tpu_custom_call" | custom-call | flops 5000000000 | bytes 4000000 | tf_op jit(solution)/shard_map/attend/pallas_call | solution.py:197
  102.1 7.8 %attend.2.refs_0_ = bf16[192,512]{1,0:T(8,128)(2,1)S(1)} custom-call(s32[2]{0:T(128)S(1)} %pad_add_fusion.3.lens_ref, bf16[192,1536]{1,0:T(8,128)(2,1)S(1)} %reshape.129.q_ref, bf16[512,2048]{1,0:T(8,128)(2,1)S(1)} %copy-done.8, bf16[2304,640]{1,0:T(8,128)(2,1)S(1)} %assemble.1.keys), custom_call_target="tpu_custom_call" | custom-call | flops 5000000000 | bytes 4000000 | tf_op jit(solution)/shard_map/attend/pallas_call | solution.py:197
  110.0 1.5 collective-permute-start.13
  111.5 0.9 collective-permute-start.16
  112.5 0.5 collective-permute-start.18
  113.0 3.3 %collective-permute-done.13.refs_2_ = bf16[192,512]{1,0:T(8,128)(2,1)S(1)} collective-permute-done((bf16[192,512]{1,0:T(8,128)(2,1)S(1)}, bf16[192,512]{1,0:T(8,128)(2,1)S(1)}, u32[]{:S(2)}, u32[]{:S(2)}) %collective-permute-start.13) | collective-permute-done | bytes 196640 | tf_op jit(solution)/shard_map/ppermute | solution.py:27
  116.3 1.1 collective-permute-start.17
  117.5 1.0 collective-permute-done.17.refs_6_
  118.5 0.7 copy-done.14
  119.2 7.0 %project.1 = bf16[8,2,24,1792]{3,2,1,0:T(8,128)(2,1)} custom-call(bf16[192,512]{1,0:T(8,128)(2,1)} %copy-done.7, bf16[192,512]{1,0:T(8,128)(2,1)} %copy-done.6, bf16[192,512]{1,0:T(8,128)(2,1)} %copy-done.10, bf16[192,512]{1,0:T(8,128)(2,1)} %copy-done.9, bf16[192,512]{1,0:T(8,128)(2,1)} %copy-done.12, bf16[192,512]{1,0:T(8,128)(2,1)} %copy-done.11, ...), custom_call_target="tpu_custom_call" | custom-call | tf_op jit(solution)/shard_map/project/pallas_call | solution.py:245
  126.2 5.7 %all-to-all-start.2 = ((bf16[8,2,24,1792]{3,2,1,0:T(8,128)(2,1)}), bf16[8,2,24,1792]{3,2,1,0:T(8,128)(2,1)S(1)}, u32[]{:S(2)}, u32[]{:S(2)}) async-start(bf16[8,2,24,1792]{3,2,1,0:T(8,128)(2,1)} %project.1), calls=%async_computation.2 | async-start | bytes 2752512 | tf_op jit(solution)/shard_map/all_to_all | solution.py:363
  131.9 20.4 %all-to-all-done.2 = bf16[8,2,24,1792]{3,2,1,0:T(8,128)(2,1)S(1)} async-done(((bf16[8,2,24,1792]{3,2,1,0:T(8,128)(2,1)}), bf16[8,2,24,1792]{3,2,1,0:T(8,128)(2,1)S(1)}, u32[]{:S(2)}, u32[]{:S(2)}) %all-to-all-start.2) | async-done | bytes 1376288 | tf_op jit(solution)/shard_map/all_to_all | solution.py:363
  152.3 0.2 reduce_sum.22
  152.5 0.1 copy.20
  152.6 0.3 constant_dynamic-slice_fusion.2
  152.9 1.7 collective-permute-start.19
  154.6 1.1 collective-permute-start.20
  155.7 0.8 collective-permute-start.21
  156.4 0.6 pad_add_fusion.2.where_ref
  157.0 0.6 copy.36
  157.7 0.6 collective-permute-done.20.y_ref
  158.2 1.4 collective-permute-done.21.both_ref
  159.6 0.6 copy-done.17
  160.2 1.7 %arrange.1 = bf16[12,7168]{1,0:T(8,128)(2,1)} custom-call(s32[2]{0:T(128)} %pad_add_fusion.2.where_ref, bf16[12,1792]{1,0:T(8,128)(2,1)} %bitcast.31, bf16[12,1792]{1,0:T(8,128)(2,1)} %copy-done.15, bf16[12,1792]{1,0:T(8,128)(2,1)} %copy-done.16, bf16[12,1792]{1,0:T(8,128)(2,1)} %copy-done.17), custom_call_target="tpu_custom_call" | custom-call | tf_op jit(solution)/shard_map/arrange/pallas_call | solution.py:272
  (75 shorter events, 0.6 us)
Async XLA Ops:
  13.1 25.7 %copy-start.18 = (bf16[1,12,512]{2,1,0:T(8,128)(2,1)S(1)}, bf16[1,12,512]{2,1,0:T(8,128)(2,1)}, u32[]{:S(2)}) copy-start(bf16[1,12,512]{2,1,0:T(8,128)(2,1)} %span_ref.1) | copy-start | bytes 36868
  13.1 26.1 %copy-start.20 = (bf16[1,12,64]{2,1,0:T(8,128)(2,1)S(1)}, bf16[1,12,64]{2,1,0:T(8,128)(2,1)}, u32[]{:S(2)}) copy-start(bf16[1,12,64]{2,1,0:T(8,128)(2,1)} %span_rope_ref.1) | copy-start | bytes 4612
  13.2 11.0 %collective-permute-start = (bf16[224,1024]{1,0:T(8,128)(2,1)S(1)}, bf16[224,1024]{1,0:T(8,128)(2,1)S(1)}, u32[]{:S(2)}, u32[]{:S(2)}) collective-permute-start(bf16[224,1024]{1,0:T(8,128)(2,1)S(1)} %get-tuple-element.22), channel_id=1, source_target_pairs={{0,1},{1,0},{2,3},{3,2},{4,5},{5,4},{6,7},{7,6},{8,9},{9,8},{10,11... | collective-permute-start | bytes 1376264 | tf_op jit(solution)/shard_map/ppermute | solution.py:27
  16.5 19.6 %all-to-all-start.1 = ((bf16[16,72,128]{2,1,0:T(8,128)(2,1)}), bf16[16,72,128]{2,1,0:T(8,128)(2,1)S(1)}, u32[]{:S(2)}, u32[]{:S(2)}) async-start(bf16[16,72,128]{2,1,0:T(8,128)(2,1)} %pack.1), calls=%async_computation.1 | async-start | bytes 589824 | tf_op jit(solution)/shard_map/all_to_all | solution.py:318
  24.1 94.4 %all-gather.3.cloned.1.call-start = ((), (), s32[]{:S(2)}) async-start(), calls=%async_computation.3 | async-start | bytes 8257536 | tf_op jit(solution)/shard_map/all_gather | solution.py:328
  36.2 11.3 %collective-permute-start.1 = (bf16[16,72,128]{2,1,0:T(8,128)(2,1)S(1)}, bf16[16,72,128]{2,1,0:T(8,128)(2,1)S(1)}, u32[]{:S(2)}, u32[]{:S(2)}) collective-permute-start(bf16[16,72,128]{2,1,0:T(8,128)(2,1)S(1)} %all-to-all-done.1), channel_id=1, source_target_pairs={{0,2},{2,0},{1,3},{3,1},{4,6},{6,4},{5,7},{7,5},{8,10},{10,8},{9,1... | collective-permute-start | bytes 884744 | tf_op jit(solution)/shard_map/ppermute | solution.py:27
  38.9 6.0 %collective-permute-start.2 = (bf16[1,12,512]{2,1,0:T(8,128)(2,1)S(1)}, bf16[1,12,512]{2,1,0:T(8,128)(2,1)S(1)}, u32[]{:S(2)}, u32[]{:S(2)}) collective-permute-start(bf16[1,12,512]{2,1,0:T(8,128)(2,1)S(1)} %copy-done.18), channel_id=1, source_target_pairs={{0,2},{2,0},{1,3},{3,1},{4,6},{6,4},{5,7},{7,5},{8,10},{10,8},{9,1... | collective-permute-start | bytes 36872 | tf_op jit(solution)/shard_map/ppermute | solution.py:27
  39.2 5.6 %collective-permute-start.3 = (bf16[1,12,64]{2,1,0:T(8,128)(2,1)S(1)}, bf16[1,12,64]{2,1,0:T(8,128)(2,1)S(1)}, u32[]{:S(2)}, u32[]{:S(2)}) collective-permute-start(bf16[1,12,64]{2,1,0:T(8,128)(2,1)S(1)} %copy-done.20), channel_id=1, source_target_pairs={{0,2},{2,0},{1,3},{3,1},{4,6},{6,4},{5,7},{7,5},{8,10},{10,8},{9,1... | collective-permute-start | bytes 4616 | tf_op jit(solution)/shard_map/ppermute | solution.py:27
  44.9 0.6 copy-start.21
  45.5 0.6 copy-start.19
  48.3 15.8 %copy-start = (bf16[34,72,128]{2,1,0:T(8,128)(2,1)}, bf16[34,72,128]{2,1,0:T(8,128)(2,1)S(1)}, u32[]{:S(2)}) copy-start(bf16[34,72,128]{2,1,0:T(8,128)(2,1)S(1)} %pad_maximum_fusion.1.rest_0_) | copy-start | bytes 1880068
  48.4 13.6 %copy-start.22 = (s32[16]{0:T(128)S(1)}, s32[16]{0:T(128)}, u32[]{:S(2)}) copy-start(s32[16]{0:T(128)} %param.16) | copy-start | bytes 196
  48.4 14.2 %copy-start.23 = (s32[16]{0:T(128)S(1)}, s32[16]{0:T(128)}, u32[]{:S(2)}) copy-start(s32[16]{0:T(128)} %param.17) | copy-start | bytes 196
  48.4 15.7 %collective-permute-start.4 = (bf16[34,72,128]{2,1,0:T(8,128)(2,1)S(1)}, bf16[34,72,128]{2,1,0:T(8,128)(2,1)S(1)}, u32[]{:S(2)}, u32[]{:S(2)}) collective-permute-start(bf16[34,72,128]{2,1,0:T(8,128)(2,1)S(1)} %pad_maximum_fusion.1.rest_0_), channel_id=1, source_target_pairs={{0,4},{4,8},{8,12},{12,0},{1,5},{5,9},{9,13},{13,1},{2,6},{6,10},{... | collective-permute-start | bytes 1880072 | tf_op jit(solution)/shard_map/ppermute | solution.py:27
  49.7 16.2 %collective-permute-start.5 = (bf16[34,72,128]{2,1,0:T(8,128)(2,1)S(1)}, bf16[34,72,128]{2,1,0:T(8,128)(2,1)S(1)}, u32[]{:S(2)}, u32[]{:S(2)}) collective-permute-start(bf16[34,72,128]{2,1,0:T(8,128)(2,1)S(1)} %pad_maximum_fusion.1.rest_0_), channel_id=1, source_target_pairs={{0,12},{4,0},{8,4},{12,8},{1,13},{5,1},{9,5},{13,9},{2,14},{6,2},{... | collective-permute-start | bytes 1880072 | tf_op jit(solution)/shard_map/ppermute | solution.py:27
  53.2 38.1 %all-to-all-start = ((bf16[16,12,1536]{2,1,0:T(8,128)(2,1)}), bf16[16,12,1536]{2,1,0:T(8,128)(2,1)}, u32[]{:S(2)}, u32[]{:S(2)}) async-start(bf16[16,12,1536]{2,1,0:T(8,128)(2,1)} %split_queries.1), calls=%async_computation | async-start | bytes 1572864 | tf_op jit(solution)/shard_map/all_to_all | solution.py:333
  63.9 17.7 %collective-permute-start.8 = (bf16[34,72,128]{2,1,0:T(8,128)(2,1)S(1)}, bf16[34,72,128]{2,1,0:T(8,128)(2,1)S(1)}, u32[]{:S(2)}, u32[]{:S(2)}) collective-permute-start(bf16[34,72,128]{2,1,0:T(8,128)(2,1)S(1)} %pad_maximum_fusion.1.rest_0_), channel_id=1, source_target_pairs={{0,1},{1,0},{2,3},{3,2},{4,5},{5,4},{6,7},{7,6},{8,9},{9,8},{10,11... | collective-permute-start | bytes 1880072 | tf_op jit(solution)/shard_map/ppermute | solution.py:27
  64.1 19.1 %copy-start.2 = (bf16[34,72,128]{2,1,0:T(8,128)(2,1)}, bf16[34,72,128]{2,1,0:T(8,128)(2,1)S(1)}, u32[]{:S(2)}) copy-start(bf16[34,72,128]{2,1,0:T(8,128)(2,1)S(1)} %collective-permute-done.4.rest_1_) | copy-start | bytes 1880068
  64.2 16.6 %collective-permute-start.6 = (bf16[17,72,128]{2,1,0:T(8,128)(2,1)S(1)}, bf16[17,72,128]{2,1,0:T(8,128)(2,1)S(1)}, u32[]{:S(2)}, u32[]{:S(2)}) collective-permute-start(bf16[17,72,128]{2,1,0:T(8,128)(2,1)S(1)} %slice.28), channel_id=1, source_target_pairs={{0,4},{4,8},{8,12},{12,0},{1,5},{5,9},{9,13},{13,1},{2,6},{6,10},{... | collective-permute-start | bytes 940040 | tf_op jit(solution)/shard_map/ppermute | solution.py:27
  65.9 17.4 %copy-start.4 = (bf16[34,72,128]{2,1,0:T(8,128)(2,1)}, bf16[34,72,128]{2,1,0:T(8,128)(2,1)S(1)}, u32[]{:S(2)}) copy-start(bf16[34,72,128]{2,1,0:T(8,128)(2,1)S(1)} %collective-permute-done.5.rest_2_) | copy-start | bytes 1880068
  65.9 15.7 %collective-permute-start.7 = (bf16[17,72,128]{2,1,0:T(8,128)(2,1)S(1)}, bf16[17,72,128]{2,1,0:T(8,128)(2,1)S(1)}, u32[]{:S(2)}, u32[]{:S(2)}) collective-permute-start(bf16[17,72,128]{2,1,0:T(8,128)(2,1)S(1)} %slice.29), channel_id=1, source_target_pairs={{0,12},{4,0},{8,4},{12,8},{1,13},{5,1},{9,5},{13,9},{2,14},{6,2},{... | collective-permute-start | bytes 940040 | tf_op jit(solution)/shard_map/ppermute | solution.py:27
  67.2 16.0 %collective-permute-start.10 = (bf16[34,72,128]{2,1,0:T(8,128)(2,1)S(1)}, bf16[34,72,128]{2,1,0:T(8,128)(2,1)S(1)}, u32[]{:S(2)}, u32[]{:S(2)}) collective-permute-start(bf16[34,72,128]{2,1,0:T(8,128)(2,1)S(1)} %collective-permute-done.5.rest_2_), channel_id=1, source_target_pairs={{0,1},{1,0},{2,3},{3,2},{4,5},{5,4},{6,7},{7,6},{8,9},{9,8},{10,11... | collective-permute-start | bytes 1880072 | tf_op jit(solution)/shard_map/ppermute | solution.py:27
  75.4 7.9 %collective-permute-start.9 = (bf16[34,72,128]{2,1,0:T(8,128)(2,1)S(1)}, bf16[34,72,128]{2,1,0:T(8,128)(2,1)S(1)}, u32[]{:S(2)}, u32[]{:S(2)}) collective-permute-start(bf16[34,72,128]{2,1,0:T(8,128)(2,1)S(1)} %collective-permute-done.4.rest_1_), channel_id=1, source_target_pairs={{0,1},{1,0},{2,3},{3,2},{4,5},{5,4},{6,7},{7,6},{8,9},{9,8},{10,11... | collective-permute-start | bytes 1880072 | tf_op jit(solution)/shard_map/ppermute | solution.py:27
  80.8 2.0 %collective-permute-start.11 = (bf16[17,72,128]{2,1,0:T(8,128)(2,1)S(1)}, bf16[17,72,128]{2,1,0:T(8,128)(2,1)S(1)}, u32[]{:S(2)}, u32[]{:S(2)}) collective-permute-start(bf16[17,72,128]{2,1,0:T(8,128)(2,1)S(1)} %collective-permute-done.6.rest_3_), channel_id=1, source_target_pairs={{0,1},{1,0},{2,3},{3,2},{4,5},{5,4},{6,7},{7,6},{8,9},{9,8},{10,11... | collective-permute-start | bytes 940040 | tf_op jit(solution)/shard_map/ppermute | solution.py:27
  81.5 1.7 collective-permute-start.12
  83.2 1.1 copy-start.1
  84.3 1.1 copy-start.3
  85.4 1.1 copy-start.5
  92.6 1.6 copy-start.8
  102.0 9.5 %copy-start.6 = (bf16[192,512]{1,0:T(8,128)(2,1)}, bf16[192,512]{1,0:T(8,128)(2,1)S(1)}, u32[]{:S(2)}) copy-start(bf16[192,512]{1,0:T(8,128)(2,1)S(1)} %attend.3.refs_1_) | copy-start | bytes 589828
  102.0 10.4 %collective-permute-start.14 = (bf16[192,512]{1,0:T(8,128)(2,1)S(1)}, bf16[192,512]{1,0:T(8,128)(2,1)S(1)}, u32[]{:S(2)}, u32[]{:S(2)}) collective-permute-start(bf16[192,512]{1,0:T(8,128)(2,1)S(1)} %attend.3.refs_1_), channel_id=1, source_target_pairs={{0,16},{16,0},{1,17},{17,1},{2,18},{18,2},{3,19},{19,3},{4,20},{20... | collective-permute-start | bytes 589832 | tf_op jit(solution)/shard_map/ppermute | solution.py:27
  110.0 7.4 %copy-start.7 = (bf16[192,512]{1,0:T(8,128)(2,1)}, bf16[192,512]{1,0:T(8,128)(2,1)S(1)}, u32[]{:S(2)}) copy-start(bf16[192,512]{1,0:T(8,128)(2,1)S(1)} %attend.2.refs_0_) | copy-start | bytes 589828
  110.0 6.3 %collective-permute-start.13 = (bf16[192,512]{1,0:T(8,128)(2,1)S(1)}, bf16[192,512]{1,0:T(8,128)(2,1)S(1)}, u32[]{:S(2)}, u32[]{:S(2)}) collective-permute-start(bf16[192,512]{1,0:T(8,128)(2,1)S(1)} %attend.2.refs_0_), channel_id=1, source_target_pairs={{0,16},{16,0},{1,17},{17,1},{2,18},{18,2},{3,19},{19,3},{4,20},{20... | collective-permute-start | bytes 589832 | tf_op jit(solution)/shard_map/ppermute | solution.py:27
  111.5 5.9 %collective-permute-start.16 = (bf16[192,512]{1,0:T(8,128)(2,1)S(1)}, bf16[192,512]{1,0:T(8,128)(2,1)S(1)}, u32[]{:S(2)}, u32[]{:S(2)}) collective-permute-start(bf16[192,512]{1,0:T(8,128)(2,1)S(1)} %attend.3.refs_1_), channel_id=1, source_target_pairs={{0,1},{1,0},{2,3},{3,2},{4,5},{5,4},{6,7},{7,6},{8,9},{9,8},{10,11... | collective-permute-start | bytes 589832 | tf_op jit(solution)/shard_map/ppermute | solution.py:27
  112.5 4.9 %collective-permute-start.15 = (bf16[192,512]{1,0:T(8,128)(2,1)S(1)}, bf16[192,512]{1,0:T(8,128)(2,1)S(1)}, u32[]{:S(2)}, u32[]{:S(2)}) collective-permute-start(bf16[192,512]{1,0:T(8,128)(2,1)S(1)} %attend.2.refs_0_), channel_id=1, source_target_pairs={{0,1},{1,0},{2,3},{3,2},{4,5},{5,4},{6,7},{7,6},{8,9},{9,8},{10,11... | collective-permute-start | bytes 589832 | tf_op jit(solution)/shard_map/ppermute | solution.py:27
  112.5 4.9 %copy-start.9 = (bf16[192,512]{1,0:T(8,128)(2,1)}, bf16[192,512]{1,0:T(8,128)(2,1)S(1)}, u32[]{:S(2)}) copy-start(bf16[192,512]{1,0:T(8,128)(2,1)S(1)} %collective-permute-done.14.refs_3_) | copy-start | bytes 589828
  112.5 5.0 %collective-permute-start.18 = (bf16[192,512]{1,0:T(8,128)(2,1)S(1)}, bf16[192,512]{1,0:T(8,128)(2,1)S(1)}, u32[]{:S(2)}, u32[]{:S(2)}) collective-permute-start(bf16[192,512]{1,0:T(8,128)(2,1)S(1)} %collective-permute-done.14.refs_3_), channel_id=1, source_target_pairs={{0,1},{1,0},{2,3},{3,2},{4,5},{5,4},{6,7},{7,6},{8,9},{9,8},{10,11... | collective-permute-start | bytes 589832 | tf_op jit(solution)/shard_map/ppermute | solution.py:27
  116.3 2.2 %copy-start.10 = (bf16[192,512]{1,0:T(8,128)(2,1)}, bf16[192,512]{1,0:T(8,128)(2,1)S(1)}, u32[]{:S(2)}) copy-start(bf16[192,512]{1,0:T(8,128)(2,1)S(1)} %collective-permute-done.13.refs_2_) | copy-start | bytes 589828
  116.3 2.2 %collective-permute-start.17 = (bf16[192,512]{1,0:T(8,128)(2,1)S(1)}, bf16[192,512]{1,0:T(8,128)(2,1)S(1)}, u32[]{:S(2)}, u32[]{:S(2)}) collective-permute-start(bf16[192,512]{1,0:T(8,128)(2,1)S(1)} %collective-permute-done.13.refs_2_), channel_id=1, source_target_pairs={{0,1},{1,0},{2,3},{3,2},{4,5},{5,4},{6,7},{7,6},{8,9},{9,8},{10,11... | collective-permute-start | bytes 589832 | tf_op jit(solution)/shard_map/ppermute | solution.py:27
  117.4 1.1 copy-start.11
  117.4 1.1 copy-start.12
  117.4 1.1 copy-start.13
  118.5 0.7 copy-start.14
  126.2 26.0 %all-to-all-start.2 = ((bf16[8,2,24,1792]{3,2,1,0:T(8,128)(2,1)}), bf16[8,2,24,1792]{3,2,1,0:T(8,128)(2,1)S(1)}, u32[]{:S(2)}, u32[]{:S(2)}) async-start(bf16[8,2,24,1792]{3,2,1,0:T(8,128)(2,1)} %project.1), calls=%async_computation.2 | async-start | bytes 2752512 | tf_op jit(solution)/shard_map/all_to_all | solution.py:363
  152.9 4.7 %collective-permute-start.19 = (bf16[12,1792]{1,0:T(8,128)(2,1)S(1)}, bf16[12,1792]{1,0:T(8,128)(2,1)S(1)}, u32[]{:S(2)}, u32[]{:S(2)}) collective-permute-start(bf16[12,1792]{1,0:T(8,128)(2,1)S(1)} %bitcast.32), channel_id=1, source_target_pairs={{0,1},{1,0},{2,3},{3,2},{4,5},{5,4},{6,7},{7,6},{8,9},{9,8},{10,11... | collective-permute-start | bytes 129032 | tf_op jit(solution)/shard_map/ppermute | solution.py:27
  154.6 3.6 %collective-permute-start.20 = (bf16[12,1792]{1,0:T(8,128)(2,1)S(1)}, bf16[12,1792]{1,0:T(8,128)(2,1)S(1)}, u32[]{:S(2)}, u32[]{:S(2)}) collective-permute-start(bf16[12,1792]{1,0:T(8,128)(2,1)S(1)} %bitcast.33), channel_id=1, source_target_pairs={{0,16},{16,0},{1,17},{17,1},{2,18},{18,2},{3,19},{19,3},{4,20},{20... | collective-permute-start | bytes 129032 | tf_op jit(solution)/shard_map/ppermute | solution.py:27
  155.7 3.9 %collective-permute-start.21 = (bf16[12,1792]{1,0:T(8,128)(2,1)S(1)}, bf16[12,1792]{1,0:T(8,128)(2,1)S(1)}, u32[]{:S(2)}, u32[]{:S(2)}) collective-permute-start(bf16[12,1792]{1,0:T(8,128)(2,1)S(1)} %bitcast.34), channel_id=1, source_target_pairs={{0,17},{1,16},{16,1},{17,0},{2,19},{3,18},{18,3},{19,2},{4,21},{5,... | collective-permute-start | bytes 129032 | tf_op jit(solution)/shard_map/ppermute | solution.py:369
  157.7 1.9 %copy-start.15 = (bf16[12,1792]{1,0:T(8,128)(2,1)}, bf16[12,1792]{1,0:T(8,128)(2,1)S(1)}, u32[]{:S(2)}) copy-start(bf16[12,1792]{1,0:T(8,128)(2,1)S(1)} %collective-permute-done.19.c_ref) | copy-start | bytes 129028
  158.2 1.4 copy-start.16
  159.6 0.6 copy-start.17
Sparse Core Ops, SparseCore 0:
  36.3 81.9 all-gather.2

commit v6 on v5

--- a/solution.py
+++ b/solution.py
@@ -324,7 +324,7 @@
             lax.dynamic_index_in_dim(span_len, group, 0, keepdims=False),
         ]
     )
-    back, columns = lax.optimization_barrier((back, columns))
+    back, columns, fresh = lax.optimization_barrier((back, columns, fresh))
     weight = lax.all_gather(columns, "z", axis=0, tiled=False)
     mine = jnp.concatenate([back, swap_yh(back), fresh], 0)
     half = PIECE // 2

time: 170 us -> 171 us (level)
  waiting for transfers between devices: 46.1 us -> 48.3 us
    all_to_all x1, waiting for transfers between devices: 10.9 us -> 1.35 us  [shards(): lax.all_to_all(sent_pages, ('z', 'yl'), split_axis=0, concat_axis=0, tile...]
    ppermute x21, waiting for transfers between devices: 13.4 us -> 19.6 us  [send(): lax.ppermute(value, axis, [(i, (i + by) % count) for i in range(count)])]
    all_gather x1, waiting for transfers between devices: 0.01 us -> 5.75 us  [shards(): weight = lax.all_gather(columns, 'z', axis=0, tiled=False)]
    unnamed x52 -> x56, local copies, waits for them, and re-layouts: 8.04 us -> 7.48 us
  transfers between devices with their start and end apart: 26 -> 26, of which waited for: 10 -> 12; matrix products, arithmetic and copies ran while one was open for 5% -> 4% of each run, Pallas kernels for 14% -> 14%
where the time goes in v6:
time: 171 us
  starting transfers between devices  54.4 us (32%)
  waiting for transfers between devices  48.3 us (28%)
  Pallas kernels  35.1 us (21%)
  local copies, waits for them, and re-layouts  13.9 us (8%)
  between operations  13.7 us (8%)
  other arithmetic  5.16 us (3%)
    ppermute x21, starting transfers between devices, send(): lax.ppermute(value, axis, [(i, (i + by) % count) for i in range(count)])  30.3 us
    all_to_all x1, waiting for transfers between devices, shards(): lax.all_to_all(partial, ('x', 'yh'), split_axis=0, concat_axis=0, tiled=T...  20.2 us
    ppermute x21, waiting for transfers between devices, send(): lax.ppermute(value, axis, [(i, (i + by) % count) for i in range(count)])  19.6 us
    pallas_call x2, Pallas kernels, attend(): pl.pallas_call(attend_body, grid_spec=pltpu.PrefetchScalarGridSpec(num_sc...  15.7 us
    all_to_all x1, starting transfers between devices, shards(): lax.all_to_all(sent, ('x', 'yh', 'c'), split_axis=0, concat_axis=0, tiled...  8.66 us
    all_to_all x1, starting transfers between devices, shards(): lax.all_to_all(sent_pages, ('z', 'yl'), split_axis=0, concat_axis=0, tile...  7.57 us
    unnamed x56, local copies, waits for them, and re-layouts  7.48 us
    pallas_call x1, Pallas kernels, project(): pl.pallas_call(project_body, grid=(2,), in_specs=[pl.BlockSpec((SPAN, 512...  7.05 us
  transfers between devices with their start and end apart: 26, of which 12 were waited for; matrix products, arithmetic and copies ran while one was open for 4% of the time, Pallas kernels for 14%

profile of v6, /device:TPU:1, one launch (start us, length us, event | category | flops | bytes accessed | tf_op | source)
XLA Modules:
  0.0 170.6 jit_solution(7208383491965133953)
XLA Ops:
  6.5 0.9 select_reduce_fusion.1
  7.5 0.6 reshape.127.slot_ref
  8.1 1.5 reshape.128.rope_ref
  9.6 2.2 %pack.1 = bf16[16,72,128]{2,1,0:T(8,128)(2,1)} custom-call(s32[32]{0:T(128)} %reshape.127.slot_ref, bf16[32,8,512]{2,1,0:T(8,128)(2,1)} %pool_ref.1, bf16[32,8,64]{2,1,0:T(8,128)(2,1)} %reshape.128.rope_ref), custom_call_target="tpu_custom_call" | custom-call | tf_op jit(solution)/shard_map/pack/pallas_call | solution.py:74
  11.8 1.2 dynamic-slice_bitcast_fusion.1
  13.1 3.3 %collective-permute-start = (bf16[224,1024]{1,0:T(8,128)(2,1)S(1)}, bf16[224,1024]{1,0:T(8,128)(2,1)S(1)}, u32[]{:S(2)}, u32[]{:S(2)}) collective-permute-start(bf16[224,1024]{1,0:T(8,128)(2,1)S(1)} %get-tuple-element.24), channel_id=1, source_target_pairs={{0,1},{1,0},{2,3},{3,2},{4,5},{5,4},{6,7},{7,6},{8,9},{9,8},{10,11... | collective-permute-start | bytes 1376264 | tf_op jit(solution)/shard_map/ppermute | solution.py:27
  16.4 7.6 %all-to-all-start.1 = ((bf16[16,72,128]{2,1,0:T(8,128)(2,1)}), bf16[16,72,128]{2,1,0:T(8,128)(2,1)S(1)}, u32[]{:S(2)}, u32[]{:S(2)}) async-start(bf16[16,72,128]{2,1,0:T(8,128)(2,1)} %pack.1), calls=%async_computation.1 | async-start | bytes 589824 | tf_op jit(solution)/shard_map/all_to_all | solution.py:318
  24.0 2.7 %collective-permute-start.1 = (bf16[1,12,512]{2,1,0:T(8,128)(2,1)S(1)}, bf16[1,12,512]{2,1,0:T(8,128)(2,1)S(1)}, u32[]{:S(2)}, u32[]{:S(2)}) collective-permute-start(bf16[1,12,512]{2,1,0:T(8,128)(2,1)S(1)} %copy-done.19), channel_id=1, source_target_pairs={{0,2},{2,0},{1,3},{3,1},{4,6},{6,4},{5,7},{7,5},{8,10},{10,8},{9,1... | collective-permute-start | bytes 36872 | tf_op jit(solution)/shard_map/ppermute | solution.py:27
  26.7 0.3 collective-permute-start.2
  27.1 3.9 %collective-permute-done.2.pair_rope_ref = bf16[1,12,64]{2,1,0:T(8,128)(2,1)S(1)} collective-permute-done((bf16[1,12,64]{2,1,0:T(8,128)(2,1)S(1)}, bf16[1,12,64]{2,1,0:T(8,128)(2,1)S(1)}, u32[]{:S(2)}, u32[]{:S(2)}) %collective-permute-start.2) | collective-permute-done | bytes 1568 | tf_op jit(solution)/shard_map/ppermute | solution.py:27
  31.0 0.6 copy-done.22
  31.6 0.6 copy-done.20
  32.2 1.4 pack_fresh.1
  33.6 1.1 pad_maximum_fusion
  34.7 1.4 all-to-all-done.1
  36.1 2.7 %collective-permute-start.3 = (bf16[16,72,128]{2,1,0:T(8,128)(2,1)S(1)}, bf16[16,72,128]{2,1,0:T(8,128)(2,1)S(1)}, u32[]{:S(2)}, u32[]{:S(2)}) collective-permute-start(bf16[16,72,128]{2,1,0:T(8,128)(2,1)S(1)} %all-to-all-done.1), channel_id=1, source_target_pairs={{0,2},{2,0},{1,3},{3,1},{4,6},{6,4},{5,7},{7,5},{8,10},{10,8},{9,1... | collective-permute-start | bytes 884744 | tf_op jit(solution)/shard_map/ppermute | solution.py:27
  38.8 5.5 %collective-permute-done.3 = bf16[16,72,128]{2,1,0:T(8,128)(2,1)S(1)} collective-permute-done((bf16[16,72,128]{2,1,0:T(8,128)(2,1)S(1)}, bf16[16,72,128]{2,1,0:T(8,128)(2,1)S(1)}, u32[]{:S(2)}, u32[]{:S(2)}) %collective-permute-start.3) | collective-permute-done | bytes 294944 | tf_op jit(solution)/shard_map/ppermute | solution.py:27
  44.4 1.3 collective-permute-start.4
  45.7 1.5 collective-permute-start.5
  47.2 2.1 %split_queries.1 = bf16[16,12,1536]{2,1,0:T(8,128)(2,1)} custom-call(bf16[12,24576]{1,0:T(8,128)(2,1)} %bitcast.30), custom_call_target="tpu_custom_call" | custom-call | tf_op jit(solution)/shard_map/split_queries/pallas_call | solution.py:39
  49.3 8.7 %all-to-all-start = ((bf16[16,12,1536]{2,1,0:T(8,128)(2,1)}), bf16[16,12,1536]{2,1,0:T(8,128)(2,1)}, u32[]{:S(2)}, u32[]{:S(2)}) async-start(bf16[16,12,1536]{2,1,0:T(8,128)(2,1)} %split_queries.1), calls=%async_computation | async-start | bytes 1572864 | tf_op jit(solution)/shard_map/all_to_all | solution.py:333
  58.0 0.7 dynamic_slice.24
  58.6 0.6 dynamic_slice.25
  59.2 0.7 and_select_fusion
  60.0 0.2 collective-permute-start.8
  60.2 1.7 collective-permute-start.6
  61.9 1.3 collective-permute-start.7
  63.3 8.2 %collective-permute-start.10 = (bf16[34,72,128]{2,1,0:T(8,128)(2,1)S(1)}, bf16[34,72,128]{2,1,0:T(8,128)(2,1)S(1)}, u32[]{:S(2)}, u32[]{:S(2)}) collective-permute-start(bf16[34,72,128]{2,1,0:T(8,128)(2,1)S(1)} %collective-permute-done.5.rest_2_), channel_id=1, source_target_pairs={{0,1},{1,0},{2,3},{3,2},{4,5},{5,4},{6,7},{7,6},{8,9},{9,8},{10,11... | collective-permute-start | bytes 1880072 | tf_op jit(solution)/shard_map/ppermute | solution.py:27
  71.5 1.4 pad_add_fusion.3.lens_ref
  72.8 0.2 convert_reduce_fusion
  73.0 3.8 %collective-permute-done.6.rest_3_ = bf16[17,72,128]{2,1,0:T(8,128)(2,1)S(1)} collective-permute-done((bf16[17,72,128]{2,1,0:T(8,128)(2,1)S(1)}, bf16[17,72,128]{2,1,0:T(8,128)(2,1)S(1)}, u32[]{:S(2)}, u32[]{:S(2)}) %collective-permute-start.6) | collective-permute-done | bytes 313376 | tf_op jit(solution)/shard_map/ppermute | solution.py:27
  76.8 0.8 collective-permute-start.11
  77.6 1.2 collective-permute-done.11.rest_8_
  78.8 0.4 collective-permute-done.12.rest_9_
  79.3 1.1 copy-done.1
  80.4 1.1 copy-done.3
  81.4 1.1 copy-done.5
  82.5 4.8 %assemble.1.keys = bf16[2304,640]{1,0:T(8,128)(2,1)S(1)} custom-call(s32[288]{0:T(512)S(1)} %pad_add_fusion.index_ref, bf16[34,72,128]{2,1,0:T(8,128)(2,1)S(1)} %copy-done.5, bf16[34,72,128]{2,1,0:T(8,128)(2,1)S(1)} %copy-done.1, bf16[34,72,128]{2,1,0:T(8,128)(2,1)S(1)} %copy-done.3, bf16[17,72,128]{2,1,0:T(8,128)(2,1)S(1)} %collective-permute-done.6.rest_3_, ...), custom_call_target="tpu_custom_call" | custom-call | bytes 16000000 | tf_op jit(solution)/shard_map/assemble/pallas_call | solution.py:140
  87.3 1.3 reshape.129.q_ref
  88.6 1.6 copy-done.8
  90.3 7.8 %attend.3.refs_1_ = bf16[192,512]{1,0:T(8,128)(2,1)S(1)} custom-call(s32[2]{0:T(128)S(1)} %pad_add_fusion.3.lens_ref, bf16[192,1536]{1,0:T(8,128)(2,1)S(1)} %reshape.129.q_ref, bf16[512,2048]{1,0:T(8,128)(2,1)S(1)} %copy-done.8, bf16[2304,640]{1,0:T(8,128)(2,1)S(1)} %assemble.1.keys), custom_call_target="tpu_custom_call" | custom-call | flops 5000000000 | bytes 4000000 | tf_op jit(solution)/shard_map/attend/pallas_call | solution.py:197
  98.2 7.8 %attend.2.refs_0_ = bf16[192,512]{1,0:T(8,128)(2,1)S(1)} custom-call(s32[2]{0:T(128)S(1)} %pad_add_fusion.3.lens_ref, bf16[192,1536]{1,0:T(8,128)(2,1)S(1)} %reshape.129.q_ref, bf16[512,2048]{1,0:T(8,128)(2,1)S(1)} %copy-done.8, bf16[2304,640]{1,0:T(8,128)(2,1)S(1)} %assemble.1.keys), custom_call_target="tpu_custom_call" | custom-call | flops 5000000000 | bytes 4000000 | tf_op jit(solution)/shard_map/attend/pallas_call | solution.py:197
  106.1 1.5 collective-permute-start.13
  107.6 0.9 collective-permute-start.16
  108.5 0.5 collective-permute-start.18
  109.0 3.3 %collective-permute-done.13.refs_2_ = bf16[192,512]{1,0:T(8,128)(2,1)S(1)} collective-permute-done((bf16[192,512]{1,0:T(8,128)(2,1)S(1)}, bf16[192,512]{1,0:T(8,128)(2,1)S(1)}, u32[]{:S(2)}, u32[]{:S(2)}) %collective-permute-start.13) | collective-permute-done | bytes 196640 | tf_op jit(solution)/shard_map/ppermute | solution.py:27
  112.4 1.1 collective-permute-start.17
  113.5 1.0 collective-permute-done.17.refs_6_
  114.5 5.8 %all-gather.3.cloned.1.call-done = bf16[3584,1024]{1,0:T(8,128)(2,1)} async-done(((bf16[448,1024]{1,0:T(8,128)(2,1)}), bf16[3584,1024]{1,0:T(8,128)(2,1)}) %all-gather.3.cloned.1.call-update) | async-done | bytes 7340048 | tf_op jit(solution)/shard_map/all_gather | solution.py:328
  120.3 7.1 %project.1 = bf16[8,2,24,1792]{3,2,1,0:T(8,128)(2,1)} custom-call(bf16[192,512]{1,0:T(8,128)(2,1)} %copy-done.7, bf16[192,512]{1,0:T(8,128)(2,1)} %copy-done.6, bf16[192,512]{1,0:T(8,128)(2,1)} %copy-done.10, bf16[192,512]{1,0:T(8,128)(2,1)} %copy-done.9, bf16[192,512]{1,0:T(8,128)(2,1)} %copy-done.12, bf16[192,512]{1,0:T(8,128)(2,1)} %copy-done.11, ...), custom_call_target="tpu_custom_call" | custom-call | tf_op jit(solution)/shard_map/project/pallas_call | solution.py:245
  127.4 6.4 %all-to-all-start.2 = ((bf16[8,2,24,1792]{3,2,1,0:T(8,128)(2,1)}), bf16[8,2,24,1792]{3,2,1,0:T(8,128)(2,1)S(1)}, u32[]{:S(2)}, u32[]{:S(2)}) async-start(bf16[8,2,24,1792]{3,2,1,0:T(8,128)(2,1)} %project.1), calls=%async_computation.2 | async-start | bytes 2752512 | tf_op jit(solution)/shard_map/all_to_all | solution.py:363
  133.8 20.2 %all-to-all-done.2 = bf16[8,2,24,1792]{3,2,1,0:T(8,128)(2,1)S(1)} async-done(((bf16[8,2,24,1792]{3,2,1,0:T(8,128)(2,1)}), bf16[8,2,24,1792]{3,2,1,0:T(8,128)(2,1)S(1)}, u32[]{:S(2)}, u32[]{:S(2)}) %all-to-all-start.2) | async-done | bytes 1376288 | tf_op jit(solution)/shard_map/all_to_all | solution.py:363
  154.0 0.2 reduce_sum.22
  154.2 0.1 copy.20
  154.4 0.3 constant_dynamic-slice_fusion.2
  154.7 1.7 %collective-permute-start.19 = (bf16[12,1792]{1,0:T(8,128)(2,1)S(1)}, bf16[12,1792]{1,0:T(8,128)(2,1)S(1)}, u32[]{:S(2)}, u32[]{:S(2)}) collective-permute-start(bf16[12,1792]{1,0:T(8,128)(2,1)S(1)} %bitcast.32), channel_id=1, source_target_pairs={{0,1},{1,0},{2,3},{3,2},{4,5},{5,4},{6,7},{7,6},{8,9},{9,8},{10,11... | collective-permute-start | bytes 129032 | tf_op jit(solution)/shard_map/ppermute | solution.py:27
  156.4 0.4 collective-permute-start.20
  156.8 1.4 collective-permute-start.21
  158.3 0.6 pad_add_fusion.2.where_ref
  158.9 0.6 copy.36
  159.5 0.5 collective-permute-done.20.y_ref
  160.0 1.3 collective-permute-done.21.both_ref
  161.4 0.6 copy-done.18
  162.0 1.7 %arrange.1 = bf16[12,7168]{1,0:T(8,128)(2,1)} custom-call(s32[2]{0:T(128)} %pad_add_fusion.2.where_ref, bf16[12,1792]{1,0:T(8,128)(2,1)} %bitcast.31, bf16[12,1792]{1,0:T(8,128)(2,1)} %copy-done.16, bf16[12,1792]{1,0:T(8,128)(2,1)} %copy-done.17, bf16[12,1792]{1,0:T(8,128)(2,1)} %copy-done.18), custom_call_target="tpu_custom_call" | custom-call | tf_op jit(solution)/shard_map/arrange/pallas_call | solution.py:272
  (79 shorter events, 0.6 us)
Async XLA Ops:
  6.5 17.5 %copy-start.19 = (bf16[1,12,512]{2,1,0:T(8,128)(2,1)S(1)}, bf16[1,12,512]{2,1,0:T(8,128)(2,1)}, u32[]{:S(2)}) copy-start(bf16[1,12,512]{2,1,0:T(8,128)(2,1)} %span_ref.1) | copy-start | bytes 36868
  6.5 20.2 %copy-start.21 = (bf16[1,12,64]{2,1,0:T(8,128)(2,1)S(1)}, bf16[1,12,64]{2,1,0:T(8,128)(2,1)}, u32[]{:S(2)}) copy-start(bf16[1,12,64]{2,1,0:T(8,128)(2,1)} %span_rope_ref.1) | copy-start | bytes 4612
  13.1 20.5 %collective-permute-start = (bf16[224,1024]{1,0:T(8,128)(2,1)S(1)}, bf16[224,1024]{1,0:T(8,128)(2,1)S(1)}, u32[]{:S(2)}, u32[]{:S(2)}) collective-permute-start(bf16[224,1024]{1,0:T(8,128)(2,1)S(1)} %get-tuple-element.24), channel_id=1, source_target_pairs={{0,1},{1,0},{2,3},{3,2},{4,5},{5,4},{6,7},{7,6},{8,9},{9,8},{10,11... | collective-permute-start | bytes 1376264 | tf_op jit(solution)/shard_map/ppermute | solution.py:27
  16.4 19.6 %all-to-all-start.1 = ((bf16[16,72,128]{2,1,0:T(8,128)(2,1)}), bf16[16,72,128]{2,1,0:T(8,128)(2,1)S(1)}, u32[]{:S(2)}, u32[]{:S(2)}) async-start(bf16[16,72,128]{2,1,0:T(8,128)(2,1)} %pack.1), calls=%async_computation.1 | async-start | bytes 589824 | tf_op jit(solution)/shard_map/all_to_all | solution.py:318
  24.0 96.3 %all-gather.3.cloned.1.call-start = ((), (), s32[]{:S(2)}) async-start(), calls=%async_computation.3 | async-start | bytes 8257536 | tf_op jit(solution)/shard_map/all_gather | solution.py:328
  24.0 6.9 %collective-permute-start.1 = (bf16[1,12,512]{2,1,0:T(8,128)(2,1)S(1)}, bf16[1,12,512]{2,1,0:T(8,128)(2,1)S(1)}, u32[]{:S(2)}, u32[]{:S(2)}) collective-permute-start(bf16[1,12,512]{2,1,0:T(8,128)(2,1)S(1)} %copy-done.19), channel_id=1, source_target_pairs={{0,2},{2,0},{1,3},{3,1},{4,6},{6,4},{5,7},{7,5},{8,10},{10,8},{9,1... | collective-permute-start | bytes 36872 | tf_op jit(solution)/shard_map/ppermute | solution.py:27
  26.7 4.2 %collective-permute-start.2 = (bf16[1,12,64]{2,1,0:T(8,128)(2,1)S(1)}, bf16[1,12,64]{2,1,0:T(8,128)(2,1)S(1)}, u32[]{:S(2)}, u32[]{:S(2)}) collective-permute-start(bf16[1,12,64]{2,1,0:T(8,128)(2,1)S(1)} %copy-done.21), channel_id=1, source_target_pairs={{0,2},{2,0},{1,3},{3,1},{4,6},{6,4},{5,7},{7,5},{8,10},{10,8},{9,1... | collective-permute-start | bytes 4616 | tf_op jit(solution)/shard_map/ppermute | solution.py:27
  31.0 0.6 copy-start.22
  31.6 0.6 copy-start.20
  33.6 10.8 %copy-start.15 = (bf16[2,72,128]{2,1,0:T(8,128)(2,1)S(1)}, bf16[2,72,128]{2,1,0:T(8,128)(2,1)}, u32[]{:S(2)}) copy-start(bf16[2,72,128]{2,1,0:T(8,128)(2,1)} %pack_fresh.1) | copy-start | bytes 110596
  36.1 8.3 %collective-permute-start.3 = (bf16[16,72,128]{2,1,0:T(8,128)(2,1)S(1)}, bf16[16,72,128]{2,1,0:T(8,128)(2,1)S(1)}, u32[]{:S(2)}, u32[]{:S(2)}) collective-permute-start(bf16[16,72,128]{2,1,0:T(8,128)(2,1)S(1)} %all-to-all-done.1), channel_id=1, source_target_pairs={{0,2},{2,0},{1,3},{3,1},{4,6},{6,4},{5,7},{7,5},{8,10},{10,8},{9,1... | collective-permute-start | bytes 884744 | tf_op jit(solution)/shard_map/ppermute | solution.py:27
  38.8 19.2 %copy-start.23 = (s32[16]{0:T(128)S(1)}, s32[16]{0:T(128)}, u32[]{:S(2)}) copy-start(s32[16]{0:T(128)} %param.16) | copy-start | bytes 196
  38.8 19.8 %copy-start.24 = (s32[16]{0:T(128)S(1)}, s32[16]{0:T(128)}, u32[]{:S(2)}) copy-start(s32[16]{0:T(128)} %param.17) | copy-start | bytes 196
  44.4 15.8 %copy-start.4 = (bf16[34,72,128]{2,1,0:T(8,128)(2,1)}, bf16[34,72,128]{2,1,0:T(8,128)(2,1)S(1)}, u32[]{:S(2)}) copy-start(bf16[34,72,128]{2,1,0:T(8,128)(2,1)S(1)} %constant_dynamic-update-slice_fusion.rest_0_) | copy-start | bytes 1880068
  44.4 15.8 %collective-permute-start.4 = (bf16[34,72,128]{2,1,0:T(8,128)(2,1)S(1)}, bf16[34,72,128]{2,1,0:T(8,128)(2,1)S(1)}, u32[]{:S(2)}, u32[]{:S(2)}) collective-permute-start(bf16[34,72,128]{2,1,0:T(8,128)(2,1)S(1)} %constant_dynamic-update-slice_fusion.rest_0_), channel_id=1, source_target_pairs={{0,4},{4,8},{8,12},{12,0},{1,5},{5,9},{9,13},{13,1},{2,6},{6,10},{... | collective-permute-start | bytes 1880072 | tf_op jit(solution)/shard_map/ppermute | solution.py:27
  45.7 16.2 %collective-permute-start.5 = (bf16[34,72,128]{2,1,0:T(8,128)(2,1)S(1)}, bf16[34,72,128]{2,1,0:T(8,128)(2,1)S(1)}, u32[]{:S(2)}, u32[]{:S(2)}) collective-permute-start(bf16[34,72,128]{2,1,0:T(8,128)(2,1)S(1)} %constant_dynamic-update-slice_fusion.rest_0_), channel_id=1, source_target_pairs={{0,12},{4,0},{8,4},{12,8},{1,13},{5,1},{9,5},{13,9},{2,14},{6,2},{... | collective-permute-start | bytes 1880072 | tf_op jit(solution)/shard_map/ppermute | solution.py:27
  49.3 38.0 %all-to-all-start = ((bf16[16,12,1536]{2,1,0:T(8,128)(2,1)}), bf16[16,12,1536]{2,1,0:T(8,128)(2,1)}, u32[]{:S(2)}, u32[]{:S(2)}) async-start(bf16[16,12,1536]{2,1,0:T(8,128)(2,1)} %split_queries.1), calls=%async_computation | async-start | bytes 1572864 | tf_op jit(solution)/shard_map/all_to_all | solution.py:333
  60.0 17.7 %collective-permute-start.8 = (bf16[34,72,128]{2,1,0:T(8,128)(2,1)S(1)}, bf16[34,72,128]{2,1,0:T(8,128)(2,1)S(1)}, u32[]{:S(2)}, u32[]{:S(2)}) collective-permute-start(bf16[34,72,128]{2,1,0:T(8,128)(2,1)S(1)} %constant_dynamic-update-slice_fusion.rest_0_), channel_id=1, source_target_pairs={{0,1},{1,0},{2,3},{3,2},{4,5},{5,4},{6,7},{7,6},{8,9},{9,8},{10,11... | collective-permute-start | bytes 1880072 | tf_op jit(solution)/shard_map/ppermute | solution.py:27
  60.2 19.1 %copy-start = (bf16[34,72,128]{2,1,0:T(8,128)(2,1)}, bf16[34,72,128]{2,1,0:T(8,128)(2,1)S(1)}, u32[]{:S(2)}) copy-start(bf16[34,72,128]{2,1,0:T(8,128)(2,1)S(1)} %collective-permute-done.4.rest_1_) | copy-start | bytes 1880068
  60.2 16.6 %collective-permute-start.6 = (bf16[17,72,128]{2,1,0:T(8,128)(2,1)S(1)}, bf16[17,72,128]{2,1,0:T(8,128)(2,1)S(1)}, u32[]{:S(2)}, u32[]{:S(2)}) collective-permute-start(bf16[17,72,128]{2,1,0:T(8,128)(2,1)S(1)} %slice.28), channel_id=1, source_target_pairs={{0,4},{4,8},{8,12},{12,0},{1,5},{5,9},{9,13},{13,1},{2,6},{6,10},{... | collective-permute-start | bytes 940040 | tf_op jit(solution)/shard_map/ppermute | solution.py:27
  61.9 17.3 %copy-start.2 = (bf16[34,72,128]{2,1,0:T(8,128)(2,1)}, bf16[34,72,128]{2,1,0:T(8,128)(2,1)S(1)}, u32[]{:S(2)}) copy-start(bf16[34,72,128]{2,1,0:T(8,128)(2,1)S(1)} %collective-permute-done.5.rest_2_) | copy-start | bytes 1880068
  61.9 15.6 %collective-permute-start.7 = (bf16[17,72,128]{2,1,0:T(8,128)(2,1)S(1)}, bf16[17,72,128]{2,1,0:T(8,128)(2,1)S(1)}, u32[]{:S(2)}, u32[]{:S(2)}) collective-permute-start(bf16[17,72,128]{2,1,0:T(8,128)(2,1)S(1)} %slice.29), channel_id=1, source_target_pairs={{0,12},{4,0},{8,4},{12,8},{1,13},{5,1},{9,5},{13,9},{2,14},{6,2},{... | collective-permute-start | bytes 940040 | tf_op jit(solution)/shard_map/ppermute | solution.py:27
  63.3 16.0 %collective-permute-start.10 = (bf16[34,72,128]{2,1,0:T(8,128)(2,1)S(1)}, bf16[34,72,128]{2,1,0:T(8,128)(2,1)S(1)}, u32[]{:S(2)}, u32[]{:S(2)}) collective-permute-start(bf16[34,72,128]{2,1,0:T(8,128)(2,1)S(1)} %collective-permute-done.5.rest_2_), channel_id=1, source_target_pairs={{0,1},{1,0},{2,3},{3,2},{4,5},{5,4},{6,7},{7,6},{8,9},{9,8},{10,11... | collective-permute-start | bytes 1880072 | tf_op jit(solution)/shard_map/ppermute | solution.py:27
  71.4 7.8 %collective-permute-start.9 = (bf16[34,72,128]{2,1,0:T(8,128)(2,1)S(1)}, bf16[34,72,128]{2,1,0:T(8,128)(2,1)S(1)}, u32[]{:S(2)}, u32[]{:S(2)}) collective-permute-start(bf16[34,72,128]{2,1,0:T(8,128)(2,1)S(1)} %collective-permute-done.4.rest_1_), channel_id=1, source_target_pairs={{0,1},{1,0},{2,3},{3,2},{4,5},{5,4},{6,7},{7,6},{8,9},{9,8},{10,11... | collective-permute-start | bytes 1880072 | tf_op jit(solution)/shard_map/ppermute | solution.py:27
  76.8 2.0 %collective-permute-start.11 = (bf16[17,72,128]{2,1,0:T(8,128)(2,1)S(1)}, bf16[17,72,128]{2,1,0:T(8,128)(2,1)S(1)}, u32[]{:S(2)}, u32[]{:S(2)}) collective-permute-start(bf16[17,72,128]{2,1,0:T(8,128)(2,1)S(1)} %collective-permute-done.6.rest_3_), channel_id=1, source_target_pairs={{0,1},{1,0},{2,3},{3,2},{4,5},{5,4},{6,7},{7,6},{8,9},{9,8},{10,11... | collective-permute-start | bytes 940040 | tf_op jit(solution)/shard_map/ppermute | solution.py:27
  77.6 1.7 collective-permute-start.12
  79.3 1.1 copy-start.1
  80.3 1.1 copy-start.3
  81.4 1.1 copy-start.5
  88.6 1.6 copy-start.8
  98.1 9.5 %copy-start.6 = (bf16[192,512]{1,0:T(8,128)(2,1)}, bf16[192,512]{1,0:T(8,128)(2,1)S(1)}, u32[]{:S(2)}) copy-start(bf16[192,512]{1,0:T(8,128)(2,1)S(1)} %attend.3.refs_1_) | copy-start | bytes 589828
  98.1 10.4 %collective-permute-start.14 = (bf16[192,512]{1,0:T(8,128)(2,1)S(1)}, bf16[192,512]{1,0:T(8,128)(2,1)S(1)}, u32[]{:S(2)}, u32[]{:S(2)}) collective-permute-start(bf16[192,512]{1,0:T(8,128)(2,1)S(1)} %attend.3.refs_1_), channel_id=1, source_target_pairs={{0,16},{16,0},{1,17},{17,1},{2,18},{18,2},{3,19},{19,3},{4,20},{20... | collective-permute-start | bytes 589832 | tf_op jit(solution)/shard_map/ppermute | solution.py:27
  106.0 7.4 %copy-start.7 = (bf16[192,512]{1,0:T(8,128)(2,1)}, bf16[192,512]{1,0:T(8,128)(2,1)S(1)}, u32[]{:S(2)}) copy-start(bf16[192,512]{1,0:T(8,128)(2,1)S(1)} %attend.2.refs_0_) | copy-start | bytes 589828
  106.1 6.3 %collective-permute-start.13 = (bf16[192,512]{1,0:T(8,128)(2,1)S(1)}, bf16[192,512]{1,0:T(8,128)(2,1)S(1)}, u32[]{:S(2)}, u32[]{:S(2)}) collective-permute-start(bf16[192,512]{1,0:T(8,128)(2,1)S(1)} %attend.2.refs_0_), channel_id=1, source_target_pairs={{0,16},{16,0},{1,17},{17,1},{2,18},{18,2},{3,19},{19,3},{4,20},{20... | collective-permute-start | bytes 589832 | tf_op jit(solution)/shard_map/ppermute | solution.py:27
  107.6 5.9 %collective-permute-start.16 = (bf16[192,512]{1,0:T(8,128)(2,1)S(1)}, bf16[192,512]{1,0:T(8,128)(2,1)S(1)}, u32[]{:S(2)}, u32[]{:S(2)}) collective-permute-start(bf16[192,512]{1,0:T(8,128)(2,1)S(1)} %attend.3.refs_1_), channel_id=1, source_target_pairs={{0,1},{1,0},{2,3},{3,2},{4,5},{5,4},{6,7},{7,6},{8,9},{9,8},{10,11... | collective-permute-start | bytes 589832 | tf_op jit(solution)/shard_map/ppermute | solution.py:27
  108.5 4.9 %collective-permute-start.15 = (bf16[192,512]{1,0:T(8,128)(2,1)S(1)}, bf16[192,512]{1,0:T(8,128)(2,1)S(1)}, u32[]{:S(2)}, u32[]{:S(2)}) collective-permute-start(bf16[192,512]{1,0:T(8,128)(2,1)S(1)} %attend.2.refs_0_), channel_id=1, source_target_pairs={{0,1},{1,0},{2,3},{3,2},{4,5},{5,4},{6,7},{7,6},{8,9},{9,8},{10,11... | collective-permute-start | bytes 589832 | tf_op jit(solution)/shard_map/ppermute | solution.py:27
  108.5 4.9 %copy-start.9 = (bf16[192,512]{1,0:T(8,128)(2,1)}, bf16[192,512]{1,0:T(8,128)(2,1)S(1)}, u32[]{:S(2)}) copy-start(bf16[192,512]{1,0:T(8,128)(2,1)S(1)} %collective-permute-done.14.refs_3_) | copy-start | bytes 589828
  108.5 5.0 %collective-permute-start.18 = (bf16[192,512]{1,0:T(8,128)(2,1)S(1)}, bf16[192,512]{1,0:T(8,128)(2,1)S(1)}, u32[]{:S(2)}, u32[]{:S(2)}) collective-permute-start(bf16[192,512]{1,0:T(8,128)(2,1)S(1)} %collective-permute-done.14.refs_3_), channel_id=1, source_target_pairs={{0,1},{1,0},{2,3},{3,2},{4,5},{5,4},{6,7},{7,6},{8,9},{9,8},{10,11... | collective-permute-start | bytes 589832 | tf_op jit(solution)/shard_map/ppermute | solution.py:27
  112.4 7.9 %copy-start.10 = (bf16[192,512]{1,0:T(8,128)(2,1)}, bf16[192,512]{1,0:T(8,128)(2,1)S(1)}, u32[]{:S(2)}) copy-start(bf16[192,512]{1,0:T(8,128)(2,1)S(1)} %collective-permute-done.13.refs_2_) | copy-start | bytes 589828
  112.4 2.2 %collective-permute-start.17 = (bf16[192,512]{1,0:T(8,128)(2,1)S(1)}, bf16[192,512]{1,0:T(8,128)(2,1)S(1)}, u32[]{:S(2)}, u32[]{:S(2)}) collective-permute-start(bf16[192,512]{1,0:T(8,128)(2,1)S(1)} %collective-permute-done.13.refs_2_), channel_id=1, source_target_pairs={{0,1},{1,0},{2,3},{3,2},{4,5},{5,4},{6,7},{7,6},{8,9},{9,8},{10,11... | collective-permute-start | bytes 589832 | tf_op jit(solution)/shard_map/ppermute | solution.py:27
  113.5 6.8 %copy-start.11 = (bf16[192,512]{1,0:T(8,128)(2,1)}, bf16[192,512]{1,0:T(8,128)(2,1)S(1)}, u32[]{:S(2)}) copy-start(bf16[192,512]{1,0:T(8,128)(2,1)S(1)} %collective-permute-done.16.refs_5_) | copy-start | bytes 589828
  113.5 6.8 %copy-start.12 = (bf16[192,512]{1,0:T(8,128)(2,1)}, bf16[192,512]{1,0:T(8,128)(2,1)S(1)}, u32[]{:S(2)}) copy-start(bf16[192,512]{1,0:T(8,128)(2,1)S(1)} %collective-permute-done.15.refs_4_) | copy-start | bytes 589828
  113.5 6.8 %copy-start.13 = (bf16[192,512]{1,0:T(8,128)(2,1)}, bf16[192,512]{1,0:T(8,128)(2,1)S(1)}, u32[]{:S(2)}) copy-start(bf16[192,512]{1,0:T(8,128)(2,1)S(1)} %collective-permute-done.18.refs_7_) | copy-start | bytes 589828
  114.5 5.8 %copy-start.14 = (bf16[192,512]{1,0:T(8,128)(2,1)}, bf16[192,512]{1,0:T(8,128)(2,1)S(1)}, u32[]{:S(2)}) copy-start(bf16[192,512]{1,0:T(8,128)(2,1)S(1)} %collective-permute-done.17.refs_6_) | copy-start | bytes 589828
  127.4 26.7 %all-to-all-start.2 = ((bf16[8,2,24,1792]{3,2,1,0:T(8,128)(2,1)}), bf16[8,2,24,1792]{3,2,1,0:T(8,128)(2,1)S(1)}, u32[]{:S(2)}, u32[]{:S(2)}) async-start(bf16[8,2,24,1792]{3,2,1,0:T(8,128)(2,1)} %project.1), calls=%async_computation.2 | async-start | bytes 2752512 | tf_op jit(solution)/shard_map/all_to_all | solution.py:363
  154.7 4.8 %collective-permute-start.19 = (bf16[12,1792]{1,0:T(8,128)(2,1)S(1)}, bf16[12,1792]{1,0:T(8,128)(2,1)S(1)}, u32[]{:S(2)}, u32[]{:S(2)}) collective-permute-start(bf16[12,1792]{1,0:T(8,128)(2,1)S(1)} %bitcast.32), channel_id=1, source_target_pairs={{0,1},{1,0},{2,3},{3,2},{4,5},{5,4},{6,7},{7,6},{8,9},{9,8},{10,11... | collective-permute-start | bytes 129032 | tf_op jit(solution)/shard_map/ppermute | solution.py:27
  156.4 3.6 %collective-permute-start.20 = (bf16[12,1792]{1,0:T(8,128)(2,1)S(1)}, bf16[12,1792]{1,0:T(8,128)(2,1)S(1)}, u32[]{:S(2)}, u32[]{:S(2)}) collective-permute-start(bf16[12,1792]{1,0:T(8,128)(2,1)S(1)} %bitcast.33), channel_id=1, source_target_pairs={{0,16},{16,0},{1,17},{17,1},{2,18},{18,2},{3,19},{19,3},{4,20},{20... | collective-permute-start | bytes 129032 | tf_op jit(solution)/shard_map/ppermute | solution.py:27
  156.8 4.6 %collective-permute-start.21 = (bf16[12,1792]{1,0:T(8,128)(2,1)S(1)}, bf16[12,1792]{1,0:T(8,128)(2,1)S(1)}, u32[]{:S(2)}, u32[]{:S(2)}) collective-permute-start(bf16[12,1792]{1,0:T(8,128)(2,1)S(1)} %bitcast.34), channel_id=1, source_target_pairs={{0,17},{1,16},{16,1},{17,0},{2,19},{3,18},{18,3},{19,2},{4,21},{5,... | collective-permute-start | bytes 129032 | tf_op jit(solution)/shard_map/ppermute | solution.py:369
  159.5 1.9 %copy-start.16 = (bf16[12,1792]{1,0:T(8,128)(2,1)}, bf16[12,1792]{1,0:T(8,128)(2,1)S(1)}, u32[]{:S(2)}) copy-start(bf16[12,1792]{1,0:T(8,128)(2,1)S(1)} %collective-permute-done.19.c_ref) | copy-start | bytes 129028
  160.0 1.3 copy-start.17
  161.4 0.6 copy-start.18
Sparse Core Ops, SparseCore 0:
  36.2 84.0 all-gather.2
